TPU v7x, 32 devices: a whole 2x2x4 slice. The times are simulated.
32 devices in a mesh: dp: 16 (over z, y, core), tensor: 2 (over x).
Axes of the slice: x: 2, y: 2, z: 4, core: 2. Of those that a mesh axis runs over, the one named last changes fastest.
Arguments:
- hidden_in: bfloat16 [16384, 8192], P(('dp', 'tensor')), parts along dimension 0, may hold values from -6 to 6
- queries: bfloat16 [16384, 4096], P('dp', 'tensor'), parts along dimension 0, may hold values from -104 to 104
- keys: bfloat16 [16384, 1024], P('dp', 'tensor'), parts along dimension 0, may hold values from -4 to 4
- values: bfloat16 [16384, 1024], P('dp', 'tensor'), parts along dimension 0, may hold values from -6 to 6
- out_grad: bfloat16 [16384, 4096], P('dp', 'tensor'), parts along dimension 0, may hold values from -6 to 6
- key_weight: bfloat16 [8192, 1024], P(None, 'tensor'), may hold values from -0.0625 to 0.0625
- value_weight: bfloat16 [8192, 1024], P(None, 'tensor'), may hold values from -0.0625 to 0.0625
- in_basis: bfloat16 [8192, 64], replicated, may hold values from -0.0625 to 0.0625
- key_basis: bfloat16 [1024, 64], P('tensor'), may hold values from -0.1875 to 0.1875
- value_basis: bfloat16 [1024, 64], P('tensor'), may hold values from -0.1875 to 0.1875
- doc_ids: int32 [16384], P('dp'), parts along dimension 0, may hold values from 0 to 7, never falling along the last dimension, each value on 1 to 256 neighbouring positions
Outputs:
- input_grad: bfloat16 [16384, 8192], P(('dp', 'tensor')), parts along dimension 0
- key_docs: float32 [128, 64, 64], P(('dp', 'tensor')), parts along dimension 0
- value_docs: float32 [128, 64, 64], P(('dp', 'tensor')), parts along dimension 0
There are 16 independent parts, one for each index of `dp`. A program takes and returns all parts, laid end to end along the dimension named above; an argument that names none is the same for every part. Nothing has to cross between parts.
Inputs may be any that keep to these rules, and one draw needn't show every extreme that they name: `doc_ids`: never falling along the tokens; each document holds 1 to 256 tokens and one holds exactly 256.
All inputs are finite; a program needn't handle non-finite values.
Results may differ from a plain program's by a relative error of at most 0.013.
Values may be sent and summed in bfloat16 or wider, within the bound.
No kernel may reach another device: no remote copies, remote signals or barrier semaphores. Data moves between devices by JAX's collectives and lax.ppermute only.
A program may use at most 256 MiB of HBM per device.

v0:
```python
import functools
import math

import jax
import jax.numpy as jnp
from jax import lax
from jax.experimental import pallas as pl
from jax.experimental.pallas import tpu as pltpu
from jax.sharding import PartitionSpec as P

HD = 128
RANK = 64
DOCS = 8
QB = 128
CHIPS_Z, CHIPS_Y, CORES = 4, 2, 2
CHIPS = CHIPS_Z * CHIPS_Y
MIB = 1 << 20
VMEM = 60 * MIB
ATT_VMEM = 60 * MIB
COST = pl.CostEstimate(flops=6*10**9, bytes_accessed=10**5, transcendentals=0)
PAIR = 2
TILE = 256
X, CORE, SEND, REST, SLABS = 0, 1, 2, 4, 5


def allowed_pairs(doc_ids):
    count = doc_ids.shape[0]
    position = jnp.arange(count, dtype=jnp.int32)
    same_doc = doc_ids[:, None] == doc_ids[None, :]
    return same_doc & (position[None, :] <= position[:, None])


def group_grads(query_heads, key_head, value_head, grad_heads, allowed):
    scale = HD ** (-0.5)

    def one_head(carry, operands):
        query, grad_out = operands
        scores = jnp.dot(query, key_head.T, preferred_element_type=jnp.float32) * scale
        scores = jnp.where(allowed, scores, -1e30)
        peak = jnp.max(scores, axis=1, keepdims=True)
        expo = jnp.exp(scores - peak)
        probs = expo / jnp.sum(expo, axis=1, keepdims=True)
        probs_low = probs.astype(jnp.bfloat16)
        value_step = lax.dot_general(
            probs_low, grad_out, (((0,), (0,)), ((), ())), preferred_element_type=jnp.float32
        )
        dprobs = jnp.dot(grad_out, value_head.T, preferred_element_type=jnp.float32)
        delta = jnp.sum(probs * dprobs, axis=1, keepdims=True)
        dscores = (probs * (dprobs - delta)).astype(jnp.bfloat16)
        key_step = (
            lax.dot_general(
                dscores, query, (((0,), (0,)), ((), ())), preferred_element_type=jnp.float32
            )
            * scale
        )
        return ((carry[0] + key_step, carry[1] + value_step), None)

    zeros = jnp.zeros((query_heads.shape[1], query_heads.shape[2]), jnp.float32)
    (key_sum, value_sum), _ = lax.scan(one_head, (zeros, zeros), (query_heads, grad_heads))
    return (key_sum.astype(jnp.bfloat16), value_sum.astype(jnp.bfloat16))


def doc_outer(weighted, grads):
    return lax.dot_general(
        weighted,
        grads,
        (((0,), (0,)), ((), ())),
        precision=lax.Precision.HIGHEST,
        preferred_element_type=jnp.float32,
    )


def spread_docs(doc_ids, doc_first, doc_count, projected):
    tok_count = doc_ids.shape[0]
    doc_range = doc_first + jnp.arange(doc_count, dtype=jnp.int32)
    onehot = (doc_ids[:, None] == doc_range[None, :]).astype(jnp.float32)
    return (onehot[:, :, None] * projected.astype(jnp.float32)[:, None, :]).reshape(
        tok_count, doc_count * RANK
    )


def general_body(
    hidden_in,
    queries,
    keys,
    values,
    out_grad,
    key_weight,
    value_weight,
    in_basis,
    key_basis,
    value_basis,
    doc_ids,
):
    tok_count = doc_ids.shape[0]
    tp_size = lax.axis_size("tensor")
    tp_index = lax.axis_index("tensor")
    local_kv = keys.shape[1] // HD
    local_q = queries.shape[1] // HD
    group = local_q // local_kv
    allowed = allowed_pairs(doc_ids)
    query_heads = queries.reshape(tok_count, local_kv, group, HD).transpose(1, 2, 0, 3)
    grad_heads = out_grad.reshape(tok_count, local_kv, group, HD).transpose(1, 2, 0, 3)
    key_heads = keys.reshape(tok_count, local_kv, HD).transpose(1, 0, 2)
    value_heads = values.reshape(tok_count, local_kv, HD).transpose(1, 0, 2)
    key_grad, value_grad = lax.map(
        lambda ops: group_grads(ops[0], ops[1], ops[2], ops[3], allowed),
        (query_heads, key_heads, value_heads, grad_heads),
    )
    key_flat = key_grad.transpose(1, 0, 2).reshape(tok_count, local_kv * HD)
    value_flat = value_grad.transpose(1, 0, 2).reshape(tok_count, local_kv * HD)
    summed = lax.dot_general(
        key_flat, key_weight, (((1,), (1,)), ((), ())), preferred_element_type=jnp.float32
    )
    input_grad = lax.psum_scatter(
        (
            summed
            + lax.dot_general(
                value_flat,
                value_weight,
                (((1,), (1,)), ((), ())),
                preferred_element_type=jnp.float32,
            )
        ).astype(jnp.bfloat16),
        "tensor",
        scatter_dimension=0,
        tiled=True,
    )
    projected = jnp.dot(
        lax.all_gather(hidden_in, "tensor", axis=0, tiled=True),
        in_basis,
        preferred_element_type=jnp.float32,
    ).astype(jnp.bfloat16)
    key_part_proj = jnp.dot(key_flat, key_basis, preferred_element_type=jnp.float32)
    value_part_proj = jnp.dot(value_flat, value_basis, preferred_element_type=jnp.float32)
    docs_local = DOCS // tp_size
    key_proj, value_proj = (
        lax.psum(key_part_proj.astype(jnp.bfloat16), "tensor").astype(jnp.float32),
        lax.psum(value_part_proj.astype(jnp.bfloat16), "tensor").astype(jnp.float32),
    )
    weighted = spread_docs(doc_ids, tp_index * docs_local, docs_local, projected)
    key_docs = doc_outer(weighted, key_proj).reshape(docs_local, RANK, RANK)
    value_docs = doc_outer(weighted, value_proj).reshape(docs_local, RANK, RANK)
    return (input_grad, key_docs, value_docs)


def chip_at(place):
    place %= CHIPS
    return (place, 0) if place < CHIPS_Z else (CHIPS - 1 - place, 1)


def place_of(z, y):
    return z if y == 0 else CHIPS - 1 - z


def device(z, y, core, x):
    return ((z * CHIPS_Y + y) * CORES + core) * 2 + x


def pairs(move):
    out = []
    for z in range(CHIPS_Z):
        for y in range(CHIPS_Y):
            for core in range(CORES):
                for x in range(2):
                    out.append((device(z, y, core, x), device(*move(z, y, core, x))))
    return out


def send_x(a):
    return lax.ppermute(a, ("dp", "tensor"), pairs(lambda z, y, c, x: (z, y, c, 1 - x)))


def send_core(a):
    return lax.ppermute(a, ("dp", "tensor"), pairs(lambda z, y, c, x: (z, y, 1 - c, x)))


def send_ring(a, step):
    def move(z, y, c, x):
        to = chip_at(place_of(z, y) + step)
        return (to[0], to[1], c, x)

    return lax.ppermute(a, ("dp", "tensor"), pairs(move))


def attention_kernel(scal, start_ref, q_ref, do_ref, k_ref, v_ref, *refs):
    own_ref, send_ref, acck, accv = refs[-4:]
    tok = q_ref.shape[0]
    heads = q_ref.shape[1] // HD
    scale = HD ** (-0.5)
    c2 = scale * math.log2(math.e)
    acck[...] = jnp.zeros_like(acck)
    accv[...] = jnp.zeros_like(accv)
    nt = (((1,), (1,)), ((), ()))
    nn = (((1,), (0,)), ((), ()))
    f32 = jnp.float32
    wide = 3 * QB
    kpos = lax.broadcasted_iota(jnp.int32, (wide, QB), 0)
    qpos = lax.broadcasted_iota(jnp.int32, (wide, QB), 1)

    @pl.loop(0, tok // QB, unroll=4)
    def _(i):
        lo = jnp.maximum(i - 2, 0) * QB
        rows = pl.ds(pl.multiple_of(i * QB, QB), QB)
        window = pl.ds(pl.multiple_of(lo, QB), wide)
        keys = k_ref[window, :]
        vals = v_ref[window, :]
        ok = (kpos >= start_ref[:, rows] - lo) & (kpos - qpos <= i * QB - lo)
        bias = jnp.where(ok, 0.0, -1e30).astype(f32)
        bias = jnp.concatenate([bias] * heads, axis=1)
        cols = [slice(n * HD, (n + 1) * HD) for n in range(heads)]
        q = jnp.concatenate([q_ref[rows, c] for c in cols], axis=0)
        do = jnp.concatenate([do_ref[rows, c] for c in cols], axis=0)
        s = lax.dot_general(keys, q, nt, preferred_element_type=f32) + bias
        dp = lax.dot_general(vals, do, nt, preferred_element_type=f32)
        peak = jnp.max(s, axis=0, keepdims=True)
        e = jnp.exp2((s - peak) * c2)
        inv = 1.0 / jnp.sum(e, axis=0, keepdims=True)
        delta = jnp.sum(e * dp, axis=0, keepdims=True) * inv
        p = e * inv
        ds = (p * (dp - delta)).astype(jnp.bfloat16)
        accv[window, :] += lax.dot_general(
            p.astype(jnp.bfloat16), do, nn, preferred_element_type=f32
        )
        acck[window, :] += lax.dot_general(ds, q, nn, preferred_element_type=f32)

    half = tok // 2
    mine = pl.multiple_of(scal[X] * half, half)
    theirs = pl.multiple_of((1 - scal[X]) * half, half)
    for ref, start in ((own_ref, mine), (send_ref, theirs)):
        ref[:, :HD] = (acck[pl.ds(start, half), :] * scale).astype(jnp.bfloat16)
        ref[:, HD:] = accv[pl.ds(start, half), :].astype(jnp.bfloat16)


def attention(scal, start, queries, out_grad, keys, values, head, waits, before):
    tok = queries.shape[0]
    group = queries.shape[1] // keys.shape[1]
    wide = pl.BlockSpec((tok, group * HD), lambda g, s: (0, head))
    narrow = pl.BlockSpec((tok, HD), lambda g, s: (0, head))
    out = jax.ShapeDtypeStruct((tok // 2, 2 * PAIR * HD), jnp.bfloat16)
    out_spec = pl.BlockSpec((tok // 2, 2 * HD), lambda g, s: (0, head % PAIR))
    args = [start, queries, out_grad, keys, values, *waits, *before]
    return pl.pallas_call(
        attention_kernel,
        out_shape=(out, out),
        grid_spec=pltpu.PrefetchScalarGridSpec(
            num_scalar_prefetch=1,
            grid=(1,),
            in_specs=[pl.BlockSpec(start.shape, lambda g, s: (0, 0)), wide, wide, narrow, narrow]
            + [pl.BlockSpec(memory_space=pl.ANY)] * (len(args) - 5),
            out_specs=(out_spec, out_spec),
            scratch_shapes=[pltpu.VMEM((tok, HD), jnp.float32)] * 2,
        ),
        input_output_aliases={len(args) - 1 + n: n for n in range(len(before))},
        compiler_params=pltpu.CompilerParams(vmem_limit_bytes=ATT_VMEM),
        cost_estimate=COST,
        name="attention_back",
    )(scal, *args)


def docs_kernel(scal, doc_own, doc_oth, proj_own, proj_oth, kb, vb, *refs):
    heads = kb.shape[1] // HD
    owns, sends = refs[: heads // PAIR], refs[heads // PAIR : 2 * heads // PAIR]
    mine_ref, theirs_ref, total = refs[-3:]
    f32 = jnp.float32
    nt = (((1,), (1,)), ((), ()))
    nn = (((1,), (0,)), ((), ()))
    for first, (doc, proj, parts) in enumerate(((doc_own, proj_own, owns), (doc_oth, proj_oth, sends))):
        cut = lambda n: [r[:, a : a + HD] for r in parts for a in range(n * HD, r.shape[1], 2 * HD)]
        gk = jnp.concatenate(cut(0), axis=1)
        gv = jnp.concatenate(cut(1), axis=1)
        pk = lax.dot_general(gk, kb[...], nt, preferred_element_type=f32)
        pv = lax.dot_general(gv, vb[...], nt, preferred_element_type=f32)
        both = jnp.concatenate([pk, pv], axis=1)
        high = both.astype(jnp.bfloat16)
        low = (both - high.astype(f32)).astype(jnp.bfloat16)
        p = proj[...].astype(f32)
        ids = doc[...]
        w = jnp.concatenate(
            [jnp.where(ids == d, p, 0.0) for d in range(DOCS)], axis=0
        ).astype(jnp.bfloat16)
        add = lax.dot_general(w, high, nn, preferred_element_type=f32)
        add += lax.dot_general(w, low, nn, preferred_element_type=f32)
        if first == 0:
            total[...] = add
        else:
            total[...] += add
    half = total.shape[0] // 2
    mine_ref[...] = total[pl.ds(pl.multiple_of(scal[X] * half, half), half), :]
    theirs_ref[...] = total[pl.ds(pl.multiple_of((1 - scal[X]) * half, half), half), :]


def doc_sums(scal, doc_own, doc_oth, proj_own, proj_oth, kb, vb, owns, sends, waits):
    args = (doc_own, doc_oth, proj_own, proj_oth, kb, vb, *owns, *sends)
    rows = DOCS * RANK
    out = jax.ShapeDtypeStruct((rows // 2, 2 * RANK), jnp.float32)
    spec = lambda a: pl.BlockSpec(a.shape, lambda g, s: (0, 0))
    return pl.pallas_call(
        docs_kernel,
        out_shape=(out, out),
        grid_spec=pltpu.PrefetchScalarGridSpec(
            num_scalar_prefetch=1,
            grid=(1,),
            in_specs=[spec(a) for a in args] + [pl.BlockSpec(memory_space=pl.ANY)] * len(waits),
            out_specs=(spec(out), spec(out)),
            scratch_shapes=[pltpu.VMEM((rows, 2 * RANK), jnp.float32)],
        ),
        compiler_params=pltpu.CompilerParams(vmem_limit_bytes=VMEM),
        cost_estimate=COST,
        name="doc_sums",
    )(scal, *args, *waits)


def join_kernel(scal, *refs):
    out = refs[-1]
    n = out.shape[1] // HD // 4
    k = n * HD
    key, value = [], []
    for ref in refs[: 2 * n // PAIR]:
        for h in range(PAIR):
            key.append((ref, slice(2 * h * HD, (2 * h + 1) * HD)))
            value.append((ref, slice((2 * h + 1) * HD, (2 * h + 2) * HD)))
    for h in range(n):
        for q, side in enumerate((key, value)):
            ref, cols = side[h]
            out[:, q * k + h * HD : q * k + (h + 1) * HD] = ref[:, cols]
    for core in range(2):

        @pl.when(scal[CORE] == core)
        def _():
            for h in range(n):
                for q, side in enumerate((key, value)):
                    ref, cols = side[n + h]
                    at = 2 * k + (q ^ core) * k + h * HD
                    out[:, at : at + HD] = ref[:, cols]


def join(scal, owns, others, waits):
    args = (*owns, *others)
    rows = owns[0].shape[0]
    out = jax.ShapeDtypeStruct((rows, sum(a.shape[1] for a in args)), jnp.bfloat16)
    spec = lambda a: pl.BlockSpec(a.shape, lambda g, s: (0, 0))
    return pl.pallas_call(
        join_kernel,
        out_shape=out,
        grid_spec=pltpu.PrefetchScalarGridSpec(
            num_scalar_prefetch=1,
            grid=(1,),
            in_specs=[spec(a) for a in args] + [pl.BlockSpec(memory_space=pl.ANY)] * len(waits),
            out_specs=spec(out),
        ),
        compiler_params=pltpu.CompilerParams(vmem_limit_bytes=VMEM),
        cost_estimate=COST,
        name="join",
    )(scal, *args, *waits)


def slabs_kernel(widths, places, counts, extra, scal, g_hbm, wk, wv, *refs):
    n = len(widths)
    out, g, w, o, sem_g, sem_w, sem_o = refs[sum(counts) + extra :]
    k = wk.shape[1]
    total = sum(widths)
    begin = [sum(widths[:s]) for s in range(n)]
    load_g = pltpu.make_async_copy(g_hbm, g, sem_g)
    load_g.start()
    loads, stores = [], []
    for s in range(n):
        rows = pl.ds(pl.multiple_of(scal[places[s]], HD), widths[s])
        a, b = begin[s], begin[s] + widths[s]
        pieces = [(wk.at[rows, :], w.at[0, a:b]), (wv.at[rows, :], w.at[1, a:b])]
        these = refs[sum(counts[:s]) : sum(counts[: s + 1])]
        step = (b - a) // (counts[s] // 2)
        for q, ref in enumerate(these):
            to = a + q % (counts[s] // 2) * step
            pieces.append((ref, w.at[2 + q // (counts[s] // 2), to : to + step]))
        loads.append([pltpu.make_async_copy(c, d, sem_w.at[s, i]) for i, (c, d) in enumerate(pieces)])
        stores.append(pltpu.make_async_copy(o.at[:, a:b], out.at[:, rows], sem_o.at[s]))

    def begin_loads(s):
        for copy in loads[s]:
            copy.start()

    def end_loads(s):
        for copy in loads[s]:
            copy.wait()

    begin_loads(0)
    load_g.wait()
    end_loads(0)
    if n > 1:
        begin_loads(1)
    cuts = [b // TILE for b in begin]

    @pl.loop(0, total // TILE)
    def _(t):
        for s in range(1, n):

            @pl.when(t == cuts[s])
            def _():
                end_loads(s)
                if s + 1 < n:
                    begin_loads(s + 1)

        rows = pl.ds(pl.multiple_of(t * TILE, TILE), TILE)
        o[:, rows] = sum(
            lax.dot_general(
                g[:, q * k : (q + 1) * k],
                w[q, rows, :],
                (((1,), (1,)), ((), ())),
                preferred_element_type=jnp.float32,
            )
            for q in range(4)
        ).astype(jnp.bfloat16)
        for s in range(n - 1):

            @pl.when(t == (begin[s] + widths[s] - 1) // TILE)
            def _():
                stores[s].start()

    left = total % TILE
    if left:
        o[:, total - left :] = sum(
            lax.dot_general(
                g[:, q * k : (q + 1) * k],
                w[q, total - left :, :],
                (((1,), (1,)), ((), ())),
                preferred_element_type=jnp.float32,
            )
            for q in range(4)
        ).astype(jnp.bfloat16)
    stores[-1].start()
    for copy in stores:
        copy.wait()


def slabs(scal, places, g, wk, wv, parts, waits, before=None):
    rows, depth = g.shape
    n = len(parts)
    counts = [len(part) for part in parts]
    widths = [sum(a.shape[0] for a in part) // 2 for part in parts]
    args = [g, wk, wv] + [a for part in parts for a in part] + waits
    aliases = {}
    if before is not None:
        aliases = {len(args) + 1: 0}
        args.append(before)
    total = sum(widths)
    return pl.pallas_call(
        functools.partial(slabs_kernel, widths, places, counts, len(waits) + (before is not None)),
        out_shape=jax.ShapeDtypeStruct((rows, wk.shape[0]), jnp.bfloat16),
        grid_spec=pltpu.PrefetchScalarGridSpec(
            num_scalar_prefetch=1,
            grid=(1,),
            in_specs=[pl.BlockSpec(memory_space=pl.ANY)] * len(args),
            out_specs=pl.BlockSpec(memory_space=pl.ANY),
            scratch_shapes=[
                pltpu.VMEM((rows, depth), jnp.bfloat16),
                pltpu.VMEM((4, total, wk.shape[1]), jnp.bfloat16),
                pltpu.VMEM((rows, total), jnp.bfloat16),
                pltpu.SemaphoreType.DMA,
                pltpu.SemaphoreType.DMA((n, 6)),
                pltpu.SemaphoreType.DMA((n,)),
            ],
        ),
        input_output_aliases=aliases,
        compiler_params=pltpu.CompilerParams(vmem_limit_bytes=VMEM),
        cost_estimate=COST,
        name="slabs",
    )(scal, *args)


def pick_kernel(at, scal, wk, wv, *refs):
    out, sem = refs[-2:]
    size = out.shape[0]
    rows = pl.ds(pl.multiple_of(scal[at], 64), size)
    for core, ref in enumerate((wk, wv)):

        @pl.when(scal[CORE] == core)
        def _():
            copy = pltpu.make_async_copy(ref.at[rows, :], out, sem)
            copy.start()
            copy.wait()


def pick(scal, at, size, wk, wv, waits=()):
    spec = pl.BlockSpec(memory_space=pl.ANY)
    return pl.pallas_call(
        functools.partial(pick_kernel, at),
        out_shape=jax.ShapeDtypeStruct((size, wk.shape[1]), wk.dtype),
        grid_spec=pltpu.PrefetchScalarGridSpec(
            num_scalar_prefetch=1,
            grid=(1,),
            in_specs=[spec] * (2 + len(waits)),
            out_specs=pl.BlockSpec((size, wk.shape[1]), lambda g, s: (0, 0)),
            scratch_shapes=[pltpu.SemaphoreType.DMA],
        ),
        compiler_params=pltpu.CompilerParams(vmem_limit_bytes=VMEM),
        cost_estimate=COST,
        name="pick",
    )(scal, wk, wv, *waits)


def plane_body(
    hidden_in,
    queries,
    keys,
    values,
    out_grad,
    key_weight,
    value_weight,
    in_basis,
    key_basis,
    value_basis,
    doc_ids,
):
    tok = doc_ids.shape[0]
    half = tok // 2
    x = lax.axis_index("tensor")
    dp = lax.axis_index("dp")
    z, y, core = dp // (CHIPS_Y * CORES), (dp // CORES) % CHIPS_Y, dp % CORES
    place = jnp.where(y == 0, z, CHIPS - 1 - z)
    rows = key_weight.shape[0]
    slab = rows * 7 // 8 // CHIPS // HD * HD
    rest = rows - slab * CHIPS
    piece = slab // 2

    weights = (key_weight, value_weight)
    first = slab * CHIPS
    mine = place * slab
    starts = [(place + n) % CHIPS * slab for n in range(CHIPS)]
    scal = jnp.stack(
        [x, core, mine, mine + piece, first, *starts, first]
    ).astype(jnp.int32)
    sent = [pick(scal, SEND + n, piece, *weights) for n in range(2)]
    got = [send_x(a) for a in sent]
    both = lambda a: [*a, *[send_core(b) for b in a]]
    own_slab = both(got)
    up, down = got, got
    ups, downs = [up], [down]
    for _ in range(CHIPS // 2 - 1):
        up = [send_ring(a, 1) for a in up]
        down = [send_ring(a, -1) for a in down]
        ups.append(up)
        downs.append(down)
    far = [send_ring(up[0], 1), send_ring(down[1], -1)]
    stage = lambda n, half: [ups[n][half], downs[n][half]]

    docq = doc_ids[None, :]
    start = jnp.sum(doc_ids[None, :] < doc_ids[:, None], axis=1, dtype=jnp.int32)[None, :]
    proj = lax.dot_general(
        in_basis, hidden_in, (((0,), (1,)), ((), ())), preferred_element_type=jnp.float32
    ).astype(jnp.bfloat16)
    proj_oth = send_x(proj)
    heads = keys.shape[1] // HD
    waits = [sent, got[:1], [*got, *stage(1, 0)], stage(1, 1)]
    waits += [[]] * (heads - len(waits))
    owns, sends, others, last = [], [], [], []
    for head in range(heads):
        before = last if head % PAIR else []
        order = [] if head % PAIR else last[:1]
        last = list(
            attention(
                scal, start, queries, out_grad, keys, values, head, waits[head] + order, before
            )
        )
        if head % PAIR == PAIR - 1:
            owns.append(last[0])
            sends.append(last[1])
            others.append(send_x(last[1]))
    rest_got = [send_x(pick(scal, REST, rest, *weights, got))]
    doc_own = lax.dynamic_slice_in_dim(docq, x * half, half, 1)
    doc_oth = lax.dynamic_slice_in_dim(docq, (1 - x) * half, half, 1)
    mine, theirs = doc_sums(
        scal, doc_own, doc_oth, proj, proj_oth, key_basis.T, value_basis.T, owns, sends, stage(2, 0)
    )
    docs = (mine + send_x(theirs)).reshape(DOCS // 2, RANK, 2 * RANK)

    g = join(scal, owns, others, stage(2, 1))
    ring = {0: own_slab, CHIPS // 2: both(far), None: both(rest_got)}
    for n in range(1, CHIPS // 2):
        ring[CHIPS - n], ring[n] = both(ups[n]), both(downs[n])
    out = None
    plan = (((0, 7, 1), stage(3, 0)), ((6, 2, None), stage(3, 1)), ((5, 3), []), ((4,), []))
    for group, waits in plan:
        places = [SLABS + (CHIPS if n is None else n) for n in group]
        out = slabs(scal, places, g, *weights, [ring[n] for n in group], waits, out)
    return out, docs[:, :, :RANK], docs[:, :, RANK:]


def solution(mesh):
    placed = (
        P(("dp", "tensor"), None),
        P("dp", "tensor"),
        P("dp", "tensor"),
        P("dp", "tensor"),
        P("dp", "tensor"),
        P(None, "tensor"),
        P(None, "tensor"),
        P(),
        P("tensor", None),
        P("tensor", None),
        P("dp"),
    )
    fits = dict(mesh.shape) == {"dp": CHIPS * CORES, "tensor": 2}
    return jax.shard_map(
        plane_body if fits else general_body,
        mesh=mesh,
        in_specs=placed,
        out_specs=(
            P(("dp", "tensor"), None),
            P(("dp", "tensor"), None, None),
            P(("dp", "tensor"), None, None),
        ),
        check_vma=False,
    )
```

profile of v0, /device:TPU:0, one launch (start us, length us, event | category | flops | bytes accessed | tf_op | source)
XLA Modules:
  0.0 161.8 jit_solution(11219003322755990124)
XLA Ops:
  1.5 2.5 %pick.3.refs_0_ = bf16[448,512]{1,0:T(8,128)(2,1)} custom-call(s32[14]{0:T(128)} %stack.51.scal, bf16[8192,512]{1,0:T(8,128)(2,1)} %wk.13, bf16[8192,512]{1,0:T(8,128)(2,1)} %wv.13), custom_call_target="tpu_custom_call" | custom-call | flops 6000000000 | bytes 100000 | tf_op jit(solution)/shard_map/pick/pallas_call | solution.py:486
  3.9 3.0 %collective-permute-start = (bf16[448,512]{1,0:T(8,128)(2,1)}, bf16[448,512]{1,0:T(8,128)(2,1)S(1)}, u32[]{:S(2)}, u32[]{:S(2)}) collective-permute-start(bf16[448,512]{1,0:T(8,128)(2,1)} %pick.3.refs_0_), channel_id=1, source_target_pairs={{0,1},{1,0},{2,3},{3,2},{4,5},{5,4},{6,7},{7,6},{8,9},{9,8},{10,11... | collective-permute-start | bytes 1376264 | tf_op jit(solution)/shard_map/ppermute | solution.py:171
  6.9 2.5 %pick.4.refs_1_ = bf16[448,512]{1,0:T(8,128)(2,1)} custom-call(s32[14]{0:T(128)} %stack.51.scal, bf16[8192,512]{1,0:T(8,128)(2,1)} %wk.13, bf16[8192,512]{1,0:T(8,128)(2,1)} %wv.13), custom_call_target="tpu_custom_call" | custom-call | flops 6000000000 | bytes 100000 | tf_op jit(solution)/shard_map/pick/pallas_call | solution.py:486
  9.5 6.0 %convolution_convert_fusion.proj_own = bf16[64,512]{1,0:T(8,128)(2,1)S(1)} fusion(bf16[8192,64]{0,1:T(8,128)(2,1)S(1)} %copy-done, bf16[512,8192]{1,0:T(8,128)(2,1)} %param.11), kind=kOutput, calls=%fused_computation.1 | convolution fusion | flops 536903680 | bytes 9502720 | tf_op jit(solution)/shard_map/dot_general | solution.py:549
  15.6 2.1 %collective-permute-start.36 = (bf16[64,512]{1,0:T(8,128)(2,1)S(1)}, bf16[64,512]{1,0:T(8,128)(2,1)S(1)}, u32[]{:S(2)}, u32[]{:S(2)}) collective-permute-start(bf16[64,512]{1,0:T(8,128)(2,1)S(1)} %convolution_convert_fusion.proj_own), channel_id=1, source_target_pairs={{0,1},{1,0},{2,3},{3,2},{4,5},{5,4},{6,7},{7,6},{8,9},{9,8},{10,11... | collective-permute-start | bytes 196616 | tf_op jit(solution)/shard_map/ppermute | solution.py:171
  17.6 1.2 convert_reduce_fusion
  19.5 9.6 %attention_back.4 = (bf16[512,512]{1,0:T(8,128)(2,1)}, bf16[512,512]{1,0:T(8,128)(2,1)}) custom-call(s32[14]{0:T(128)} %stack.51.scal, s32[1,1024]{1,0:T(1,128)} %bitcast.21, bf16[1024,2048]{1,0:T(8,128)(2,1)} %q_ref.7, bf16[1024,2048]{1,0:T(8,128)(2,1)} %do_ref.7, bf16[1024,512]{1,0:T(8,128)(2,1)} %k_ref.7, bf16[1024,512]{1,0:T(8,128)(2,1)} %v_ref.7, ...), custom_call_target="tpu_custom_call" | custom-call | flops 6000000000 | bytes 100000 | tf_op jit(solution)/shard_map/attention_back/pallas_call | solution.py:243
  29.1 1.6 %collective-permute-start.4 = (bf16[448,512]{1,0:T(8,128)(2,1)S(1)}, bf16[448,512]{1,0:T(8,128)(2,1)S(1)}, u32[]{:S(2)}, u32[]{:S(2)}) collective-permute-start(bf16[448,512]{1,0:T(8,128)(2,1)S(1)} %collective-permute-done.refs_0_), channel_id=1, source_target_pairs={{0,8},{1,9},{2,10},{3,11},{4,0},{5,1},{6,2},{7,3},{8,16},{9,17},{1... | collective-permute-start | bytes 1376264 | tf_op jit(solution)/shard_map/ppermute | solution.py:183
  31.2 1.6 collective-permute-start.2
  33.2 2.9 %pick.5 = bf16[1024,512]{1,0:T(8,128)(2,1)} custom-call(s32[14]{0:T(128)} %stack.51.scal, bf16[8192,512]{1,0:T(8,128)(2,1)} %wk.13, bf16[8192,512]{1,0:T(8,128)(2,1)} %wv.13, bf16[448,512]{1,0:T(8,128)(2,1)} %copy-done.8, bf16[448,512]{1,0:T(8,128)(2,1)} %copy-done.10), custom_call_target="tpu_custom_call" | custom-call | flops 6000000000 | bytes 100000 | tf_op jit(solution)/shard_map/pick/pallas_call | solution.py:486
  36.1 9.7 %attention_back.5 = (bf16[512,512]{1,0:T(8,128)(2,1)}, bf16[512,512]{1,0:T(8,128)(2,1)}) custom-call(s32[14]{0:T(128)} %stack.51.scal, s32[1,1024]{1,0:T(1,128)} %bitcast.22, bf16[1024,2048]{1,0:T(8,128)(2,1)} %q_ref.7, bf16[1024,2048]{1,0:T(8,128)(2,1)} %do_ref.7, bf16[1024,512]{1,0:T(8,128)(2,1)} %k_ref.7, ...), custom_call_target="tpu_custom_call", output_to_operand_aliasing={{0}: (7, {}), {1}: (8, {})} | custom-call | flops 6000000000 | bytes 100000 | tf_op jit(solution)/shard_map/attention_back/pallas_call | solution.py:243
  46.7 3.7 %collective-permute-done.2.refs_0_.refs_5_ = bf16[448,512]{1,0:T(8,128)(2,1)S(1)} collective-permute-done((bf16[448,512]{1,0:T(8,128)(2,1)S(1)}, bf16[448,512]{1,0:T(8,128)(2,1)S(1)}, u32[]{:S(2)}, u32[]{:S(2)}) %collective-permute-start.2) | collective-permute-done | bytes 458784 | tf_op jit(solution)/shard_map/ppermute | solution.py:183
  50.4 1.6 collective-permute-start.8
  52.5 9.6 %attention_back.6 = (bf16[512,512]{1,0:T(8,128)(2,1)}, bf16[512,512]{1,0:T(8,128)(2,1)}) custom-call(s32[14]{0:T(128)} %stack.51.scal, s32[1,1024]{1,0:T(1,128)} %bitcast.23, bf16[1024,2048]{1,0:T(8,128)(2,1)} %q_ref.7, bf16[1024,2048]{1,0:T(8,128)(2,1)} %do_ref.7, bf16[1024,512]{1,0:T(8,128)(2,1)} %k_ref.7, bf16[1024,512]{1,0:T(8,128)(2,1)} %v_ref.7, ...), custom_call_target="tpu_custom_call" | custom-call | flops 6000000000 | bytes 100000 | tf_op jit(solution)/shard_map/attention_back/pallas_call | solution.py:243
  62.5 1.8 %collective-permute-start.10 = (bf16[448,512]{1,0:T(8,128)(2,1)}, bf16[448,512]{1,0:T(8,128)(2,1)S(1)}, u32[]{:S(2)}, u32[]{:S(2)}) collective-permute-start(bf16[448,512]{1,0:T(8,128)(2,1)} %copy-done.12), channel_id=1, source_target_pairs={{0,8},{1,9},{2,10},{3,11},{4,0},{5,1},{6,2},{7,3},{8,16},{9,17},{1... | collective-permute-start | bytes 1376264 | tf_op jit(solution)/shard_map/ppermute | solution.py:183
  65.0 9.7 %attention_back.7 = (bf16[512,512]{1,0:T(8,128)(2,1)}, bf16[512,512]{1,0:T(8,128)(2,1)}) custom-call(s32[14]{0:T(128)} %stack.51.scal, s32[1,1024]{1,0:T(1,128)} %bitcast.24, bf16[1024,2048]{1,0:T(8,128)(2,1)} %q_ref.7, bf16[1024,2048]{1,0:T(8,128)(2,1)} %do_ref.7, bf16[1024,512]{1,0:T(8,128)(2,1)} %k_ref.7, ...), custom_call_target="tpu_custom_call", output_to_operand_aliasing={{0}: (8, {}), {1}: (9, {})} | custom-call | flops 6000000000 | bytes 100000 | tf_op jit(solution)/shard_map/attention_back/pallas_call | solution.py:243
  74.8 1.7 %collective-permute-start.7 = (bf16[512,512]{1,0:T(8,128)(2,1)}, bf16[512,512]{1,0:T(8,128)(2,1)}, u32[]{:S(2)}, u32[]{:S(2)}) collective-permute-start(bf16[512,512]{1,0:T(8,128)(2,1)} %get-tuple-element.20.refs_3_), channel_id=1, source_target_pairs={{0,1},{1,0},{2,3},{3,2},{4,5},{5,4},{6,7},{7,6},{8,9},{9,8},{10,11... | collective-permute-start | bytes 1572872 | tf_op jit(solution)/shard_map/ppermute | solution.py:171
  77.3 1.6 collective-permute-start.11
  78.9 5.0 %doc_sums.1 = (f32[256,128]{1,0:T(8,128)}, f32[256,128]{1,0:T(8,128)}) custom-call(s32[14]{0:T(128)} %stack.51.scal, s32[1,512]{1,0:T(1,128)} %bitcast.26, s32[1,512]{1,0:T(1,128)} %bitcast.25, bf16[64,512]{1,0:T(8,128)(2,1)} %copy-done.27, bf16[64,512]{1,0:T(8,128)(2,1)} %copy-done.29, bf16[64,512]{1,0:T(8,128)(2,1)} %bitcast.27, bf16[64,512]{1,0:T(8,128)(2,1)} %bitcast.28, ...), custom_call_target="tpu_custom_call" | custom-call | flops 6000000000 | bytes 100000 | tf_op jit(solution)/shard_map/doc_sums/pallas_call | solution.py:298
  84.8 12.9 %collective-permute-done.7.refs_3_ = bf16[512,512]{1,0:T(8,128)(2,1)} collective-permute-done((bf16[512,512]{1,0:T(8,128)(2,1)}, bf16[512,512]{1,0:T(8,128)(2,1)}, u32[]{:S(2)}, u32[]{:S(2)}) %collective-permute-start.7) | collective-permute-done | bytes 524320 | tf_op jit(solution)/shard_map/ppermute | solution.py:171
  97.7 1.6 %collective-permute-start.13 = (bf16[448,512]{1,0:T(8,128)(2,1)}, bf16[448,512]{1,0:T(8,128)(2,1)S(1)}, u32[]{:S(2)}, u32[]{:S(2)}) collective-permute-start(bf16[448,512]{1,0:T(8,128)(2,1)} %collective-permute-done.9.refs_5_), channel_id=1, source_target_pairs={{0,4},{1,5},{2,6},{3,7},{4,12},{5,13},{6,14},{7,15},{8,0},{9,1},{1... | collective-permute-start | bytes 1376264 | tf_op jit(solution)/shard_map/ppermute | solution.py:183
  99.4 1.3 collective-permute-start.17
  100.7 4.1 %join.1.g_hbm = bf16[512,2048]{1,0:T(8,128)(2,1)} custom-call(s32[14]{0:T(128)} %stack.51.scal, bf16[512,512]{1,0:T(8,128)(2,1)} %get-tuple-element.15.refs_4_.refs_0_, bf16[512,512]{1,0:T(8,128)(2,1)} %get-tuple-element.18.refs_1_, bf16[512,512]{1,0:T(8,128)(2,1)} %collective-permute-done.6.refs_2_, bf16[512,512]{1,0:T(8,128)(2,1)} %collective-permute-done.7.refs_3_, ...), custom_call_target="tpu_custom_call" | custom-call | flops 6000000000 | bytes 100000 | tf_op jit(solution)/shard_map/join/pallas_call | solution.py:343
  104.8 0.9 add.86
  107.0 3.9 %collective-permute-done.13.refs_11_.refs_5_ = bf16[448,512]{1,0:T(8,128)(2,1)S(1)} collective-permute-done((bf16[448,512]{1,0:T(8,128)(2,1)}, bf16[448,512]{1,0:T(8,128)(2,1)S(1)}, u32[]{:S(2)}, u32[]{:S(2)}) %collective-permute-start.13) | collective-permute-done | bytes 458784 | tf_op jit(solution)/shard_map/ppermute | solution.py:183
  110.9 1.3 collective-permute-done.17.refs_10_.refs_1_
  112.7 12.8 %slabs.4.refs_12_ = bf16[512,8192]{1,0:T(8,128)(2,1)} custom-call(s32[14]{0:T(128)} %stack.51.scal, bf16[512,2048]{1,0:T(8,128)(2,1)} %join.1.g_hbm, bf16[8192,512]{1,0:T(8,128)(2,1)} %wk.13, bf16[8192,512]{1,0:T(8,128)(2,1)} %wv.13, bf16[448,512]{1,0:T(8,128)(2,1)} %copy-done.8, bf16[448,512]{1,0:T(8,128)(2,1)} %copy-done.10, ...), custom_call_target="tpu_custom_call" | custom-call | flops 6000000000 | bytes 100000 | tf_op jit(solution)/shard_map/slabs/pallas_call | solution.py:447
  126.4 1.5 collective-permute-start.14
  128.0 0.9 copy-done.7
  128.9 12.9 %slabs.5.refs_8_ = bf16[512,8192]{1,0:T(8,128)(2,1)} custom-call(s32[14]{0:T(128)} %stack.51.scal, bf16[512,2048]{1,0:T(8,128)(2,1)} %join.1.g_hbm, bf16[8192,512]{1,0:T(8,128)(2,1)} %wk.13, bf16[8192,512]{1,0:T(8,128)(2,1)} %wv.13, bf16[448,512]{1,0:T(8,128)(2,1)} %copy-done.18, ...), custom_call_target="tpu_custom_call", output_to_operand_aliasing={{}: (16, {})} | custom-call | flops 6000000000 | bytes 100000 | tf_op jit(solution)/shard_map/slabs/pallas_call | solution.py:447
  143.2 9.6 %slabs.6.refs_4_ = bf16[512,8192]{1,0:T(8,128)(2,1)} custom-call(s32[14]{0:T(128)} %stack.51.scal, bf16[512,2048]{1,0:T(8,128)(2,1)} %join.1.g_hbm, bf16[8192,512]{1,0:T(8,128)(2,1)} %wk.13, bf16[8192,512]{1,0:T(8,128)(2,1)} %wv.13, bf16[448,512]{1,0:T(8,128)(2,1)} %copy-done.2, bf16[448,512]{1,0:T(8,128)(2,1)} %copy-done.5, ...), custom_call_target="tpu_custom_call", output_to_operand_aliasing={{}: (12, {})} | custom-call | flops 6000000000 | bytes 100000 | tf_op jit(solution)/shard_map/slabs/pallas_call | solution.py:447
  154.3 7.3 %slabs.7 = bf16[512,8192]{1,0:T(8,128)(2,1)} custom-call(s32[14]{0:T(128)} %stack.51.scal, bf16[512,2048]{1,0:T(8,128)(2,1)} %join.1.g_hbm, bf16[8192,512]{1,0:T(8,128)(2,1)} %wk.13, bf16[8192,512]{1,0:T(8,128)(2,1)} %wv.13, bf16[448,512]{1,0:T(8,128)(2,1)} %copy-done.21, bf16[448,512]{1,0:T(8,128)(2,1)} %copy-done.22, ...), custom_call_target="tpu_custom_call", output_to_operand_aliasing={{}: (8, {})} | custom-call | flops 6000000000 | bytes 100000 | tf_op jit(solution)/shard_map/slabs/pallas_call | solution.py:447
  (123 shorter events, 12.0 us)
Async XLA Ops:
  3.9 25.2 %collective-permute-start = (bf16[448,512]{1,0:T(8,128)(2,1)}, bf16[448,512]{1,0:T(8,128)(2,1)S(1)}, u32[]{:S(2)}, u32[]{:S(2)}) collective-permute-start(bf16[448,512]{1,0:T(8,128)(2,1)} %pick.3.refs_0_), channel_id=1, source_target_pairs={{0,1},{1,0},{2,3},{3,2},{4,5},{5,4},{6,7},{7,6},{8,9},{9,8},{10,11... | collective-permute-start | bytes 1376264 | tf_op jit(solution)/shard_map/ppermute | solution.py:171
  9.4 21.8 %collective-permute-start.1 = (bf16[448,512]{1,0:T(8,128)(2,1)}, bf16[448,512]{1,0:T(8,128)(2,1)S(1)}, u32[]{:S(2)}, u32[]{:S(2)}) collective-permute-start(bf16[448,512]{1,0:T(8,128)(2,1)} %pick.4.refs_1_), channel_id=1, source_target_pairs={{0,1},{1,0},{2,3},{3,2},{4,5},{5,4},{6,7},{7,6},{8,9},{9,8},{10,11... | collective-permute-start | bytes 1376264 | tf_op jit(solution)/shard_map/ppermute | solution.py:171
  15.6 30.3 %collective-permute-start.36 = (bf16[64,512]{1,0:T(8,128)(2,1)S(1)}, bf16[64,512]{1,0:T(8,128)(2,1)S(1)}, u32[]{:S(2)}, u32[]{:S(2)}) collective-permute-start(bf16[64,512]{1,0:T(8,128)(2,1)S(1)} %convolution_convert_fusion.proj_own), channel_id=1, source_target_pairs={{0,1},{1,0},{2,3},{3,2},{4,5},{5,4},{6,7},{7,6},{8,9},{9,8},{10,11... | collective-permute-start | bytes 196616 | tf_op jit(solution)/shard_map/ppermute | solution.py:171
  29.1 16.9 %collective-permute-start.4 = (bf16[448,512]{1,0:T(8,128)(2,1)S(1)}, bf16[448,512]{1,0:T(8,128)(2,1)S(1)}, u32[]{:S(2)}, u32[]{:S(2)}) collective-permute-start(bf16[448,512]{1,0:T(8,128)(2,1)S(1)} %collective-permute-done.refs_0_), channel_id=1, source_target_pairs={{0,8},{1,9},{2,10},{3,11},{4,0},{5,1},{6,2},{7,3},{8,16},{9,17},{1... | collective-permute-start | bytes 1376264 | tf_op jit(solution)/shard_map/ppermute | solution.py:183
  30.8 15.4 %collective-permute-start.5 = (bf16[448,512]{1,0:T(8,128)(2,1)S(1)}, bf16[448,512]{1,0:T(8,128)(2,1)S(1)}, u32[]{:S(2)}, u32[]{:S(2)}) collective-permute-start(bf16[448,512]{1,0:T(8,128)(2,1)S(1)} %collective-permute-done.refs_0_), channel_id=1, source_target_pairs={{0,4},{1,5},{2,6},{3,7},{4,12},{5,13},{6,14},{7,15},{8,0},{9,1},{1... | collective-permute-start | bytes 1376264 | tf_op jit(solution)/shard_map/ppermute | solution.py:183
  31.2 19.2 %collective-permute-start.2 = (bf16[448,512]{1,0:T(8,128)(2,1)S(1)}, bf16[448,512]{1,0:T(8,128)(2,1)S(1)}, u32[]{:S(2)}, u32[]{:S(2)}) collective-permute-start(bf16[448,512]{1,0:T(8,128)(2,1)S(1)} %collective-permute-done.1.refs_1_), channel_id=1, source_target_pairs={{0,8},{1,9},{2,10},{3,11},{4,0},{5,1},{6,2},{7,3},{8,16},{9,17},{1... | collective-permute-start | bytes 1376264 | tf_op jit(solution)/shard_map/ppermute | solution.py:183
  32.8 19.2 %collective-permute-start.3 = (bf16[448,512]{1,0:T(8,128)(2,1)S(1)}, bf16[448,512]{1,0:T(8,128)(2,1)S(1)}, u32[]{:S(2)}, u32[]{:S(2)}) collective-permute-start(bf16[448,512]{1,0:T(8,128)(2,1)S(1)} %collective-permute-done.1.refs_1_), channel_id=1, source_target_pairs={{0,4},{1,5},{2,6},{3,7},{4,12},{5,13},{6,14},{7,15},{8,0},{9,1},{1... | collective-permute-start | bytes 1376264 | tf_op jit(solution)/shard_map/ppermute | solution.py:183
  45.9 18.4 %collective-permute-start.6 = (bf16[512,512]{1,0:T(8,128)(2,1)}, bf16[512,512]{1,0:T(8,128)(2,1)}, u32[]{:S(2)}, u32[]{:S(2)}) collective-permute-start(bf16[512,512]{1,0:T(8,128)(2,1)} %get-tuple-element.19.refs_2_), channel_id=1, source_target_pairs={{0,1},{1,0},{2,3},{3,2},{4,5},{5,4},{6,7},{7,6},{8,9},{9,8},{10,11... | collective-permute-start | bytes 1572872 | tf_op jit(solution)/shard_map/ppermute | solution.py:171
  46.0 16.1 %collective-permute-start.30 = (bf16[448,512]{1,0:T(8,128)(2,1)S(1)}, bf16[448,512]{1,0:T(8,128)(2,1)}, u32[]{:S(2)}, u32[]{:S(2)}) collective-permute-start(bf16[448,512]{1,0:T(8,128)(2,1)S(1)} %copy-done.9), channel_id=1, source_target_pairs={{0,2},{1,3},{2,0},{3,1},{4,6},{5,7},{6,4},{7,5},{8,10},{9,11},{10,... | collective-permute-start | bytes 1376264 | tf_op jit(solution)/shard_map/ppermute | solution.py:175
  46.2 16.3 %collective-permute-start.31 = (bf16[448,512]{1,0:T(8,128)(2,1)S(1)}, bf16[448,512]{1,0:T(8,128)(2,1)}, u32[]{:S(2)}, u32[]{:S(2)}) collective-permute-start(bf16[448,512]{1,0:T(8,128)(2,1)S(1)} %copy-done.11), channel_id=1, source_target_pairs={{0,2},{1,3},{2,0},{3,1},{4,6},{5,7},{6,4},{7,5},{8,10},{9,11},{10,... | collective-permute-start | bytes 1376264 | tf_op jit(solution)/shard_map/ppermute | solution.py:175
  50.4 14.1 %collective-permute-start.8 = (bf16[448,512]{1,0:T(8,128)(2,1)S(1)}, bf16[448,512]{1,0:T(8,128)(2,1)}, u32[]{:S(2)}, u32[]{:S(2)}) collective-permute-start(bf16[448,512]{1,0:T(8,128)(2,1)S(1)} %collective-permute-done.2.refs_0_.refs_5_), channel_id=1, source_target_pairs={{0,8},{1,9},{2,10},{3,11},{4,0},{5,1},{6,2},{7,3},{8,16},{9,17},{1... | collective-permute-start | bytes 1376264 | tf_op jit(solution)/shard_map/ppermute | solution.py:183
  52.0 12.5 %collective-permute-start.9 = (bf16[448,512]{1,0:T(8,128)(2,1)S(1)}, bf16[448,512]{1,0:T(8,128)(2,1)}, u32[]{:S(2)}, u32[]{:S(2)}) collective-permute-start(bf16[448,512]{1,0:T(8,128)(2,1)S(1)} %collective-permute-done.3.refs_1_.refs_9_), channel_id=1, source_target_pairs={{0,4},{1,5},{2,6},{3,7},{4,12},{5,13},{6,14},{7,15},{8,0},{9,1},{1... | collective-permute-start | bytes 1376264 | tf_op jit(solution)/shard_map/ppermute | solution.py:183
  62.1 35.6 %collective-permute-start.28 = (bf16[1024,512]{1,0:T(8,128)(2,1)}, bf16[1024,512]{1,0:T(8,128)(2,1)S(1)}, u32[]{:S(2)}, u32[]{:S(2)}) collective-permute-start(bf16[1024,512]{1,0:T(8,128)(2,1)} %pick.5), channel_id=1, source_target_pairs={{0,1},{1,0},{2,3},{3,2},{4,5},{5,4},{6,7},{7,6},{8,9},{9,8},{10,11... | collective-permute-start | bytes 3145736 | tf_op jit(solution)/shard_map/ppermute | solution.py:171
  62.5 12.3 %collective-permute-start.10 = (bf16[448,512]{1,0:T(8,128)(2,1)}, bf16[448,512]{1,0:T(8,128)(2,1)S(1)}, u32[]{:S(2)}, u32[]{:S(2)}) collective-permute-start(bf16[448,512]{1,0:T(8,128)(2,1)} %copy-done.12), channel_id=1, source_target_pairs={{0,8},{1,9},{2,10},{3,11},{4,0},{5,1},{6,2},{7,3},{8,16},{9,17},{1... | collective-permute-start | bytes 1376264 | tf_op jit(solution)/shard_map/ppermute | solution.py:183
  64.5 12.8 %collective-permute-start.33 = (bf16[448,512]{1,0:T(8,128)(2,1)S(1)}, bf16[448,512]{1,0:T(8,128)(2,1)S(1)}, u32[]{:S(2)}, u32[]{:S(2)}) collective-permute-start(bf16[448,512]{1,0:T(8,128)(2,1)S(1)} %collective-permute-done.2.refs_0_.refs_5_), channel_id=1, source_target_pairs={{0,2},{1,3},{2,0},{3,1},{4,6},{5,7},{6,4},{7,5},{8,10},{9,11},{10,... | collective-permute-start | bytes 1376264 | tf_op jit(solution)/shard_map/ppermute | solution.py:175
  74.8 22.9 %collective-permute-start.7 = (bf16[512,512]{1,0:T(8,128)(2,1)}, bf16[512,512]{1,0:T(8,128)(2,1)}, u32[]{:S(2)}, u32[]{:S(2)}) collective-permute-start(bf16[512,512]{1,0:T(8,128)(2,1)} %get-tuple-element.20.refs_3_), channel_id=1, source_target_pairs={{0,1},{1,0},{2,3},{3,2},{4,5},{5,4},{6,7},{7,6},{8,9},{9,8},{10,11... | collective-permute-start | bytes 1572872 | tf_op jit(solution)/shard_map/ppermute | solution.py:171
  77.3 23.4 %collective-permute-start.11 = (bf16[448,512]{1,0:T(8,128)(2,1)S(1)}, bf16[448,512]{1,0:T(8,128)(2,1)S(1)}, u32[]{:S(2)}, u32[]{:S(2)}) collective-permute-start(bf16[448,512]{1,0:T(8,128)(2,1)S(1)} %collective-permute-done.10.refs_0_.refs_4_), channel_id=1, source_target_pairs={{0,8},{1,9},{2,10},{3,11},{4,0},{5,1},{6,2},{7,3},{8,16},{9,17},{1... | collective-permute-start | bytes 1376264 | tf_op jit(solution)/shard_map/ppermute | solution.py:183
  84.0 15.4 %collective-permute-start.37 = (f32[256,128]{1,0:T(8,128)}, f32[256,128]{1,0:T(8,128)}, u32[]{:S(2)}, u32[]{:S(2)}) collective-permute-start(f32[256,128]{1,0:T(8,128)} %get-tuple-element.22), channel_id=1, source_target_pairs={{0,1},{1,0},{2,3},{3,2},{4,5},{5,4},{6,7},{7,6},{8,9},{9,8},{10,11... | collective-permute-start | bytes 393224 | tf_op jit(solution)/shard_map/ppermute | solution.py:171
  84.6 21.9 %collective-permute-start.21 = (bf16[448,512]{1,0:T(8,128)(2,1)}, bf16[448,512]{1,0:T(8,128)(2,1)S(1)}, u32[]{:S(2)}, u32[]{:S(2)}) collective-permute-start(bf16[448,512]{1,0:T(8,128)(2,1)} %collective-permute-done.20.refs_4_.refs_5_), channel_id=1, source_target_pairs={{0,4},{1,5},{2,6},{3,7},{4,12},{5,13},{6,14},{7,15},{8,0},{9,1},{1... | collective-permute-start | bytes 1376264 | tf_op jit(solution)/shard_map/ppermute | solution.py:183
  97.7 14.5 %collective-permute-start.24 = (bf16[448,512]{1,0:T(8,128)(2,1)}, bf16[448,512]{1,0:T(8,128)(2,1)}, u32[]{:S(2)}, u32[]{:S(2)}) collective-permute-start(bf16[448,512]{1,0:T(8,128)(2,1)} %copy-done.18), channel_id=1, source_target_pairs={{0,2},{1,3},{2,0},{3,1},{4,6},{5,7},{6,4},{7,5},{8,10},{9,11},{10,... | collective-permute-start | bytes 1376264 | tf_op jit(solution)/shard_map/ppermute | solution.py:175
  97.7 13.1 %collective-permute-start.13 = (bf16[448,512]{1,0:T(8,128)(2,1)}, bf16[448,512]{1,0:T(8,128)(2,1)S(1)}, u32[]{:S(2)}, u32[]{:S(2)}) collective-permute-start(bf16[448,512]{1,0:T(8,128)(2,1)} %collective-permute-done.9.refs_5_), channel_id=1, source_target_pairs={{0,4},{1,5},{2,6},{3,7},{4,12},{5,13},{6,14},{7,15},{8,0},{9,1},{1... | collective-permute-start | bytes 1376264 | tf_op jit(solution)/shard_map/ppermute | solution.py:183
  99.4 12.8 %collective-permute-start.17 = (bf16[448,512]{1,0:T(8,128)(2,1)}, bf16[448,512]{1,0:T(8,128)(2,1)S(1)}, u32[]{:S(2)}, u32[]{:S(2)}) collective-permute-start(bf16[448,512]{1,0:T(8,128)(2,1)} %collective-permute-done.8.refs_4_.refs_1_), channel_id=1, source_target_pairs={{0,8},{1,9},{2,10},{3,11},{4,0},{5,1},{6,2},{7,3},{8,16},{9,17},{1... | collective-permute-start | bytes 1376264 | tf_op jit(solution)/shard_map/ppermute | solution.py:183
  100.7 27.2 %collective-permute-start.29 = (bf16[1024,512]{1,0:T(8,128)(2,1)S(1)}, bf16[1024,512]{1,0:T(8,128)(2,1)S(1)}, u32[]{:S(2)}, u32[]{:S(2)}) collective-permute-start(bf16[1024,512]{1,0:T(8,128)(2,1)S(1)} %collective-permute-done.28.refs_8_), channel_id=1, source_target_pairs={{0,2},{1,3},{2,0},{3,1},{4,6},{5,7},{6,4},{7,5},{8,10},{9,11},{10,... | collective-permute-start | bytes 3145736 | tf_op jit(solution)/shard_map/ppermute | solution.py:175
  106.5 19.0 %collective-permute-start.25 = (bf16[448,512]{1,0:T(8,128)(2,1)}, bf16[448,512]{1,0:T(8,128)(2,1)}, u32[]{:S(2)}, u32[]{:S(2)}) collective-permute-start(bf16[448,512]{1,0:T(8,128)(2,1)} %collective-permute-done.8.refs_4_.refs_1_), channel_id=1, source_target_pairs={{0,2},{1,3},{2,0},{3,1},{4,6},{5,7},{6,4},{7,5},{8,10},{9,11},{10,... | collective-permute-start | bytes 1376264 | tf_op jit(solution)/shard_map/ppermute | solution.py:175
  110.9 14.8 %collective-permute-start.26 = (bf16[448,512]{1,0:T(8,128)(2,1)}, bf16[448,512]{1,0:T(8,128)(2,1)}, u32[]{:S(2)}, u32[]{:S(2)}) collective-permute-start(bf16[448,512]{1,0:T(8,128)(2,1)} %collective-permute-done.20.refs_4_.refs_5_), channel_id=1, source_target_pairs={{0,2},{1,3},{2,0},{3,1},{4,6},{5,7},{6,4},{7,5},{8,10},{9,11},{10,... | collective-permute-start | bytes 1376264 | tf_op jit(solution)/shard_map/ppermute | solution.py:175
  112.2 14.2 %collective-permute-start.27 = (bf16[448,512]{1,0:T(8,128)(2,1)}, bf16[448,512]{1,0:T(8,128)(2,1)}, u32[]{:S(2)}, u32[]{:S(2)}) collective-permute-start(bf16[448,512]{1,0:T(8,128)(2,1)} %collective-permute-done.9.refs_5_), channel_id=1, source_target_pairs={{0,2},{1,3},{2,0},{3,1},{4,6},{5,7},{6,4},{7,5},{8,10},{9,11},{10,... | collective-permute-start | bytes 1376264 | tf_op jit(solution)/shard_map/ppermute | solution.py:175
  112.2 14.2 %collective-permute-start.18 = (bf16[448,512]{1,0:T(8,128)(2,1)S(1)}, bf16[448,512]{1,0:T(8,128)(2,1)}, u32[]{:S(2)}, u32[]{:S(2)}) collective-permute-start(bf16[448,512]{1,0:T(8,128)(2,1)S(1)} %collective-permute-done.11.refs_12_.refs_0_), channel_id=1, source_target_pairs={{0,2},{1,3},{2,0},{3,1},{4,6},{5,7},{6,4},{7,5},{8,10},{9,11},{10,... | collective-permute-start | bytes 1376264 | tf_op jit(solution)/shard_map/ppermute | solution.py:175
  125.5 16.9 %collective-permute-start.22 = (bf16[448,512]{1,0:T(8,128)(2,1)}, bf16[448,512]{1,0:T(8,128)(2,1)}, u32[]{:S(2)}, u32[]{:S(2)}) collective-permute-start(bf16[448,512]{1,0:T(8,128)(2,1)} %copy-done.3), channel_id=1, source_target_pairs={{0,2},{1,3},{2,0},{3,1},{4,6},{5,7},{6,4},{7,5},{8,10},{9,11},{10,... | collective-permute-start | bytes 1376264 | tf_op jit(solution)/shard_map/ppermute | solution.py:175
  125.7 16.1 %collective-permute-start.12 = (bf16[448,512]{1,0:T(8,128)(2,1)}, bf16[448,512]{1,0:T(8,128)(2,1)S(1)}, u32[]{:S(2)}, u32[]{:S(2)}) collective-permute-start(bf16[448,512]{1,0:T(8,128)(2,1)} %copy-done.2), channel_id=1, source_target_pairs={{0,8},{1,9},{2,10},{3,11},{4,0},{5,1},{6,2},{7,3},{8,16},{9,17},{1... | collective-permute-start | bytes 1376264 | tf_op jit(solution)/shard_map/ppermute | solution.py:183
  126.4 16.0 %collective-permute-start.23 = (bf16[448,512]{1,0:T(8,128)(2,1)S(1)}, bf16[448,512]{1,0:T(8,128)(2,1)}, u32[]{:S(2)}, u32[]{:S(2)}) collective-permute-start(bf16[448,512]{1,0:T(8,128)(2,1)S(1)} %collective-permute-done.13.refs_11_.refs_5_), channel_id=1, source_target_pairs={{0,2},{1,3},{2,0},{3,1},{4,6},{5,7},{6,4},{7,5},{8,10},{9,11},{10,... | collective-permute-start | bytes 1376264 | tf_op jit(solution)/shard_map/ppermute | solution.py:175
  126.4 15.5 %collective-permute-start.14 = (bf16[448,512]{1,0:T(8,128)(2,1)S(1)}, bf16[448,512]{1,0:T(8,128)(2,1)S(1)}, u32[]{:S(2)}, u32[]{:S(2)}) collective-permute-start(bf16[448,512]{1,0:T(8,128)(2,1)S(1)} %collective-permute-done.13.refs_11_.refs_5_), channel_id=1, source_target_pairs={{0,4},{1,5},{2,6},{3,7},{4,12},{5,13},{6,14},{7,15},{8,0},{9,1},{1... | collective-permute-start | bytes 1376264 | tf_op jit(solution)/shard_map/ppermute | solution.py:183
  127.9 14.5 %collective-permute-start.19 = (bf16[448,512]{1,0:T(8,128)(2,1)S(1)}, bf16[448,512]{1,0:T(8,128)(2,1)S(1)}, u32[]{:S(2)}, u32[]{:S(2)}) collective-permute-start(bf16[448,512]{1,0:T(8,128)(2,1)S(1)} %collective-permute-done.17.refs_10_.refs_1_), channel_id=1, source_target_pairs={{0,2},{1,3},{2,0},{3,1},{4,6},{5,7},{6,4},{7,5},{8,10},{9,11},{10,... | collective-permute-start | bytes 1376264 | tf_op jit(solution)/shard_map/ppermute | solution.py:175
  (36 other events, 332.5 us)
where the time goes:
time: 162 us
  Pallas kernels  98.2 us (61%)
  starting transfers between devices  26.6 us (16%)
  waiting for transfers between devices  21.9 us (14%)
  matrix products  6.04 us (4%)
  local copies, waits for them, and re-layouts  5.55 us (3%)
  other arithmetic  2.16 us (1%)
    pallas_call x4, Pallas kernels, slabs(): pl.pallas_call(functools.partial(slabs_kernel, widths, places, counts, le...  42.6 us
    pallas_call x4, Pallas kernels, attention(): pl.pallas_call(attention_kernel, out_shape=(out, out), grid_spec=pltpu.Pr...  38.7 us
    ppermute x14, starting transfers between devices, send_ring(): return lax.ppermute(a, ('dp', 'tensor'), pairs(move))  15.1 us
    ppermute x7, waiting for transfers between devices, send_x(): lax.ppermute(a, ('dp', 'tensor'), pairs(lambda z, y, c, x: (z, y, c, 1 -...  12.9 us
    ppermute x14, waiting for transfers between devices, send_ring(): return lax.ppermute(a, ('dp', 'tensor'), pairs(move))  8.96 us
    ppermute x7, starting transfers between devices, send_x(): lax.ppermute(a, ('dp', 'tensor'), pairs(lambda z, y, c, x: (z, y, c, 1 -...  8.03 us
    pallas_call x3, Pallas kernels, pick(): pl.pallas_call(functools.partial(pick_kernel, at), out_shape=jax.ShapeDty...  7.8 us
    dot_general x1, matrix products, plane_body(): lax.dot_general(in_basis, hidden_in, (((0,), (1,)), ((), ())), preferred_...  6.04 us
  transfers between devices with their start and end apart: 38, of which 4 were waited for; matrix products, arithmetic and copies ran while one was open for 6% of the time, Pallas kernels for 55%

commit v1 on v0

--- a/solution.py
+++ b/solution.py
@@ -15,11 +15,11 @@
 CHIPS_Z, CHIPS_Y, CORES = 4, 2, 2
 CHIPS = CHIPS_Z * CHIPS_Y
 MIB = 1 << 20
-VMEM = 60 * MIB
+VMEM = 52 * MIB
 ATT_VMEM = 60 * MIB
-COST = pl.CostEstimate(flops=6*10**9, bytes_accessed=10**5, transcendentals=0)
+COST = pl.CostEstimate(flops=5 * 10**9, bytes_accessed=10**5, transcendentals=0)
 PAIR = 2
-TILE = 256
+TILE = 896
 X, CORE, SEND, REST, SLABS = 0, 1, 2, 4, 5
 
 
@@ -311,37 +311,28 @@
     )(scal, *args, *waits)
 
 
-def join_kernel(scal, *refs):
+def join_kernel(swap, scal, *refs):
     out = refs[-1]
-    n = out.shape[1] // HD // 4
+    n = out.shape[1] // HD // 2
     k = n * HD
-    key, value = [], []
-    for ref in refs[: 2 * n // PAIR]:
-        for h in range(PAIR):
-            key.append((ref, slice(2 * h * HD, (2 * h + 1) * HD)))
-            value.append((ref, slice((2 * h + 1) * HD, (2 * h + 2) * HD)))
-    for h in range(n):
-        for q, side in enumerate((key, value)):
-            ref, cols = side[h]
-            out[:, q * k + h * HD : q * k + (h + 1) * HD] = ref[:, cols]
-    for core in range(2):
-
-        @pl.when(scal[CORE] == core)
+    for core in range(2 if swap else 1):
+
+        @pl.when(scal[CORE] == core if swap else scal[CORE] >= 0)
         def _():
             for h in range(n):
-                for q, side in enumerate((key, value)):
-                    ref, cols = side[n + h]
-                    at = 2 * k + (q ^ core) * k + h * HD
+                ref = refs[h // PAIR]
+                for q in range(2):
+                    at = (q ^ core) * k + h * HD
+                    cols = slice((2 * (h % PAIR) + q) * HD, (2 * (h % PAIR) + q + 1) * HD)
                     out[:, at : at + HD] = ref[:, cols]
 
 
-def join(scal, owns, others, waits):
-    args = (*owns, *others)
-    rows = owns[0].shape[0]
+def join(scal, args, swap, waits):
+    rows = args[0].shape[0]
     out = jax.ShapeDtypeStruct((rows, sum(a.shape[1] for a in args)), jnp.bfloat16)
     spec = lambda a: pl.BlockSpec(a.shape, lambda g, s: (0, 0))
     return pl.pallas_call(
-        join_kernel,
+        functools.partial(join_kernel, swap),
         out_shape=out,
         grid_spec=pltpu.PrefetchScalarGridSpec(
             num_scalar_prefetch=1,
@@ -355,14 +346,18 @@
     )(scal, *args, *waits)
 
 
-def slabs_kernel(widths, places, counts, extra, scal, g_hbm, wk, wv, *refs):
+def slabs_kernel(widths, places, counts, extra, scal, g_own, g_oth, wk, wv, *refs):
     n = len(widths)
     out, g, w, o, sem_g, sem_w, sem_o = refs[sum(counts) + extra :]
     k = wk.shape[1]
     total = sum(widths)
     begin = [sum(widths[:s]) for s in range(n)]
-    load_g = pltpu.make_async_copy(g_hbm, g, sem_g)
-    load_g.start()
+    load_g = [
+        pltpu.make_async_copy(g_own, g.at[0], sem_g.at[0]),
+        pltpu.make_async_copy(g_oth, g.at[1], sem_g.at[1]),
+    ]
+    for copy in load_g:
+        copy.start()
     loads, stores = [], []
     for s in range(n):
         rows = pl.ds(pl.multiple_of(scal[places[s]], HD), widths[s])
@@ -385,7 +380,8 @@
             copy.wait()
 
     begin_loads(0)
-    load_g.wait()
+    for copy in load_g:
+        copy.wait()
     end_loads(0)
     if n > 1:
         begin_loads(1)
@@ -404,7 +400,7 @@
         rows = pl.ds(pl.multiple_of(t * TILE, TILE), TILE)
         o[:, rows] = sum(
             lax.dot_general(
-                g[:, q * k : (q + 1) * k],
+                g[q // 2, :, q % 2 * k : (q % 2 + 1) * k],
                 w[q, rows, :],
                 (((1,), (1,)), ((), ())),
                 preferred_element_type=jnp.float32,
@@ -421,7 +417,7 @@
     if left:
         o[:, total - left :] = sum(
             lax.dot_general(
-                g[:, q * k : (q + 1) * k],
+                g[q // 2, :, q % 2 * k : (q % 2 + 1) * k],
                 w[q, total - left :, :],
                 (((1,), (1,)), ((), ())),
                 preferred_element_type=jnp.float32,
@@ -434,11 +430,11 @@
 
 
 def slabs(scal, places, g, wk, wv, parts, waits, before=None):
-    rows, depth = g.shape
+    rows, depth = g[0].shape
     n = len(parts)
     counts = [len(part) for part in parts]
     widths = [sum(a.shape[0] for a in part) // 2 for part in parts]
-    args = [g, wk, wv] + [a for part in parts for a in part] + waits
+    args = [*g, wk, wv] + [a for part in parts for a in part] + waits
     aliases = {}
     if before is not None:
         aliases = {len(args) + 1: 0}
@@ -453,10 +449,10 @@
             in_specs=[pl.BlockSpec(memory_space=pl.ANY)] * len(args),
             out_specs=pl.BlockSpec(memory_space=pl.ANY),
             scratch_shapes=[
-                pltpu.VMEM((rows, depth), jnp.bfloat16),
+                pltpu.VMEM((2, rows, depth), jnp.bfloat16),
                 pltpu.VMEM((4, total, wk.shape[1]), jnp.bfloat16),
                 pltpu.VMEM((rows, total), jnp.bfloat16),
-                pltpu.SemaphoreType.DMA,
+                pltpu.SemaphoreType.DMA((2,)),
                 pltpu.SemaphoreType.DMA((n, 6)),
                 pltpu.SemaphoreType.DMA((n,)),
             ],
@@ -551,7 +547,8 @@
     ).astype(jnp.bfloat16)
     proj_oth = send_x(proj)
     heads = keys.shape[1] // HD
-    waits = [sent, got[:1], [*got, *stage(1, 0)], stage(1, 1)]
+    rest_got = [send_x(pick(scal, REST, rest, *weights, got))]
+    waits = [sent, got, stage(1, 0), stage(1, 1)]
     waits += [[]] * (heads - len(waits))
     owns, sends, others, last = [], [], [], []
     for head in range(heads):
@@ -566,20 +563,19 @@
             owns.append(last[0])
             sends.append(last[1])
             others.append(send_x(last[1]))
-    rest_got = [send_x(pick(scal, REST, rest, *weights, got))]
     doc_own = lax.dynamic_slice_in_dim(docq, x * half, half, 1)
     doc_oth = lax.dynamic_slice_in_dim(docq, (1 - x) * half, half, 1)
     mine, theirs = doc_sums(
-        scal, doc_own, doc_oth, proj, proj_oth, key_basis.T, value_basis.T, owns, sends, stage(2, 0)
+        scal, doc_own, doc_oth, proj, proj_oth, key_basis.T, value_basis.T, owns, sends, [*stage(2, 0), *rest_got]
     )
     docs = (mine + send_x(theirs)).reshape(DOCS // 2, RANK, 2 * RANK)
 
-    g = join(scal, owns, others, stage(2, 1))
+    g = [join(scal, owns, False, [*stage(2, 0), *stage(2, 1)]), join(scal, others, True, [])]
     ring = {0: own_slab, CHIPS // 2: both(far), None: both(rest_got)}
     for n in range(1, CHIPS // 2):
         ring[CHIPS - n], ring[n] = both(ups[n]), both(downs[n])
     out = None
-    plan = (((0, 7, 1), stage(3, 0)), ((6, 2, None), stage(3, 1)), ((5, 3), []), ((4,), []))
+    plan = (((0, 7, 1), []), ((6, 2), stage(3, 0)), ((5, 3, None), []), ((4,), []))
     for group, waits in plan:
         places = [SLABS + (CHIPS if n is None else n) for n in group]
         out = slabs(scal, places, g, *weights, [ring[n] for n in group], waits, out)

time: 162 us -> 153 us (0.944)
  Pallas kernels: 98.2 us -> 90.9 us
  waiting for transfers between devices: 21.9 us -> 26.4 us
  matrix products: 6.04 us -> 2.66 us
    ppermute x14, waiting for transfers between devices: 8.96 us -> 21.8 us  [send_ring(): return lax.ppermute(a, ('dp', 'tensor'), pairs(move))]
    ppermute x7, waiting for transfers between devices: 12.9 us -> 4.6 us  [send_x(): lax.ppermute(a, ('dp', 'tensor'), pairs(lambda z, y, c, x: (z, y, c, 1 -...]
    pallas_call x4, Pallas kernels: 42.6 us -> 37.2 us  [slabs(): pl.pallas_call(functools.partial(slabs_kernel, widths, places, counts, le...]
    dot_general x1, matrix products: 6.04 us -> 2.66 us  [plane_body(): lax.dot_general(in_basis, hidden_in, (((0,), (1,)), ((), ())), preferred_...]
    pallas_call x3, Pallas kernels: 7.8 us -> 5.2 us  [pick(): pl.pallas_call(functools.partial(pick_kernel, at), out_shape=jax.ShapeDty...]
    pallas_call x1 -> x2, Pallas kernels: 4.09 us -> 5.91 us  [join(): pl.pallas_call(functools.partial(join_kernel, swap), out_shape=out, grid_...]
    unnamed x60 -> x64, local copies, waits for them, and re-layouts: 3.5 us -> 3.02 us
  transfers between devices with their start and end apart: 38 -> 38, of which waited for: 4 -> 9; matrix products, arithmetic and copies ran while one was open for 6% -> 3% of each run, Pallas kernels for 55% -> 54%
where the time goes in v1:
time: 153 us
  Pallas kernels  90.9 us (59%)
  waiting for transfers between devices  26.4 us (17%)
  starting transfers between devices  26.2 us (17%)
  local copies, waits for them, and re-layouts  3.95 us (3%)
  matrix products  2.66 us (2%)
    pallas_call x4, Pallas kernels, attention(): pl.pallas_call(attention_kernel, out_shape=(out, out), grid_spec=pltpu.Pr...  38.7 us
    pallas_call x4, Pallas kernels, slabs(): pl.pallas_call(functools.partial(slabs_kernel, widths, places, counts, le...  37.2 us
    ppermute x14, waiting for transfers between devices, send_ring(): return lax.ppermute(a, ('dp', 'tensor'), pairs(move))  21.8 us
    ppermute x14, starting transfers between devices, send_ring(): return lax.ppermute(a, ('dp', 'tensor'), pairs(move))  14.4 us
    ppermute x7, starting transfers between devices, send_x(): lax.ppermute(a, ('dp', 'tensor'), pairs(lambda z, y, c, x: (z, y, c, 1 -...  9.54 us
    pallas_call x2, Pallas kernels, join(): pl.pallas_call(functools.partial(join_kernel, swap), out_shape=out, grid_...  5.91 us
    pallas_call x3, Pallas kernels, pick(): pl.pallas_call(functools.partial(pick_kernel, at), out_shape=jax.ShapeDty...  5.2 us
    ppermute x7, waiting for transfers between devices, send_x(): lax.ppermute(a, ('dp', 'tensor'), pairs(lambda z, y, c, x: (z, y, c, 1 -...  4.6 us
  transfers between devices with their start and end apart: 38, of which 9 were waited for; matrix products, arithmetic and copies ran while one was open for 3% of the time, Pallas kernels for 54%

profile of v1, /device:TPU:0, one launch (start us, length us, event | category | flops | bytes accessed | tf_op | source)
XLA Modules:
  0.0 152.8 jit_solution(1132841601278570301)
XLA Ops:
  0.9 1.9 %pick.3.refs_0_ = bf16[448,512]{1,0:T(8,128)(2,1)S(1)} custom-call(s32[14]{0:T(128)S(1)} %stack.51.scal, bf16[8192,512]{1,0:T(8,128)(2,1)} %wk.13, bf16[8192,512]{1,0:T(8,128)(2,1)} %wv.13), custom_call_target="tpu_custom_call" | custom-call | flops 5000000000 | bytes 100000 | tf_op jit(solution)/shard_map/pick/pallas_call | solution.py:482
  2.8 3.0 %collective-permute-start = (bf16[448,512]{1,0:T(8,128)(2,1)S(1)}, bf16[448,512]{1,0:T(8,128)(2,1)S(1)}, u32[]{:S(2)}, u32[]{:S(2)}) collective-permute-start(bf16[448,512]{1,0:T(8,128)(2,1)S(1)} %pick.3.refs_0_), channel_id=1, source_target_pairs={{0,1},{1,0},{2,3},{3,2},{4,5},{5,4},{6,7},{7,6},{8,9},{9,8},{10,11... | collective-permute-start | bytes 1376264 | tf_op jit(solution)/shard_map/ppermute | solution.py:171
  5.8 1.6 %pick.4.refs_1_ = bf16[448,512]{1,0:T(8,128)(2,1)S(1)} custom-call(s32[14]{0:T(128)S(1)} %stack.51.scal, bf16[8192,512]{1,0:T(8,128)(2,1)} %wk.13, bf16[8192,512]{1,0:T(8,128)(2,1)} %wv.13), custom_call_target="tpu_custom_call" | custom-call | flops 5000000000 | bytes 100000 | tf_op jit(solution)/shard_map/pick/pallas_call | solution.py:482
  8.0 2.7 %convolution_convert_fusion.proj_own = bf16[64,512]{1,0:T(8,128)(2,1)S(1)} fusion(bf16[8192,64]{0,1:T(8,128)(2,1)S(1)} %copy-done, bf16[512,8192]{1,0:T(8,128)(2,1)S(1)} %bitcast.25), kind=kOutput, calls=%fused_computation.1 | convolution fusion | flops 536903680 | bytes 9502720 | tf_op jit(solution)/shard_map/dot_general | solution.py:545
  10.6 1.6 %collective-permute-start.36 = (bf16[64,512]{1,0:T(8,128)(2,1)S(1)}, bf16[64,512]{1,0:T(8,128)(2,1)S(1)}, u32[]{:S(2)}, u32[]{:S(2)}) collective-permute-start(bf16[64,512]{1,0:T(8,128)(2,1)S(1)} %convolution_convert_fusion.proj_own), channel_id=1, source_target_pairs={{0,1},{1,0},{2,3},{3,2},{4,5},{5,4},{6,7},{7,6},{8,9},{9,8},{10,11... | collective-permute-start | bytes 196616 | tf_op jit(solution)/shard_map/ppermute | solution.py:171
  13.6 9.7 %attention_back.4 = (bf16[512,512]{1,0:T(8,128)(2,1)}, bf16[512,512]{1,0:T(8,128)(2,1)}) custom-call(s32[14]{0:T(128)} %copy-done.8, s32[1,1024]{1,0:T(1,128)} %bitcast.27, bf16[1024,2048]{1,0:T(8,128)(2,1)} %q_ref.7, bf16[1024,2048]{1,0:T(8,128)(2,1)} %do_ref.7, bf16[1024,512]{1,0:T(8,128)(2,1)} %k_ref.7, bf16[1024,512]{1,0:T(8,128)(2,1)} %v_ref.7, ...), custom_call_target="tpu_custom_call" | custom-call | flops 5000000000 | bytes 100000 | tf_op jit(solution)/shard_map/attention_back/pallas_call | solution.py:243
  23.3 3.6 %collective-permute-done.1.refs_1_ = bf16[448,512]{1,0:T(8,128)(2,1)S(1)} collective-permute-done((bf16[448,512]{1,0:T(8,128)(2,1)S(1)}, bf16[448,512]{1,0:T(8,128)(2,1)S(1)}, u32[]{:S(2)}, u32[]{:S(2)}) %collective-permute-start.1) | collective-permute-done | bytes 458784 | tf_op jit(solution)/shard_map/ppermute | solution.py:171
  26.9 1.8 %pick.5 = bf16[1024,512]{1,0:T(8,128)(2,1)S(1)} custom-call(s32[14]{0:T(128)S(1)} %copy-done.9, bf16[8192,512]{1,0:T(8,128)(2,1)} %wk.13, bf16[8192,512]{1,0:T(8,128)(2,1)} %wv.13, bf16[448,512]{1,0:T(8,128)(2,1)S(1)} %collective-permute-done.refs_0_, bf16[448,512]{1,0:T(8,128)(2,1)S(1)} %collective-permute-done.1.refs_1_), custom_call_target="tpu_custom_call" | custom-call | flops 5000000000 | bytes 100000 | tf_op jit(solution)/shard_map/pick/pallas_call | solution.py:482
  28.7 1.8 %collective-permute-start.24 = (bf16[1024,512]{1,0:T(8,128)(2,1)S(1)}, bf16[1024,512]{1,0:T(8,128)(2,1)}, u32[]{:S(2)}, u32[]{:S(2)}) collective-permute-start(bf16[1024,512]{1,0:T(8,128)(2,1)S(1)} %pick.5), channel_id=1, source_target_pairs={{0,1},{1,0},{2,3},{3,2},{4,5},{5,4},{6,7},{7,6},{8,9},{9,8},{10,11... | collective-permute-start | bytes 3145736 | tf_op jit(solution)/shard_map/ppermute | solution.py:171
  30.5 1.6 %collective-permute-start.4 = (bf16[448,512]{1,0:T(8,128)(2,1)S(1)}, bf16[448,512]{1,0:T(8,128)(2,1)}, u32[]{:S(2)}, u32[]{:S(2)}) collective-permute-start(bf16[448,512]{1,0:T(8,128)(2,1)S(1)} %collective-permute-done.refs_0_), channel_id=1, source_target_pairs={{0,8},{1,9},{2,10},{3,11},{4,0},{5,1},{6,2},{7,3},{8,16},{9,17},{1... | collective-permute-start | bytes 1376264 | tf_op jit(solution)/shard_map/ppermute | solution.py:183
  32.5 9.7 %attention_back.5 = (bf16[512,512]{1,0:T(8,128)(2,1)}, bf16[512,512]{1,0:T(8,128)(2,1)}) custom-call(s32[14]{0:T(128)} %copy-done.8, s32[1,1024]{1,0:T(1,128)} %bitcast.28, bf16[1024,2048]{1,0:T(8,128)(2,1)} %q_ref.7, bf16[1024,2048]{1,0:T(8,128)(2,1)} %do_ref.7, bf16[1024,512]{1,0:T(8,128)(2,1)} %k_ref.7, ...), custom_call_target="tpu_custom_call", output_to_operand_aliasing={{0}: (8, {}), {1}: (9, {})} | custom-call | flops 5000000000 | bytes 100000 | tf_op jit(solution)/shard_map/attention_back/pallas_call | solution.py:243
  42.5 1.9 %collective-permute-start.2 = (bf16[448,512]{1,0:T(8,128)(2,1)S(1)}, bf16[448,512]{1,0:T(8,128)(2,1)}, u32[]{:S(2)}, u32[]{:S(2)}) collective-permute-start(bf16[448,512]{1,0:T(8,128)(2,1)S(1)} %copy-done.5), channel_id=1, source_target_pairs={{0,8},{1,9},{2,10},{3,11},{4,0},{5,1},{6,2},{7,3},{8,16},{9,17},{1... | collective-permute-start | bytes 1376264 | tf_op jit(solution)/shard_map/ppermute | solution.py:183
  44.6 9.6 %attention_back.6 = (bf16[512,512]{1,0:T(8,128)(2,1)}, bf16[512,512]{1,0:T(8,128)(2,1)}) custom-call(s32[14]{0:T(128)} %copy-done.8, s32[1,1024]{1,0:T(1,128)} %bitcast.29, bf16[1024,2048]{1,0:T(8,128)(2,1)} %q_ref.7, bf16[1024,2048]{1,0:T(8,128)(2,1)} %do_ref.7, bf16[1024,512]{1,0:T(8,128)(2,1)} %k_ref.7, bf16[1024,512]{1,0:T(8,128)(2,1)} %v_ref.7, ...), custom_call_target="tpu_custom_call" | custom-call | flops 5000000000 | bytes 100000 | tf_op jit(solution)/shard_map/attention_back/pallas_call | solution.py:243
  54.8 1.8 %collective-permute-start.6 = (bf16[448,512]{1,0:T(8,128)(2,1)}, bf16[448,512]{1,0:T(8,128)(2,1)S(1)}, u32[]{:S(2)}, u32[]{:S(2)}) collective-permute-start(bf16[448,512]{1,0:T(8,128)(2,1)} %collective-permute-done.4.refs_0_.refs_4_), channel_id=1, source_target_pairs={{0,8},{1,9},{2,10},{3,11},{4,0},{5,1},{6,2},{7,3},{8,16},{9,17},{1... | collective-permute-start | bytes 1376264 | tf_op jit(solution)/shard_map/ppermute | solution.py:183
  56.8 9.7 %attention_back.7 = (bf16[512,512]{1,0:T(8,128)(2,1)}, bf16[512,512]{1,0:T(8,128)(2,1)}) custom-call(s32[14]{0:T(128)} %copy-done.8, s32[1,1024]{1,0:T(1,128)} %bitcast.30, bf16[1024,2048]{1,0:T(8,128)(2,1)} %q_ref.7, bf16[1024,2048]{1,0:T(8,128)(2,1)} %do_ref.7, bf16[1024,512]{1,0:T(8,128)(2,1)} %k_ref.7, ...), custom_call_target="tpu_custom_call", output_to_operand_aliasing={{0}: (8, {}), {1}: (9, {})} | custom-call | flops 5000000000 | bytes 100000 | tf_op jit(solution)/shard_map/attention_back/pallas_call | solution.py:243
  66.5 1.7 %collective-permute-start.11 = (bf16[512,512]{1,0:T(8,128)(2,1)}, bf16[512,512]{1,0:T(8,128)(2,1)S(1)}, u32[]{:S(2)}, u32[]{:S(2)}) collective-permute-start(bf16[512,512]{1,0:T(8,128)(2,1)} %get-tuple-element.20.refs_3_), channel_id=1, source_target_pairs={{0,1},{1,0},{2,3},{3,2},{4,5},{5,4},{6,7},{7,6},{8,9},{9,8},{10,11... | collective-permute-start | bytes 1572872 | tf_op jit(solution)/shard_map/ppermute | solution.py:171
  68.3 1.6 %collective-permute-start.8 = (bf16[448,512]{1,0:T(8,128)(2,1)}, bf16[448,512]{1,0:T(8,128)(2,1)S(1)}, u32[]{:S(2)}, u32[]{:S(2)}) collective-permute-start(bf16[448,512]{1,0:T(8,128)(2,1)} %collective-permute-done.2.refs_0_.refs_5_), channel_id=1, source_target_pairs={{0,8},{1,9},{2,10},{3,11},{4,0},{5,1},{6,2},{7,3},{8,16},{9,17},{1... | collective-permute-start | bytes 1376264 | tf_op jit(solution)/shard_map/ppermute | solution.py:183
  71.9 3.9 %doc_sums.1 = (f32[256,128]{1,0:T(8,128)S(1)}, f32[256,128]{1,0:T(8,128)S(1)}) custom-call(s32[14]{0:T(128)S(1)} %copy-done.10, s32[1,512]{1,0:T(1,128)S(1)} %bitcast.21, s32[1,512]{1,0:T(1,128)S(1)} %bitcast.20, bf16[64,512]{1,0:T(8,128)(2,1)S(1)} %convolution_convert_fusion.proj_own, bf16[64,512]{1,0:T(8,128)(2,1)S(1)} %copy-done.16, ...), custom_call_target="tpu_custom_call" | custom-call | flops 5000000000 | bytes 100000 | tf_op jit(solution)/shard_map/doc_sums/pallas_call | solution.py:298
  75.8 4.3 %collective-permute-done.8.refs_4_.refs_1_ = bf16[448,512]{1,0:T(8,128)(2,1)S(1)} collective-permute-done((bf16[448,512]{1,0:T(8,128)(2,1)}, bf16[448,512]{1,0:T(8,128)(2,1)S(1)}, u32[]{:S(2)}, u32[]{:S(2)}) %collective-permute-start.8) | collective-permute-done | bytes 458784 | tf_op jit(solution)/shard_map/ppermute | solution.py:183
  81.5 1.6 %collective-permute-start.12 = (bf16[448,512]{1,0:T(8,128)(2,1)S(1)}, bf16[448,512]{1,0:T(8,128)(2,1)}, u32[]{:S(2)}, u32[]{:S(2)}) collective-permute-start(bf16[448,512]{1,0:T(8,128)(2,1)S(1)} %collective-permute-done.6.refs_2_.refs_0_.refs_4_), channel_id=1, source_target_pairs={{0,8},{1,9},{2,10},{3,11},{4,0},{5,1},{6,2},{7,3},{8,16},{9,17},{1... | collective-permute-start | bytes 1376264 | tf_op jit(solution)/shard_map/ppermute | solution.py:183
  83.6 3.0 %join.2.g_own = bf16[512,1024]{1,0:T(8,128)(2,1)} custom-call(s32[14]{0:T(128)S(1)} %copy-done.10, bf16[512,512]{1,0:T(8,128)(2,1)} %get-tuple-element.15.refs_2_.refs_0_, bf16[512,512]{1,0:T(8,128)(2,1)} %get-tuple-element.18.refs_1_, bf16[448,512]{1,0:T(8,128)(2,1)S(1)} %collective-permute-done.6.refs_2_.refs_0_.refs_4_, ...), custom_call_target="tpu_custom_call" | custom-call | flops 5000000000 | bytes 100000 | tf_op jit(solution)/shard_map/join/pallas_call | solution.py:334
  88.7 5.8 %collective-permute-done.12.refs_8_.refs_0_ = bf16[448,512]{1,0:T(8,128)(2,1)} collective-permute-done((bf16[448,512]{1,0:T(8,128)(2,1)S(1)}, bf16[448,512]{1,0:T(8,128)(2,1)}, u32[]{:S(2)}, u32[]{:S(2)}) %collective-permute-start.12) | collective-permute-done | bytes 458784 | tf_op jit(solution)/shard_map/ppermute | solution.py:183
  94.5 1.6 %collective-permute-start.18 = (bf16[448,512]{1,0:T(8,128)(2,1)S(1)}, bf16[448,512]{1,0:T(8,128)(2,1)S(1)}, u32[]{:S(2)}, u32[]{:S(2)}) collective-permute-start(bf16[448,512]{1,0:T(8,128)(2,1)S(1)} %collective-permute-done.8.refs_4_.refs_1_), channel_id=1, source_target_pairs={{0,8},{1,9},{2,10},{3,11},{4,0},{5,1},{6,2},{7,3},{8,16},{9,17},{1... | collective-permute-start | bytes 1376264 | tf_op jit(solution)/shard_map/ppermute | solution.py:183
  96.1 2.9 %join.3.g_oth = bf16[512,1024]{1,0:T(8,128)(2,1)} custom-call(s32[14]{0:T(128)S(1)} %copy-done.10, bf16[512,512]{1,0:T(8,128)(2,1)} %collective-permute-done.10.refs_0_, bf16[512,512]{1,0:T(8,128)(2,1)S(1)} %collective-permute-done.11.refs_1_), custom_call_target="tpu_custom_call" | custom-call | flops 5000000000 | bytes 100000 | tf_op jit(solution)/shard_map/join/pallas_call | solution.py:334
  100.1 6.5 %collective-permute-done.18.refs_1_ = bf16[448,512]{1,0:T(8,128)(2,1)S(1)} collective-permute-done((bf16[448,512]{1,0:T(8,128)(2,1)S(1)}, bf16[448,512]{1,0:T(8,128)(2,1)S(1)}, u32[]{:S(2)}, u32[]{:S(2)}) %collective-permute-start.18) | collective-permute-done | bytes 458784 | tf_op jit(solution)/shard_map/ppermute | solution.py:183
  106.6 10.9 %slabs.4.refs_10_ = bf16[512,8192]{1,0:T(8,128)(2,1)} custom-call(s32[14]{0:T(128)S(1)} %copy-done.10, bf16[512,1024]{1,0:T(8,128)(2,1)} %join.2.g_own, bf16[512,1024]{1,0:T(8,128)(2,1)} %join.3.g_oth, bf16[8192,512]{1,0:T(8,128)(2,1)} %wk.13, bf16[8192,512]{1,0:T(8,128)(2,1)} %wv.13, bf16[448,512]{1,0:T(8,128)(2,1)S(1)} %copy-done.3, ...), custom_call_target="tpu_custom_call" | custom-call | flops 5000000000 | bytes 100000 | tf_op jit(solution)/shard_map/slabs/pallas_call | solution.py:443
  118.3 1.6 %collective-permute-start.13 = (bf16[448,512]{1,0:T(8,128)(2,1)}, bf16[448,512]{1,0:T(8,128)(2,1)S(1)}, u32[]{:S(2)}, u32[]{:S(2)}) collective-permute-start(bf16[448,512]{1,0:T(8,128)(2,1)} %collective-permute-done.12.refs_8_.refs_0_), channel_id=1, source_target_pairs={{0,8},{1,9},{2,10},{3,11},{4,0},{5,1},{6,2},{7,3},{8,16},{9,17},{1... | collective-permute-start | bytes 1376264 | tf_op jit(solution)/shard_map/ppermute | solution.py:183
  120.6 8.4 %slabs.5.refs_10_ = bf16[512,8192]{1,0:T(8,128)(2,1)} custom-call(s32[14]{0:T(128)S(1)} %copy-done.10, bf16[512,1024]{1,0:T(8,128)(2,1)} %join.2.g_own, bf16[512,1024]{1,0:T(8,128)(2,1)} %join.3.g_oth, bf16[8192,512]{1,0:T(8,128)(2,1)} %wk.13, bf16[8192,512]{1,0:T(8,128)(2,1)} %wv.13, ...), custom_call_target="tpu_custom_call", output_to_operand_aliasing={{}: (15, {})} | custom-call | flops 5000000000 | bytes 100000 | tf_op jit(solution)/shard_map/slabs/pallas_call | solution.py:443
  129.0 2.4 %collective-permute-done.13.refs_0_ = bf16[448,512]{1,0:T(8,128)(2,1)S(1)} collective-permute-done((bf16[448,512]{1,0:T(8,128)(2,1)}, bf16[448,512]{1,0:T(8,128)(2,1)S(1)}, u32[]{:S(2)}, u32[]{:S(2)}) %collective-permute-start.13) | collective-permute-done | bytes 458784 | tf_op jit(solution)/shard_map/ppermute | solution.py:183
  131.4 1.4 collective-permute-done.15.refs_1_
  134.7 11.8 %slabs.6.refs_4_ = bf16[512,8192]{1,0:T(8,128)(2,1)} custom-call(s32[14]{0:T(128)S(1)} %copy-done.10, bf16[512,1024]{1,0:T(8,128)(2,1)} %join.2.g_own, bf16[512,1024]{1,0:T(8,128)(2,1)} %join.3.g_oth, bf16[8192,512]{1,0:T(8,128)(2,1)} %wk.13, bf16[8192,512]{1,0:T(8,128)(2,1)} %wv.13, ...), custom_call_target="tpu_custom_call", output_to_operand_aliasing={{}: (15, {})} | custom-call | flops 5000000000 | bytes 100000 | tf_op jit(solution)/shard_map/slabs/pallas_call | solution.py:443
  146.6 6.0 %slabs.7 = bf16[512,8192]{1,0:T(8,128)(2,1)} custom-call(s32[14]{0:T(128)S(1)} %copy-done.10, bf16[512,1024]{1,0:T(8,128)(2,1)} %join.2.g_own, bf16[512,1024]{1,0:T(8,128)(2,1)} %join.3.g_oth, bf16[8192,512]{1,0:T(8,128)(2,1)} %wk.13, bf16[8192,512]{1,0:T(8,128)(2,1)} %wv.13, ...), custom_call_target="tpu_custom_call", output_to_operand_aliasing={{}: (9, {})} | custom-call | flops 5000000000 | bytes 100000 | tf_op jit(solution)/shard_map/slabs/pallas_call | solution.py:443
  (129 shorter events, 14.1 us)
Async XLA Ops:
  2.8 20.4 %collective-permute-start = (bf16[448,512]{1,0:T(8,128)(2,1)S(1)}, bf16[448,512]{1,0:T(8,128)(2,1)S(1)}, u32[]{:S(2)}, u32[]{:S(2)}) collective-permute-start(bf16[448,512]{1,0:T(8,128)(2,1)S(1)} %pick.3.refs_0_), channel_id=1, source_target_pairs={{0,1},{1,0},{2,3},{3,2},{4,5},{5,4},{6,7},{7,6},{8,9},{9,8},{10,11... | collective-permute-start | bytes 1376264 | tf_op jit(solution)/shard_map/ppermute | solution.py:171
  7.4 19.4 %collective-permute-start.1 = (bf16[448,512]{1,0:T(8,128)(2,1)S(1)}, bf16[448,512]{1,0:T(8,128)(2,1)S(1)}, u32[]{:S(2)}, u32[]{:S(2)}) collective-permute-start(bf16[448,512]{1,0:T(8,128)(2,1)S(1)} %pick.4.refs_1_), channel_id=1, source_target_pairs={{0,1},{1,0},{2,3},{3,2},{4,5},{5,4},{6,7},{7,6},{8,9},{9,8},{10,11... | collective-permute-start | bytes 1376264 | tf_op jit(solution)/shard_map/ppermute | solution.py:171
  10.6 31.9 %collective-permute-start.36 = (bf16[64,512]{1,0:T(8,128)(2,1)S(1)}, bf16[64,512]{1,0:T(8,128)(2,1)S(1)}, u32[]{:S(2)}, u32[]{:S(2)}) collective-permute-start(bf16[64,512]{1,0:T(8,128)(2,1)S(1)} %convolution_convert_fusion.proj_own), channel_id=1, source_target_pairs={{0,1},{1,0},{2,3},{3,2},{4,5},{5,4},{6,7},{7,6},{8,9},{9,8},{10,11... | collective-permute-start | bytes 196616 | tf_op jit(solution)/shard_map/ppermute | solution.py:171
  28.7 41.6 %collective-permute-start.24 = (bf16[1024,512]{1,0:T(8,128)(2,1)S(1)}, bf16[1024,512]{1,0:T(8,128)(2,1)}, u32[]{:S(2)}, u32[]{:S(2)}) collective-permute-start(bf16[1024,512]{1,0:T(8,128)(2,1)S(1)} %pick.5), channel_id=1, source_target_pairs={{0,1},{1,0},{2,3},{3,2},{4,5},{5,4},{6,7},{7,6},{8,9},{9,8},{10,11... | collective-permute-start | bytes 3145736 | tf_op jit(solution)/shard_map/ppermute | solution.py:171
  30.5 13.9 %collective-permute-start.4 = (bf16[448,512]{1,0:T(8,128)(2,1)S(1)}, bf16[448,512]{1,0:T(8,128)(2,1)}, u32[]{:S(2)}, u32[]{:S(2)}) collective-permute-start(bf16[448,512]{1,0:T(8,128)(2,1)S(1)} %collective-permute-done.refs_0_), channel_id=1, source_target_pairs={{0,8},{1,9},{2,10},{3,11},{4,0},{5,1},{6,2},{7,3},{8,16},{9,17},{1... | collective-permute-start | bytes 1376264 | tf_op jit(solution)/shard_map/ppermute | solution.py:183
  32.1 12.5 %collective-permute-start.5 = (bf16[448,512]{1,0:T(8,128)(2,1)S(1)}, bf16[448,512]{1,0:T(8,128)(2,1)}, u32[]{:S(2)}, u32[]{:S(2)}) collective-permute-start(bf16[448,512]{1,0:T(8,128)(2,1)S(1)} %collective-permute-done.refs_0_), channel_id=1, source_target_pairs={{0,4},{1,5},{2,6},{3,7},{4,12},{5,13},{6,14},{7,15},{8,0},{9,1},{1... | collective-permute-start | bytes 1376264 | tf_op jit(solution)/shard_map/ppermute | solution.py:183
  42.2 26.0 %collective-permute-start.10 = (bf16[512,512]{1,0:T(8,128)(2,1)}, bf16[512,512]{1,0:T(8,128)(2,1)}, u32[]{:S(2)}, u32[]{:S(2)}) collective-permute-start(bf16[512,512]{1,0:T(8,128)(2,1)} %get-tuple-element.19.refs_2_), channel_id=1, source_target_pairs={{0,1},{1,0},{2,3},{3,2},{4,5},{5,4},{6,7},{7,6},{8,9},{9,8},{10,11... | collective-permute-start | bytes 1572872 | tf_op jit(solution)/shard_map/ppermute | solution.py:171
  42.5 11.7 %collective-permute-start.2 = (bf16[448,512]{1,0:T(8,128)(2,1)S(1)}, bf16[448,512]{1,0:T(8,128)(2,1)}, u32[]{:S(2)}, u32[]{:S(2)}) collective-permute-start(bf16[448,512]{1,0:T(8,128)(2,1)S(1)} %copy-done.5), channel_id=1, source_target_pairs={{0,8},{1,9},{2,10},{3,11},{4,0},{5,1},{6,2},{7,3},{8,16},{9,17},{1... | collective-permute-start | bytes 1376264 | tf_op jit(solution)/shard_map/ppermute | solution.py:183
  44.6 12.0 %collective-permute-start.30 = (bf16[448,512]{1,0:T(8,128)(2,1)S(1)}, bf16[448,512]{1,0:T(8,128)(2,1)S(1)}, u32[]{:S(2)}, u32[]{:S(2)}) collective-permute-start(bf16[448,512]{1,0:T(8,128)(2,1)S(1)} %copy-done.3), channel_id=1, source_target_pairs={{0,2},{1,3},{2,0},{3,1},{4,6},{5,7},{6,4},{7,5},{8,10},{9,11},{10,... | collective-permute-start | bytes 1376264 | tf_op jit(solution)/shard_map/ppermute | solution.py:175
  54.2 12.3 %collective-permute-start.31 = (bf16[448,512]{1,0:T(8,128)(2,1)S(1)}, bf16[448,512]{1,0:T(8,128)(2,1)S(1)}, u32[]{:S(2)}, u32[]{:S(2)}) collective-permute-start(bf16[448,512]{1,0:T(8,128)(2,1)S(1)} %copy-done.5), channel_id=1, source_target_pairs={{0,2},{1,3},{2,0},{3,1},{4,6},{5,7},{6,4},{7,5},{8,10},{9,11},{10,... | collective-permute-start | bytes 1376264 | tf_op jit(solution)/shard_map/ppermute | solution.py:175
  54.8 15.0 %collective-permute-start.6 = (bf16[448,512]{1,0:T(8,128)(2,1)}, bf16[448,512]{1,0:T(8,128)(2,1)S(1)}, u32[]{:S(2)}, u32[]{:S(2)}) collective-permute-start(bf16[448,512]{1,0:T(8,128)(2,1)} %collective-permute-done.4.refs_0_.refs_4_), channel_id=1, source_target_pairs={{0,8},{1,9},{2,10},{3,11},{4,0},{5,1},{6,2},{7,3},{8,16},{9,17},{1... | collective-permute-start | bytes 1376264 | tf_op jit(solution)/shard_map/ppermute | solution.py:183
  56.6 13.7 %collective-permute-start.7 = (bf16[448,512]{1,0:T(8,128)(2,1)}, bf16[448,512]{1,0:T(8,128)(2,1)S(1)}, u32[]{:S(2)}, u32[]{:S(2)}) collective-permute-start(bf16[448,512]{1,0:T(8,128)(2,1)} %collective-permute-done.5.refs_1_.refs_8_), channel_id=1, source_target_pairs={{0,4},{1,5},{2,6},{3,7},{4,12},{5,13},{6,14},{7,15},{8,0},{9,1},{1... | collective-permute-start | bytes 1376264 | tf_op jit(solution)/shard_map/ppermute | solution.py:183
  66.5 20.7 %collective-permute-start.11 = (bf16[512,512]{1,0:T(8,128)(2,1)}, bf16[512,512]{1,0:T(8,128)(2,1)S(1)}, u32[]{:S(2)}, u32[]{:S(2)}) collective-permute-start(bf16[512,512]{1,0:T(8,128)(2,1)} %get-tuple-element.20.refs_3_), channel_id=1, source_target_pairs={{0,1},{1,0},{2,3},{3,2},{4,5},{5,4},{6,7},{7,6},{8,9},{9,8},{10,11... | collective-permute-start | bytes 1572872 | tf_op jit(solution)/shard_map/ppermute | solution.py:171
  68.3 11.9 %collective-permute-start.8 = (bf16[448,512]{1,0:T(8,128)(2,1)}, bf16[448,512]{1,0:T(8,128)(2,1)S(1)}, u32[]{:S(2)}, u32[]{:S(2)}) collective-permute-start(bf16[448,512]{1,0:T(8,128)(2,1)} %collective-permute-done.2.refs_0_.refs_5_), channel_id=1, source_target_pairs={{0,8},{1,9},{2,10},{3,11},{4,0},{5,1},{6,2},{7,3},{8,16},{9,17},{1... | collective-permute-start | bytes 1376264 | tf_op jit(solution)/shard_map/ppermute | solution.py:183
  69.8 11.6 %collective-permute-start.9 = (bf16[448,512]{1,0:T(8,128)(2,1)}, bf16[448,512]{1,0:T(8,128)(2,1)S(1)}, u32[]{:S(2)}, u32[]{:S(2)}) collective-permute-start(bf16[448,512]{1,0:T(8,128)(2,1)} %collective-permute-done.3.refs_1_.refs_9_), channel_id=1, source_target_pairs={{0,4},{1,5},{2,6},{3,7},{4,12},{5,13},{6,14},{7,15},{8,0},{9,1},{1... | collective-permute-start | bytes 1376264 | tf_op jit(solution)/shard_map/ppermute | solution.py:183
  70.3 12.8 %collective-permute-start.33 = (bf16[448,512]{1,0:T(8,128)(2,1)}, bf16[448,512]{1,0:T(8,128)(2,1)S(1)}, u32[]{:S(2)}, u32[]{:S(2)}) collective-permute-start(bf16[448,512]{1,0:T(8,128)(2,1)} %collective-permute-done.2.refs_0_.refs_5_), channel_id=1, source_target_pairs={{0,2},{1,3},{2,0},{3,1},{4,6},{5,7},{6,4},{7,5},{8,10},{9,11},{10,... | collective-permute-start | bytes 1376264 | tf_op jit(solution)/shard_map/ppermute | solution.py:175
  81.5 13.0 %collective-permute-start.12 = (bf16[448,512]{1,0:T(8,128)(2,1)S(1)}, bf16[448,512]{1,0:T(8,128)(2,1)}, u32[]{:S(2)}, u32[]{:S(2)}) collective-permute-start(bf16[448,512]{1,0:T(8,128)(2,1)S(1)} %collective-permute-done.6.refs_2_.refs_0_.refs_4_), channel_id=1, source_target_pairs={{0,8},{1,9},{2,10},{3,11},{4,0},{5,1},{6,2},{7,3},{8,16},{9,17},{1... | collective-permute-start | bytes 1376264 | tf_op jit(solution)/shard_map/ppermute | solution.py:183
  86.7 12.4 %collective-permute-start.21 = (bf16[448,512]{1,0:T(8,128)(2,1)S(1)}, bf16[448,512]{1,0:T(8,128)(2,1)S(1)}, u32[]{:S(2)}, u32[]{:S(2)}) collective-permute-start(bf16[448,512]{1,0:T(8,128)(2,1)S(1)} %collective-permute-done.7.refs_3_.refs_4_.refs_5_), channel_id=1, source_target_pairs={{0,4},{1,5},{2,6},{3,7},{4,12},{5,13},{6,14},{7,15},{8,0},{9,1},{1... | collective-permute-start | bytes 1376264 | tf_op jit(solution)/shard_map/ppermute | solution.py:183
  87.2 11.9 %collective-permute-start.26 = (bf16[448,512]{1,0:T(8,128)(2,1)S(1)}, bf16[448,512]{1,0:T(8,128)(2,1)S(1)}, u32[]{:S(2)}, u32[]{:S(2)}) collective-permute-start(bf16[448,512]{1,0:T(8,128)(2,1)S(1)} %collective-permute-done.6.refs_2_.refs_0_.refs_4_), channel_id=1, source_target_pairs={{0,2},{1,3},{2,0},{3,1},{4,6},{5,7},{6,4},{7,5},{8,10},{9,11},{10,... | collective-permute-start | bytes 1376264 | tf_op jit(solution)/shard_map/ppermute | solution.py:175
  87.2 12.4 %collective-permute-start.27 = (bf16[448,512]{1,0:T(8,128)(2,1)S(1)}, bf16[448,512]{1,0:T(8,128)(2,1)S(1)}, u32[]{:S(2)}, u32[]{:S(2)}) collective-permute-start(bf16[448,512]{1,0:T(8,128)(2,1)S(1)} %collective-permute-done.8.refs_4_.refs_1_), channel_id=1, source_target_pairs={{0,2},{1,3},{2,0},{3,1},{4,6},{5,7},{6,4},{7,5},{8,10},{9,11},{10,... | collective-permute-start | bytes 1376264 | tf_op jit(solution)/shard_map/ppermute | solution.py:175
  94.5 12.1 %collective-permute-start.18 = (bf16[448,512]{1,0:T(8,128)(2,1)S(1)}, bf16[448,512]{1,0:T(8,128)(2,1)S(1)}, u32[]{:S(2)}, u32[]{:S(2)}) collective-permute-start(bf16[448,512]{1,0:T(8,128)(2,1)S(1)} %collective-permute-done.8.refs_4_.refs_1_), channel_id=1, source_target_pairs={{0,8},{1,9},{2,10},{3,11},{4,0},{5,1},{6,2},{7,3},{8,16},{9,17},{1... | collective-permute-start | bytes 1376264 | tf_op jit(solution)/shard_map/ppermute | solution.py:183
  99.0 19.2 %collective-permute-start.29 = (bf16[448,512]{1,0:T(8,128)(2,1)S(1)}, bf16[448,512]{1,0:T(8,128)(2,1)S(1)}, u32[]{:S(2)}, u32[]{:S(2)}) collective-permute-start(bf16[448,512]{1,0:T(8,128)(2,1)S(1)} %collective-permute-done.9.refs_5_), channel_id=1, source_target_pairs={{0,2},{1,3},{2,0},{3,1},{4,6},{5,7},{6,4},{7,5},{8,10},{9,11},{10,... | collective-permute-start | bytes 1376264 | tf_op jit(solution)/shard_map/ppermute | solution.py:175
  99.1 20.8 %collective-permute-start.14 = (bf16[448,512]{1,0:T(8,128)(2,1)S(1)}, bf16[448,512]{1,0:T(8,128)(2,1)S(1)}, u32[]{:S(2)}, u32[]{:S(2)}) collective-permute-start(bf16[448,512]{1,0:T(8,128)(2,1)S(1)} %collective-permute-done.9.refs_5_), channel_id=1, source_target_pairs={{0,4},{1,5},{2,6},{3,7},{4,12},{5,13},{6,14},{7,15},{8,0},{9,1},{1... | collective-permute-start | bytes 1376264 | tf_op jit(solution)/shard_map/ppermute | solution.py:183
  99.6 33.3 %collective-permute-start.25 = (bf16[1024,512]{1,0:T(8,128)(2,1)}, bf16[1024,512]{1,0:T(8,128)(2,1)S(1)}, u32[]{:S(2)}, u32[]{:S(2)}) collective-permute-start(bf16[1024,512]{1,0:T(8,128)(2,1)} %collective-permute-done.24.refs_8_.refs_6_), channel_id=1, source_target_pairs={{0,2},{1,3},{2,0},{3,1},{4,6},{5,7},{6,4},{7,5},{8,10},{9,11},{10,... | collective-permute-start | bytes 3145736 | tf_op jit(solution)/shard_map/ppermute | solution.py:175
  99.8 20.3 %collective-permute-start.19 = (bf16[448,512]{1,0:T(8,128)(2,1)}, bf16[448,512]{1,0:T(8,128)(2,1)S(1)}, u32[]{:S(2)}, u32[]{:S(2)}) collective-permute-start(bf16[448,512]{1,0:T(8,128)(2,1)} %collective-permute-done.12.refs_8_.refs_0_), channel_id=1, source_target_pairs={{0,2},{1,3},{2,0},{3,1},{4,6},{5,7},{6,4},{7,5},{8,10},{9,11},{10,... | collective-permute-start | bytes 1376264 | tf_op jit(solution)/shard_map/ppermute | solution.py:175
  106.6 14.0 %collective-permute-start.20 = (bf16[448,512]{1,0:T(8,128)(2,1)S(1)}, bf16[448,512]{1,0:T(8,128)(2,1)S(1)}, u32[]{:S(2)}, u32[]{:S(2)}) collective-permute-start(bf16[448,512]{1,0:T(8,128)(2,1)S(1)} %collective-permute-done.18.refs_1_), channel_id=1, source_target_pairs={{0,2},{1,3},{2,0},{3,1},{4,6},{5,7},{6,4},{7,5},{8,10},{9,11},{10,... | collective-permute-start | bytes 1376264 | tf_op jit(solution)/shard_map/ppermute | solution.py:175
  118.3 13.1 %collective-permute-start.13 = (bf16[448,512]{1,0:T(8,128)(2,1)}, bf16[448,512]{1,0:T(8,128)(2,1)S(1)}, u32[]{:S(2)}, u32[]{:S(2)}) collective-permute-start(bf16[448,512]{1,0:T(8,128)(2,1)} %collective-permute-done.12.refs_8_.refs_0_), channel_id=1, source_target_pairs={{0,8},{1,9},{2,10},{3,11},{4,0},{5,1},{6,2},{7,3},{8,16},{9,17},{1... | collective-permute-start | bytes 1376264 | tf_op jit(solution)/shard_map/ppermute | solution.py:183
  119.9 13.0 %collective-permute-start.23 = (bf16[448,512]{1,0:T(8,128)(2,1)S(1)}, bf16[448,512]{1,0:T(8,128)(2,1)S(1)}, u32[]{:S(2)}, u32[]{:S(2)}) collective-permute-start(bf16[448,512]{1,0:T(8,128)(2,1)S(1)} %collective-permute-done.14.refs_5_), channel_id=1, source_target_pairs={{0,2},{1,3},{2,0},{3,1},{4,6},{5,7},{6,4},{7,5},{8,10},{9,11},{10,... | collective-permute-start | bytes 1376264 | tf_op jit(solution)/shard_map/ppermute | solution.py:175
  120.1 12.7 %collective-permute-start.15 = (bf16[448,512]{1,0:T(8,128)(2,1)S(1)}, bf16[448,512]{1,0:T(8,128)(2,1)S(1)}, u32[]{:S(2)}, u32[]{:S(2)}) collective-permute-start(bf16[448,512]{1,0:T(8,128)(2,1)S(1)} %collective-permute-done.14.refs_5_), channel_id=1, source_target_pairs={{0,4},{1,5},{2,6},{3,7},{4,12},{5,13},{6,14},{7,15},{8,0},{9,1},{1... | collective-permute-start | bytes 1376264 | tf_op jit(solution)/shard_map/ppermute | solution.py:183
  120.5 12.3 %collective-permute-start.22 = (bf16[448,512]{1,0:T(8,128)(2,1)S(1)}, bf16[448,512]{1,0:T(8,128)(2,1)S(1)}, u32[]{:S(2)}, u32[]{:S(2)}) collective-permute-start(bf16[448,512]{1,0:T(8,128)(2,1)S(1)} %collective-permute-done.21.refs_9_.refs_4_), channel_id=1, source_target_pairs={{0,2},{1,3},{2,0},{3,1},{4,6},{5,7},{6,4},{7,5},{8,10},{9,11},{10,... | collective-permute-start | bytes 1376264 | tf_op jit(solution)/shard_map/ppermute | solution.py:175
  131.4 15.1 %collective-permute-start.16 = (bf16[448,512]{1,0:T(8,128)(2,1)S(1)}, bf16[448,512]{1,0:T(8,128)(2,1)S(1)}, u32[]{:S(2)}, u32[]{:S(2)}) collective-permute-start(bf16[448,512]{1,0:T(8,128)(2,1)S(1)} %collective-permute-done.13.refs_0_), channel_id=1, source_target_pairs={{0,2},{1,3},{2,0},{3,1},{4,6},{5,7},{6,4},{7,5},{8,10},{9,11},{10,... | collective-permute-start | bytes 1376264 | tf_op jit(solution)/shard_map/ppermute | solution.py:175
  132.8 13.8 %collective-permute-start.17 = (bf16[448,512]{1,0:T(8,128)(2,1)S(1)}, bf16[448,512]{1,0:T(8,128)(2,1)S(1)}, u32[]{:S(2)}, u32[]{:S(2)}) collective-permute-start(bf16[448,512]{1,0:T(8,128)(2,1)S(1)} %collective-permute-done.15.refs_1_), channel_id=1, source_target_pairs={{0,2},{1,3},{2,0},{3,1},{4,6},{5,7},{6,4},{7,5},{8,10},{9,11},{10,... | collective-permute-start | bytes 1376264 | tf_op jit(solution)/shard_map/ppermute | solution.py:175
  (38 other events, 333.4 us)

commit v2 on v1

--- a/solution.py
+++ b/solution.py
@@ -16,7 +16,7 @@
 CHIPS = CHIPS_Z * CHIPS_Y
 MIB = 1 << 20
 VMEM = 52 * MIB
-ATT_VMEM = 60 * MIB
+ATT_VMEM = 52 * MIB
 COST = pl.CostEstimate(flops=5 * 10**9, bytes_accessed=10**5, transcendentals=0)
 PAIR = 2
 TILE = 896
@@ -575,7 +575,7 @@
     for n in range(1, CHIPS // 2):
         ring[CHIPS - n], ring[n] = both(ups[n]), both(downs[n])
     out = None
-    plan = (((0, 7, 1), []), ((6, 2), stage(3, 0)), ((5, 3, None), []), ((4,), []))
+    plan = (((0, 7, 1), []), ((6, 2, None), stage(3, 0)), ((5, 3), []), ((4,), []))
     for group, waits in plan:
         places = [SLABS + (CHIPS if n is None else n) for n in group]
         out = slabs(scal, places, g, *weights, [ring[n] for n in group], waits, out)

time: 153 us -> 143 us (0.935)
  Pallas kernels: 90.9 us -> 85.4 us
  waiting for transfers between devices: 26.4 us -> 21.4 us
    ppermute x14, waiting for transfers between devices: 21.8 us -> 14.9 us  [send_ring(): return lax.ppermute(a, ('dp', 'tensor'), pairs(move))]
    pallas_call x4, Pallas kernels: 38.7 us -> 34.2 us  [attention(): pl.pallas_call(attention_kernel, out_shape=(out, out), grid_spec=pltpu.Pr...]
    ppermute x7, waiting for transfers between devices: 4.6 us -> 6.39 us  [send_x(): lax.ppermute(a, ('dp', 'tensor'), pairs(lambda z, y, c, x: (z, y, c, 1 -...]
    unnamed x64 -> x58, local copies, waits for them, and re-layouts: 3.02 us -> 3.71 us
  transfers between devices with their start and end apart: 38 -> 38, of which waited for: 9 -> 6; matrix products, arithmetic and copies ran while one was open for 3% -> 3% of each run, Pallas kernels for 54% -> 54%
where the time goes in v2:
time: 143 us
  Pallas kernels  85.4 us (60%)
  starting transfers between devices  26.9 us (19%)
  waiting for transfers between devices  21.4 us (15%)
  local copies, waits for them, and re-layouts  4.65 us (3%)
  matrix products  2.66 us (2%)
    pallas_call x4, Pallas kernels, slabs(): pl.pallas_call(functools.partial(slabs_kernel, widths, places, counts, le...  37.2 us
    pallas_call x4, Pallas kernels, attention(): pl.pallas_call(attention_kernel, out_shape=(out, out), grid_spec=pltpu.Pr...  34.2 us
    ppermute x14, waiting for transfers between devices, send_ring(): return lax.ppermute(a, ('dp', 'tensor'), pairs(move))  14.9 us
    ppermute x14, starting transfers between devices, send_ring(): return lax.ppermute(a, ('dp', 'tensor'), pairs(move))  14.3 us
    ppermute x7, starting transfers between devices, send_x(): lax.ppermute(a, ('dp', 'tensor'), pairs(lambda z, y, c, x: (z, y, c, 1 -...  9.53 us
    ppermute x7, waiting for transfers between devices, send_x(): lax.ppermute(a, ('dp', 'tensor'), pairs(lambda z, y, c, x: (z, y, c, 1 -...  6.39 us
    pallas_call x3, Pallas kernels, pick(): pl.pallas_call(functools.partial(pick_kernel, at), out_shape=jax.ShapeDty...  5.21 us
    pallas_call x2, Pallas kernels, join(): pl.pallas_call(functools.partial(join_kernel, swap), out_shape=out, grid_...  4.87 us
  transfers between devices with their start and end apart: 38, of which 6 were waited for; matrix products, arithmetic and copies ran while one was open for 3% of the time, Pallas kernels for 54%

profile of v2, /device:TPU:0, one launch (start us, length us, event | category | flops | bytes accessed | tf_op | source)
XLA Modules:
  0.0 143.0 jit_solution(10932412193784172318)
XLA Ops:
  0.9 1.9 %pick.3.refs_0_ = bf16[448,512]{1,0:T(8,128)(2,1)S(1)} custom-call(s32[14]{0:T(128)S(1)} %stack.51.scal, bf16[8192,512]{1,0:T(8,128)(2,1)} %wk.13, bf16[8192,512]{1,0:T(8,128)(2,1)} %wv.13), custom_call_target="tpu_custom_call" | custom-call | flops 5000000000 | bytes 100000 | tf_op jit(solution)/shard_map/pick/pallas_call | solution.py:482
  2.8 3.0 %collective-permute-start = (bf16[448,512]{1,0:T(8,128)(2,1)S(1)}, bf16[448,512]{1,0:T(8,128)(2,1)S(1)}, u32[]{:S(2)}, u32[]{:S(2)}) collective-permute-start(bf16[448,512]{1,0:T(8,128)(2,1)S(1)} %pick.3.refs_0_), channel_id=1, source_target_pairs={{0,1},{1,0},{2,3},{3,2},{4,5},{5,4},{6,7},{7,6},{8,9},{9,8},{10,11... | collective-permute-start | bytes 1376264 | tf_op jit(solution)/shard_map/ppermute | solution.py:171
  5.8 1.6 %pick.4.refs_1_ = bf16[448,512]{1,0:T(8,128)(2,1)S(1)} custom-call(s32[14]{0:T(128)S(1)} %stack.51.scal, bf16[8192,512]{1,0:T(8,128)(2,1)} %wk.13, bf16[8192,512]{1,0:T(8,128)(2,1)} %wv.13), custom_call_target="tpu_custom_call" | custom-call | flops 5000000000 | bytes 100000 | tf_op jit(solution)/shard_map/pick/pallas_call | solution.py:482
  7.8 2.7 %convolution_convert_fusion.proj_own = bf16[64,512]{1,0:T(8,128)(2,1)S(1)} fusion(bf16[8192,64]{0,1:T(8,128)(2,1)S(1)} %copy-done, bf16[512,8192]{1,0:T(8,128)(2,1)S(1)} %bitcast.29), kind=kOutput, calls=%fused_computation.1 | convolution fusion | flops 536903680 | bytes 9502720 | tf_op jit(solution)/shard_map/dot_general | solution.py:545
  10.4 1.8 %collective-permute-start.36 = (bf16[64,512]{1,0:T(8,128)(2,1)S(1)}, bf16[64,512]{1,0:T(8,128)(2,1)S(1)}, u32[]{:S(2)}, u32[]{:S(2)}) collective-permute-start(bf16[64,512]{1,0:T(8,128)(2,1)S(1)} %convolution_convert_fusion.proj_own), channel_id=1, source_target_pairs={{0,1},{1,0},{2,3},{3,2},{4,5},{5,4},{6,7},{7,6},{8,9},{9,8},{10,11... | collective-permute-start | bytes 196616 | tf_op jit(solution)/shard_map/ppermute | solution.py:171
  12.9 8.5 %attention_back.4 = (bf16[512,512]{1,0:T(8,128)(2,1)S(1)}, bf16[512,512]{1,0:T(8,128)(2,1)S(1)}) custom-call(s32[14]{0:T(128)S(1)} %stack.51.scal, s32[1,1024]{1,0:T(1,128)S(1)} %bitcast.20, bf16[1024,2048]{1,0:T(8,128)(2,1)} %q_ref.7, bf16[1024,2048]{1,0:T(8,128)(2,1)} %do_ref.7, bf16[1024,512]{1,0:T(8,128)(2,1)} %k_ref.7, bf16[1024,512]{1,0:T(8,128)(2,1)} %v_ref.7, ...), custom_call_target="tpu_custom_call" | custom-call | flops 5000000000 | bytes 100000 | tf_op jit(solution)/shard_map/attention_back/pallas_call | solution.py:243
  21.4 5.4 %collective-permute-done.1.refs_1_ = bf16[448,512]{1,0:T(8,128)(2,1)S(1)} collective-permute-done((bf16[448,512]{1,0:T(8,128)(2,1)S(1)}, bf16[448,512]{1,0:T(8,128)(2,1)S(1)}, u32[]{:S(2)}, u32[]{:S(2)}) %collective-permute-start.1) | collective-permute-done | bytes 458784 | tf_op jit(solution)/shard_map/ppermute | solution.py:171
  26.9 1.8 %pick.5 = bf16[1024,512]{1,0:T(8,128)(2,1)S(1)} custom-call(s32[14]{0:T(128)S(1)} %stack.51.scal, bf16[8192,512]{1,0:T(8,128)(2,1)} %wk.13, bf16[8192,512]{1,0:T(8,128)(2,1)} %wv.13, bf16[448,512]{1,0:T(8,128)(2,1)S(1)} %collective-permute-done.refs_0_, bf16[448,512]{1,0:T(8,128)(2,1)S(1)} %collective-permute-done.1.refs_1_), custom_call_target="tpu_custom_call" | custom-call | flops 5000000000 | bytes 100000 | tf_op jit(solution)/shard_map/pick/pallas_call | solution.py:482
  28.7 1.8 %collective-permute-start.28 = (bf16[1024,512]{1,0:T(8,128)(2,1)S(1)}, bf16[1024,512]{1,0:T(8,128)(2,1)}, u32[]{:S(2)}, u32[]{:S(2)}) collective-permute-start(bf16[1024,512]{1,0:T(8,128)(2,1)S(1)} %pick.5), channel_id=1, source_target_pairs={{0,1},{1,0},{2,3},{3,2},{4,5},{5,4},{6,7},{7,6},{8,9},{9,8},{10,11... | collective-permute-start | bytes 3145736 | tf_op jit(solution)/shard_map/ppermute | solution.py:171
  30.5 1.6 %collective-permute-start.4 = (bf16[448,512]{1,0:T(8,128)(2,1)S(1)}, bf16[448,512]{1,0:T(8,128)(2,1)S(1)}, u32[]{:S(2)}, u32[]{:S(2)}) collective-permute-start(bf16[448,512]{1,0:T(8,128)(2,1)S(1)} %collective-permute-done.refs_0_), channel_id=1, source_target_pairs={{0,8},{1,9},{2,10},{3,11},{4,0},{5,1},{6,2},{7,3},{8,16},{9,17},{1... | collective-permute-start | bytes 1376264 | tf_op jit(solution)/shard_map/ppermute | solution.py:183
  32.5 8.5 %attention_back.5 = (bf16[512,512]{1,0:T(8,128)(2,1)S(1)}, bf16[512,512]{1,0:T(8,128)(2,1)S(1)}) custom-call(s32[14]{0:T(128)S(1)} %stack.51.scal, s32[1,1024]{1,0:T(1,128)S(1)} %bitcast.21, bf16[1024,2048]{1,0:T(8,128)(2,1)} %q_ref.7, bf16[1024,2048]{1,0:T(8,128)(2,1)} %do_ref.7, ...), custom_call_target="tpu_custom_call", output_to_operand_aliasing={{0}: (8, {}), {1}: (9, {})} | custom-call | flops 5000000000 | bytes 100000 | tf_op jit(solution)/shard_map/attention_back/pallas_call | solution.py:243
  42.1 1.8 %collective-permute-start.2 = (bf16[448,512]{1,0:T(8,128)(2,1)S(1)}, bf16[448,512]{1,0:T(8,128)(2,1)S(1)}, u32[]{:S(2)}, u32[]{:S(2)}) collective-permute-start(bf16[448,512]{1,0:T(8,128)(2,1)S(1)} %collective-permute-done.1.refs_1_), channel_id=1, source_target_pairs={{0,8},{1,9},{2,10},{3,11},{4,0},{5,1},{6,2},{7,3},{8,16},{9,17},{1... | collective-permute-start | bytes 1376264 | tf_op jit(solution)/shard_map/ppermute | solution.py:183
  44.2 8.6 %attention_back.6 = (bf16[512,512]{1,0:T(8,128)(2,1)S(1)}, bf16[512,512]{1,0:T(8,128)(2,1)S(1)}) custom-call(s32[14]{0:T(128)S(1)} %stack.51.scal, s32[1,1024]{1,0:T(1,128)S(1)} %bitcast.22, bf16[1024,2048]{1,0:T(8,128)(2,1)} %q_ref.7, bf16[1024,2048]{1,0:T(8,128)(2,1)} %do_ref.7, bf16[1024,512]{1,0:T(8,128)(2,1)} %k_ref.7, bf16[1024,512]{1,0:T(8,128)(2,1)} %v_ref.7, ...), custom_call_target="tpu_custom_call" | custom-call | flops 5000000000 | bytes 100000 | tf_op jit(solution)/shard_map/attention_back/pallas_call | solution.py:243
  53.4 1.8 %collective-permute-start.6 = (bf16[448,512]{1,0:T(8,128)(2,1)S(1)}, bf16[448,512]{1,0:T(8,128)(2,1)S(1)}, u32[]{:S(2)}, u32[]{:S(2)}) collective-permute-start(bf16[448,512]{1,0:T(8,128)(2,1)S(1)} %collective-permute-done.4.refs_0_.refs_4_), channel_id=1, source_target_pairs={{0,8},{1,9},{2,10},{3,11},{4,0},{5,1},{6,2},{7,3},{8,16},{9,17},{1... | collective-permute-start | bytes 1376264 | tf_op jit(solution)/shard_map/ppermute | solution.py:183
  55.4 8.5 %attention_back.7 = (bf16[512,512]{1,0:T(8,128)(2,1)S(1)}, bf16[512,512]{1,0:T(8,128)(2,1)S(1)}) custom-call(s32[14]{0:T(128)S(1)} %stack.51.scal, s32[1,1024]{1,0:T(1,128)S(1)} %bitcast.23, bf16[1024,2048]{1,0:T(8,128)(2,1)} %q_ref.7, bf16[1024,2048]{1,0:T(8,128)(2,1)} %do_ref.7, ...), custom_call_target="tpu_custom_call", output_to_operand_aliasing={{0}: (8, {}), {1}: (9, {})} | custom-call | flops 5000000000 | bytes 100000 | tf_op jit(solution)/shard_map/attention_back/pallas_call | solution.py:243
  64.8 1.7 %collective-permute-start.11 = (bf16[512,512]{1,0:T(8,128)(2,1)S(1)}, bf16[512,512]{1,0:T(8,128)(2,1)S(1)}, u32[]{:S(2)}, u32[]{:S(2)}) collective-permute-start(bf16[512,512]{1,0:T(8,128)(2,1)S(1)} %get-tuple-element.20.refs_3_), channel_id=1, source_target_pairs={{0,1},{1,0},{2,3},{3,2},{4,5},{5,4},{6,7},{7,6},{8,9},{9,8},{10,11... | collective-permute-start | bytes 1572872 | tf_op jit(solution)/shard_map/ppermute | solution.py:171
  66.5 1.6 %collective-permute-start.8 = (bf16[448,512]{1,0:T(8,128)(2,1)S(1)}, bf16[448,512]{1,0:T(8,128)(2,1)S(1)}, u32[]{:S(2)}, u32[]{:S(2)}) collective-permute-start(bf16[448,512]{1,0:T(8,128)(2,1)S(1)} %collective-permute-done.2.refs_0_.refs_5_), channel_id=1, source_target_pairs={{0,8},{1,9},{2,10},{3,11},{4,0},{5,1},{6,2},{7,3},{8,16},{9,17},{1... | collective-permute-start | bytes 1376264 | tf_op jit(solution)/shard_map/ppermute | solution.py:183
  69.1 3.9 %doc_sums.1 = (f32[256,128]{1,0:T(8,128)S(1)}, f32[256,128]{1,0:T(8,128)S(1)}) custom-call(s32[14]{0:T(128)S(1)} %stack.51.scal, s32[1,512]{1,0:T(1,128)S(1)} %bitcast.25, s32[1,512]{1,0:T(1,128)S(1)} %bitcast.24, bf16[64,512]{1,0:T(8,128)(2,1)S(1)} %convolution_convert_fusion.proj_own, bf16[64,512]{1,0:T(8,128)(2,1)S(1)} %collective-permute-done.36.proj_oth, ...), custom_call_target="tpu_custom_call" | custom-call | flops 5000000000 | bytes 100000 | tf_op jit(solution)/shard_map/doc_sums/pallas_call | solution.py:298
  73.1 5.1 %collective-permute-done.8.refs_4_.refs_1_ = bf16[448,512]{1,0:T(8,128)(2,1)S(1)} collective-permute-done((bf16[448,512]{1,0:T(8,128)(2,1)S(1)}, bf16[448,512]{1,0:T(8,128)(2,1)S(1)}, u32[]{:S(2)}, u32[]{:S(2)}) %collective-permute-start.8) | collective-permute-done | bytes 458784 | tf_op jit(solution)/shard_map/ppermute | solution.py:183
  78.2 1.3 collective-permute-done.9.refs_5_
  79.5 1.6 %collective-permute-start.12 = (bf16[448,512]{1,0:T(8,128)(2,1)S(1)}, bf16[448,512]{1,0:T(8,128)(2,1)}, u32[]{:S(2)}, u32[]{:S(2)}) collective-permute-start(bf16[448,512]{1,0:T(8,128)(2,1)S(1)} %collective-permute-done.6.refs_2_.refs_0_.refs_4_), channel_id=1, source_target_pairs={{0,8},{1,9},{2,10},{3,11},{4,0},{5,1},{6,2},{7,3},{8,16},{9,17},{1... | collective-permute-start | bytes 1376264 | tf_op jit(solution)/shard_map/ppermute | solution.py:183
  81.7 3.0 %join.2.g_own = bf16[512,1024]{1,0:T(8,128)(2,1)} custom-call(s32[14]{0:T(128)S(1)} %stack.51.scal, bf16[512,512]{1,0:T(8,128)(2,1)} %copy-done.13, bf16[512,512]{1,0:T(8,128)(2,1)} %copy-done.12, bf16[448,512]{1,0:T(8,128)(2,1)S(1)} %collective-permute-done.6.refs_2_.refs_0_.refs_4_, bf16[448,512]{1,0:T(8,128)(2,1)S(1)} %collective-permute-done.7.refs_3_.refs_4_.refs_5_, ...), custom_call_target="tpu_custom_call" | custom-call | flops 5000000000 | bytes 100000 | tf_op jit(solution)/shard_map/join/pallas_call | solution.py:334
  85.7 0.9 collective-permute-done.37
  86.7 5.8 %collective-permute-done.12.refs_10_.refs_0_ = bf16[448,512]{1,0:T(8,128)(2,1)} collective-permute-done((bf16[448,512]{1,0:T(8,128)(2,1)S(1)}, bf16[448,512]{1,0:T(8,128)(2,1)}, u32[]{:S(2)}, u32[]{:S(2)}) %collective-permute-start.12) | collective-permute-done | bytes 458784 | tf_op jit(solution)/shard_map/ppermute | solution.py:183
  92.5 1.8 %join.3.g_oth = bf16[512,1024]{1,0:T(8,128)(2,1)} custom-call(s32[14]{0:T(128)S(1)} %stack.51.scal, bf16[512,512]{1,0:T(8,128)(2,1)S(1)} %collective-permute-done.10.refs_0_, bf16[512,512]{1,0:T(8,128)(2,1)S(1)} %collective-permute-done.11.refs_1_), custom_call_target="tpu_custom_call" | custom-call | flops 5000000000 | bytes 100000 | tf_op jit(solution)/shard_map/join/pallas_call | solution.py:334
  94.4 2.7 %collective-permute-done.21.refs_11_.refs_4_ = bf16[448,512]{1,0:T(8,128)(2,1)S(1)} collective-permute-done((bf16[448,512]{1,0:T(8,128)(2,1)S(1)}, bf16[448,512]{1,0:T(8,128)(2,1)S(1)}, u32[]{:S(2)}, u32[]{:S(2)}) %collective-permute-start.21) | collective-permute-done | bytes 458784 | tf_op jit(solution)/shard_map/ppermute | solution.py:183
  97.1 1.6 %collective-permute-start.18 = (bf16[448,512]{1,0:T(8,128)(2,1)S(1)}, bf16[448,512]{1,0:T(8,128)(2,1)S(1)}, u32[]{:S(2)}, u32[]{:S(2)}) collective-permute-start(bf16[448,512]{1,0:T(8,128)(2,1)S(1)} %collective-permute-done.8.refs_4_.refs_1_), channel_id=1, source_target_pairs={{0,8},{1,9},{2,10},{3,11},{4,0},{5,1},{6,2},{7,3},{8,16},{9,17},{1... | collective-permute-start | bytes 1376264 | tf_op jit(solution)/shard_map/ppermute | solution.py:183
  99.2 10.9 %slabs.4.refs_12_ = bf16[512,8192]{1,0:T(8,128)(2,1)} custom-call(s32[14]{0:T(128)S(1)} %stack.51.scal, bf16[512,1024]{1,0:T(8,128)(2,1)} %join.2.g_own, bf16[512,1024]{1,0:T(8,128)(2,1)} %join.3.g_oth, bf16[8192,512]{1,0:T(8,128)(2,1)} %wk.13, bf16[8192,512]{1,0:T(8,128)(2,1)} %wv.13, bf16[448,512]{1,0:T(8,128)(2,1)S(1)} %collective-permute-done.refs_0_, ...), custom_call_target="tpu_custom_call" | custom-call | flops 5000000000 | bytes 100000 | tf_op jit(solution)/shard_map/slabs/pallas_call | solution.py:443
  110.9 1.6 %collective-permute-start.13 = (bf16[448,512]{1,0:T(8,128)(2,1)}, bf16[448,512]{1,0:T(8,128)(2,1)S(1)}, u32[]{:S(2)}, u32[]{:S(2)}) collective-permute-start(bf16[448,512]{1,0:T(8,128)(2,1)} %collective-permute-done.12.refs_10_.refs_0_), channel_id=1, source_target_pairs={{0,8},{1,9},{2,10},{3,11},{4,0},{5,1},{6,2},{7,3},{8,16},{9,17},{1... | collective-permute-start | bytes 1376264 | tf_op jit(solution)/shard_map/ppermute | solution.py:183
  114.2 11.7 %slabs.5.refs_8_ = bf16[512,8192]{1,0:T(8,128)(2,1)} custom-call(s32[14]{0:T(128)S(1)} %stack.51.scal, bf16[512,1024]{1,0:T(8,128)(2,1)} %join.2.g_own, bf16[512,1024]{1,0:T(8,128)(2,1)} %join.3.g_oth, bf16[8192,512]{1,0:T(8,128)(2,1)} %wk.13, bf16[8192,512]{1,0:T(8,128)(2,1)} %wv.13, ...), custom_call_target="tpu_custom_call", output_to_operand_aliasing={{}: (17, {})} | custom-call | flops 5000000000 | bytes 100000 | tf_op jit(solution)/shard_map/slabs/pallas_call | solution.py:443
  128.2 8.6 %slabs.6.refs_4_ = bf16[512,8192]{1,0:T(8,128)(2,1)} custom-call(s32[14]{0:T(128)S(1)} %stack.51.scal, bf16[512,1024]{1,0:T(8,128)(2,1)} %join.2.g_own, bf16[512,1024]{1,0:T(8,128)(2,1)} %join.3.g_oth, bf16[8192,512]{1,0:T(8,128)(2,1)} %wk.13, bf16[8192,512]{1,0:T(8,128)(2,1)} %wv.13, ...), custom_call_target="tpu_custom_call", output_to_operand_aliasing={{}: (13, {})} | custom-call | flops 5000000000 | bytes 100000 | tf_op jit(solution)/shard_map/slabs/pallas_call | solution.py:443
  136.8 6.0 %slabs.7 = bf16[512,8192]{1,0:T(8,128)(2,1)} custom-call(s32[14]{0:T(128)S(1)} %stack.51.scal, bf16[512,1024]{1,0:T(8,128)(2,1)} %join.2.g_own, bf16[512,1024]{1,0:T(8,128)(2,1)} %join.3.g_oth, bf16[8192,512]{1,0:T(8,128)(2,1)} %wk.13, bf16[8192,512]{1,0:T(8,128)(2,1)} %wv.13, ...), custom_call_target="tpu_custom_call", output_to_operand_aliasing={{}: (9, {})} | custom-call | flops 5000000000 | bytes 100000 | tf_op jit(solution)/shard_map/slabs/pallas_call | solution.py:443
  (123 shorter events, 12.2 us)
Async XLA Ops:
  2.8 18.6 %collective-permute-start = (bf16[448,512]{1,0:T(8,128)(2,1)S(1)}, bf16[448,512]{1,0:T(8,128)(2,1)S(1)}, u32[]{:S(2)}, u32[]{:S(2)}) collective-permute-start(bf16[448,512]{1,0:T(8,128)(2,1)S(1)} %pick.3.refs_0_), channel_id=1, source_target_pairs={{0,1},{1,0},{2,3},{3,2},{4,5},{5,4},{6,7},{7,6},{8,9},{9,8},{10,11... | collective-permute-start | bytes 1376264 | tf_op jit(solution)/shard_map/ppermute | solution.py:171
  7.4 19.5 %collective-permute-start.1 = (bf16[448,512]{1,0:T(8,128)(2,1)S(1)}, bf16[448,512]{1,0:T(8,128)(2,1)S(1)}, u32[]{:S(2)}, u32[]{:S(2)}) collective-permute-start(bf16[448,512]{1,0:T(8,128)(2,1)S(1)} %pick.4.refs_1_), channel_id=1, source_target_pairs={{0,1},{1,0},{2,3},{3,2},{4,5},{5,4},{6,7},{7,6},{8,9},{9,8},{10,11... | collective-permute-start | bytes 1376264 | tf_op jit(solution)/shard_map/ppermute | solution.py:171
  10.4 31.7 %collective-permute-start.36 = (bf16[64,512]{1,0:T(8,128)(2,1)S(1)}, bf16[64,512]{1,0:T(8,128)(2,1)S(1)}, u32[]{:S(2)}, u32[]{:S(2)}) collective-permute-start(bf16[64,512]{1,0:T(8,128)(2,1)S(1)} %convolution_convert_fusion.proj_own), channel_id=1, source_target_pairs={{0,1},{1,0},{2,3},{3,2},{4,5},{5,4},{6,7},{7,6},{8,9},{9,8},{10,11... | collective-permute-start | bytes 196616 | tf_op jit(solution)/shard_map/ppermute | solution.py:171
  28.7 40.0 %collective-permute-start.28 = (bf16[1024,512]{1,0:T(8,128)(2,1)S(1)}, bf16[1024,512]{1,0:T(8,128)(2,1)}, u32[]{:S(2)}, u32[]{:S(2)}) collective-permute-start(bf16[1024,512]{1,0:T(8,128)(2,1)S(1)} %pick.5), channel_id=1, source_target_pairs={{0,1},{1,0},{2,3},{3,2},{4,5},{5,4},{6,7},{7,6},{8,9},{9,8},{10,11... | collective-permute-start | bytes 3145736 | tf_op jit(solution)/shard_map/ppermute | solution.py:171
  30.5 13.5 %collective-permute-start.4 = (bf16[448,512]{1,0:T(8,128)(2,1)S(1)}, bf16[448,512]{1,0:T(8,128)(2,1)S(1)}, u32[]{:S(2)}, u32[]{:S(2)}) collective-permute-start(bf16[448,512]{1,0:T(8,128)(2,1)S(1)} %collective-permute-done.refs_0_), channel_id=1, source_target_pairs={{0,8},{1,9},{2,10},{3,11},{4,0},{5,1},{6,2},{7,3},{8,16},{9,17},{1... | collective-permute-start | bytes 1376264 | tf_op jit(solution)/shard_map/ppermute | solution.py:183
  32.0 12.1 %collective-permute-start.5 = (bf16[448,512]{1,0:T(8,128)(2,1)S(1)}, bf16[448,512]{1,0:T(8,128)(2,1)S(1)}, u32[]{:S(2)}, u32[]{:S(2)}) collective-permute-start(bf16[448,512]{1,0:T(8,128)(2,1)S(1)} %collective-permute-done.refs_0_), channel_id=1, source_target_pairs={{0,4},{1,5},{2,6},{3,7},{4,12},{5,13},{6,14},{7,15},{8,0},{9,1},{1... | collective-permute-start | bytes 1376264 | tf_op jit(solution)/shard_map/ppermute | solution.py:183
  41.8 24.7 %collective-permute-start.10 = (bf16[512,512]{1,0:T(8,128)(2,1)S(1)}, bf16[512,512]{1,0:T(8,128)(2,1)S(1)}, u32[]{:S(2)}, u32[]{:S(2)}) collective-permute-start(bf16[512,512]{1,0:T(8,128)(2,1)S(1)} %get-tuple-element.19.refs_2_), channel_id=1, source_target_pairs={{0,1},{1,0},{2,3},{3,2},{4,5},{5,4},{6,7},{7,6},{8,9},{9,8},{10,11... | collective-permute-start | bytes 1572872 | tf_op jit(solution)/shard_map/ppermute | solution.py:171
  44.2 11.1 %collective-permute-start.30 = (bf16[448,512]{1,0:T(8,128)(2,1)S(1)}, bf16[448,512]{1,0:T(8,128)(2,1)S(1)}, u32[]{:S(2)}, u32[]{:S(2)}) collective-permute-start(bf16[448,512]{1,0:T(8,128)(2,1)S(1)} %collective-permute-done.refs_0_), channel_id=1, source_target_pairs={{0,2},{1,3},{2,0},{3,1},{4,6},{5,7},{6,4},{7,5},{8,10},{9,11},{10,... | collective-permute-start | bytes 1376264 | tf_op jit(solution)/shard_map/ppermute | solution.py:175
  52.8 12.0 %collective-permute-start.31 = (bf16[448,512]{1,0:T(8,128)(2,1)S(1)}, bf16[448,512]{1,0:T(8,128)(2,1)S(1)}, u32[]{:S(2)}, u32[]{:S(2)}) collective-permute-start(bf16[448,512]{1,0:T(8,128)(2,1)S(1)} %collective-permute-done.1.refs_1_), channel_id=1, source_target_pairs={{0,2},{1,3},{2,0},{3,1},{4,6},{5,7},{6,4},{7,5},{8,10},{9,11},{10,... | collective-permute-start | bytes 1376264 | tf_op jit(solution)/shard_map/ppermute | solution.py:175
  53.4 14.7 %collective-permute-start.6 = (bf16[448,512]{1,0:T(8,128)(2,1)S(1)}, bf16[448,512]{1,0:T(8,128)(2,1)S(1)}, u32[]{:S(2)}, u32[]{:S(2)}) collective-permute-start(bf16[448,512]{1,0:T(8,128)(2,1)S(1)} %collective-permute-done.4.refs_0_.refs_4_), channel_id=1, source_target_pairs={{0,8},{1,9},{2,10},{3,11},{4,0},{5,1},{6,2},{7,3},{8,16},{9,17},{1... | collective-permute-start | bytes 1376264 | tf_op jit(solution)/shard_map/ppermute | solution.py:183
  55.2 13.3 %collective-permute-start.7 = (bf16[448,512]{1,0:T(8,128)(2,1)S(1)}, bf16[448,512]{1,0:T(8,128)(2,1)S(1)}, u32[]{:S(2)}, u32[]{:S(2)}) collective-permute-start(bf16[448,512]{1,0:T(8,128)(2,1)S(1)} %collective-permute-done.5.refs_1_.refs_8_), channel_id=1, source_target_pairs={{0,4},{1,5},{2,6},{3,7},{4,12},{5,13},{6,14},{7,15},{8,0},{9,1},{1... | collective-permute-start | bytes 1376264 | tf_op jit(solution)/shard_map/ppermute | solution.py:183
  64.8 20.5 %collective-permute-start.11 = (bf16[512,512]{1,0:T(8,128)(2,1)S(1)}, bf16[512,512]{1,0:T(8,128)(2,1)S(1)}, u32[]{:S(2)}, u32[]{:S(2)}) collective-permute-start(bf16[512,512]{1,0:T(8,128)(2,1)S(1)} %get-tuple-element.20.refs_3_), channel_id=1, source_target_pairs={{0,1},{1,0},{2,3},{3,2},{4,5},{5,4},{6,7},{7,6},{8,9},{9,8},{10,11... | collective-permute-start | bytes 1572872 | tf_op jit(solution)/shard_map/ppermute | solution.py:171
  66.5 11.7 %collective-permute-start.8 = (bf16[448,512]{1,0:T(8,128)(2,1)S(1)}, bf16[448,512]{1,0:T(8,128)(2,1)S(1)}, u32[]{:S(2)}, u32[]{:S(2)}) collective-permute-start(bf16[448,512]{1,0:T(8,128)(2,1)S(1)} %collective-permute-done.2.refs_0_.refs_5_), channel_id=1, source_target_pairs={{0,8},{1,9},{2,10},{3,11},{4,0},{5,1},{6,2},{7,3},{8,16},{9,17},{1... | collective-permute-start | bytes 1376264 | tf_op jit(solution)/shard_map/ppermute | solution.py:183
  68.1 11.4 %collective-permute-start.9 = (bf16[448,512]{1,0:T(8,128)(2,1)S(1)}, bf16[448,512]{1,0:T(8,128)(2,1)S(1)}, u32[]{:S(2)}, u32[]{:S(2)}) collective-permute-start(bf16[448,512]{1,0:T(8,128)(2,1)S(1)} %collective-permute-done.3.refs_1_.refs_9_), channel_id=1, source_target_pairs={{0,4},{1,5},{2,6},{3,7},{4,12},{5,13},{6,14},{7,15},{8,0},{9,1},{1... | collective-permute-start | bytes 1376264 | tf_op jit(solution)/shard_map/ppermute | solution.py:183
  68.5 10.9 %collective-permute-start.32 = (bf16[448,512]{1,0:T(8,128)(2,1)S(1)}, bf16[448,512]{1,0:T(8,128)(2,1)S(1)}, u32[]{:S(2)}, u32[]{:S(2)}) collective-permute-start(bf16[448,512]{1,0:T(8,128)(2,1)S(1)} %collective-permute-done.4.refs_0_.refs_4_), channel_id=1, source_target_pairs={{0,2},{1,3},{2,0},{3,1},{4,6},{5,7},{6,4},{7,5},{8,10},{9,11},{10,... | collective-permute-start | bytes 1376264 | tf_op jit(solution)/shard_map/ppermute | solution.py:175
  68.6 12.5 %collective-permute-start.33 = (bf16[448,512]{1,0:T(8,128)(2,1)S(1)}, bf16[448,512]{1,0:T(8,128)(2,1)S(1)}, u32[]{:S(2)}, u32[]{:S(2)}) collective-permute-start(bf16[448,512]{1,0:T(8,128)(2,1)S(1)} %collective-permute-done.2.refs_0_.refs_5_), channel_id=1, source_target_pairs={{0,2},{1,3},{2,0},{3,1},{4,6},{5,7},{6,4},{7,5},{8,10},{9,11},{10,... | collective-permute-start | bytes 1376264 | tf_op jit(solution)/shard_map/ppermute | solution.py:175
  79.5 13.0 %collective-permute-start.12 = (bf16[448,512]{1,0:T(8,128)(2,1)S(1)}, bf16[448,512]{1,0:T(8,128)(2,1)}, u32[]{:S(2)}, u32[]{:S(2)}) collective-permute-start(bf16[448,512]{1,0:T(8,128)(2,1)S(1)} %collective-permute-done.6.refs_2_.refs_0_.refs_4_), channel_id=1, source_target_pairs={{0,8},{1,9},{2,10},{3,11},{4,0},{5,1},{6,2},{7,3},{8,16},{9,17},{1... | collective-permute-start | bytes 1376264 | tf_op jit(solution)/shard_map/ppermute | solution.py:183
  84.7 12.4 %collective-permute-start.21 = (bf16[448,512]{1,0:T(8,128)(2,1)S(1)}, bf16[448,512]{1,0:T(8,128)(2,1)S(1)}, u32[]{:S(2)}, u32[]{:S(2)}) collective-permute-start(bf16[448,512]{1,0:T(8,128)(2,1)S(1)} %collective-permute-done.7.refs_3_.refs_4_.refs_5_), channel_id=1, source_target_pairs={{0,4},{1,5},{2,6},{3,7},{4,12},{5,13},{6,14},{7,15},{8,0},{9,1},{1... | collective-permute-start | bytes 1376264 | tf_op jit(solution)/shard_map/ppermute | solution.py:183
  85.2 11.9 %collective-permute-start.24 = (bf16[448,512]{1,0:T(8,128)(2,1)S(1)}, bf16[448,512]{1,0:T(8,128)(2,1)S(1)}, u32[]{:S(2)}, u32[]{:S(2)}) collective-permute-start(bf16[448,512]{1,0:T(8,128)(2,1)S(1)} %collective-permute-done.6.refs_2_.refs_0_.refs_4_), channel_id=1, source_target_pairs={{0,2},{1,3},{2,0},{3,1},{4,6},{5,7},{6,4},{7,5},{8,10},{9,11},{10,... | collective-permute-start | bytes 1376264 | tf_op jit(solution)/shard_map/ppermute | solution.py:175
  85.2 13.5 %collective-permute-start.25 = (bf16[448,512]{1,0:T(8,128)(2,1)S(1)}, bf16[448,512]{1,0:T(8,128)(2,1)S(1)}, u32[]{:S(2)}, u32[]{:S(2)}) collective-permute-start(bf16[448,512]{1,0:T(8,128)(2,1)S(1)} %collective-permute-done.8.refs_4_.refs_1_), channel_id=1, source_target_pairs={{0,2},{1,3},{2,0},{3,1},{4,6},{5,7},{6,4},{7,5},{8,10},{9,11},{10,... | collective-permute-start | bytes 1376264 | tf_op jit(solution)/shard_map/ppermute | solution.py:175
  86.7 12.5 %collective-permute-start.26 = (bf16[448,512]{1,0:T(8,128)(2,1)S(1)}, bf16[448,512]{1,0:T(8,128)(2,1)S(1)}, u32[]{:S(2)}, u32[]{:S(2)}) collective-permute-start(bf16[448,512]{1,0:T(8,128)(2,1)S(1)} %collective-permute-done.7.refs_3_.refs_4_.refs_5_), channel_id=1, source_target_pairs={{0,2},{1,3},{2,0},{3,1},{4,6},{5,7},{6,4},{7,5},{8,10},{9,11},{10,... | collective-permute-start | bytes 1376264 | tf_op jit(solution)/shard_map/ppermute | solution.py:175
  92.5 20.7 %collective-permute-start.29 = (bf16[1024,512]{1,0:T(8,128)(2,1)}, bf16[1024,512]{1,0:T(8,128)(2,1)S(1)}, u32[]{:S(2)}, u32[]{:S(2)}) collective-permute-start(bf16[1024,512]{1,0:T(8,128)(2,1)} %collective-permute-done.28.refs_8_.refs_6_), channel_id=1, source_target_pairs={{0,2},{1,3},{2,0},{3,1},{4,6},{5,7},{6,4},{7,5},{8,10},{9,11},{10,... | collective-permute-start | bytes 3145736 | tf_op jit(solution)/shard_map/ppermute | solution.py:175
  97.1 13.8 %collective-permute-start.27 = (bf16[448,512]{1,0:T(8,128)(2,1)S(1)}, bf16[448,512]{1,0:T(8,128)(2,1)S(1)}, u32[]{:S(2)}, u32[]{:S(2)}) collective-permute-start(bf16[448,512]{1,0:T(8,128)(2,1)S(1)} %collective-permute-done.9.refs_5_), channel_id=1, source_target_pairs={{0,2},{1,3},{2,0},{3,1},{4,6},{5,7},{6,4},{7,5},{8,10},{9,11},{10,... | collective-permute-start | bytes 1376264 | tf_op jit(solution)/shard_map/ppermute | solution.py:175
  97.1 15.6 %collective-permute-start.18 = (bf16[448,512]{1,0:T(8,128)(2,1)S(1)}, bf16[448,512]{1,0:T(8,128)(2,1)S(1)}, u32[]{:S(2)}, u32[]{:S(2)}) collective-permute-start(bf16[448,512]{1,0:T(8,128)(2,1)S(1)} %collective-permute-done.8.refs_4_.refs_1_), channel_id=1, source_target_pairs={{0,8},{1,9},{2,10},{3,11},{4,0},{5,1},{6,2},{7,3},{8,16},{9,17},{1... | collective-permute-start | bytes 1376264 | tf_op jit(solution)/shard_map/ppermute | solution.py:183
  98.7 13.8 %collective-permute-start.14 = (bf16[448,512]{1,0:T(8,128)(2,1)S(1)}, bf16[448,512]{1,0:T(8,128)(2,1)S(1)}, u32[]{:S(2)}, u32[]{:S(2)}) collective-permute-start(bf16[448,512]{1,0:T(8,128)(2,1)S(1)} %collective-permute-done.9.refs_5_), channel_id=1, source_target_pairs={{0,4},{1,5},{2,6},{3,7},{4,12},{5,13},{6,14},{7,15},{8,0},{9,1},{1... | collective-permute-start | bytes 1376264 | tf_op jit(solution)/shard_map/ppermute | solution.py:183
  99.2 14.0 %collective-permute-start.19 = (bf16[448,512]{1,0:T(8,128)(2,1)}, bf16[448,512]{1,0:T(8,128)(2,1)S(1)}, u32[]{:S(2)}, u32[]{:S(2)}) collective-permute-start(bf16[448,512]{1,0:T(8,128)(2,1)} %collective-permute-done.12.refs_10_.refs_0_), channel_id=1, source_target_pairs={{0,2},{1,3},{2,0},{3,1},{4,6},{5,7},{6,4},{7,5},{8,10},{9,11},{10,... | collective-permute-start | bytes 1376264 | tf_op jit(solution)/shard_map/ppermute | solution.py:175
  110.9 15.1 %collective-permute-start.13 = (bf16[448,512]{1,0:T(8,128)(2,1)}, bf16[448,512]{1,0:T(8,128)(2,1)S(1)}, u32[]{:S(2)}, u32[]{:S(2)}) collective-permute-start(bf16[448,512]{1,0:T(8,128)(2,1)} %collective-permute-done.12.refs_10_.refs_0_), channel_id=1, source_target_pairs={{0,8},{1,9},{2,10},{3,11},{4,0},{5,1},{6,2},{7,3},{8,16},{9,17},{1... | collective-permute-start | bytes 1376264 | tf_op jit(solution)/shard_map/ppermute | solution.py:183
  112.5 14.1 %collective-permute-start.23 = (bf16[448,512]{1,0:T(8,128)(2,1)S(1)}, bf16[448,512]{1,0:T(8,128)(2,1)S(1)}, u32[]{:S(2)}, u32[]{:S(2)}) collective-permute-start(bf16[448,512]{1,0:T(8,128)(2,1)S(1)} %collective-permute-done.14.refs_5_), channel_id=1, source_target_pairs={{0,2},{1,3},{2,0},{3,1},{4,6},{5,7},{6,4},{7,5},{8,10},{9,11},{10,... | collective-permute-start | bytes 1376264 | tf_op jit(solution)/shard_map/ppermute | solution.py:175
  112.7 13.8 %collective-permute-start.15 = (bf16[448,512]{1,0:T(8,128)(2,1)S(1)}, bf16[448,512]{1,0:T(8,128)(2,1)S(1)}, u32[]{:S(2)}, u32[]{:S(2)}) collective-permute-start(bf16[448,512]{1,0:T(8,128)(2,1)S(1)} %collective-permute-done.14.refs_5_), channel_id=1, source_target_pairs={{0,4},{1,5},{2,6},{3,7},{4,12},{5,13},{6,14},{7,15},{8,0},{9,1},{1... | collective-permute-start | bytes 1376264 | tf_op jit(solution)/shard_map/ppermute | solution.py:183
  113.2 13.5 %collective-permute-start.20 = (bf16[448,512]{1,0:T(8,128)(2,1)S(1)}, bf16[448,512]{1,0:T(8,128)(2,1)S(1)}, u32[]{:S(2)}, u32[]{:S(2)}) collective-permute-start(bf16[448,512]{1,0:T(8,128)(2,1)S(1)} %collective-permute-done.18.refs_1_), channel_id=1, source_target_pairs={{0,2},{1,3},{2,0},{3,1},{4,6},{5,7},{6,4},{7,5},{8,10},{9,11},{10,... | collective-permute-start | bytes 1376264 | tf_op jit(solution)/shard_map/ppermute | solution.py:175
  113.2 13.4 %collective-permute-start.22 = (bf16[448,512]{1,0:T(8,128)(2,1)S(1)}, bf16[448,512]{1,0:T(8,128)(2,1)S(1)}, u32[]{:S(2)}, u32[]{:S(2)}) collective-permute-start(bf16[448,512]{1,0:T(8,128)(2,1)S(1)} %collective-permute-done.21.refs_11_.refs_4_), channel_id=1, source_target_pairs={{0,2},{1,3},{2,0},{3,1},{4,6},{5,7},{6,4},{7,5},{8,10},{9,11},{10,... | collective-permute-start | bytes 1376264 | tf_op jit(solution)/shard_map/ppermute | solution.py:175
  126.0 10.8 %collective-permute-start.16 = (bf16[448,512]{1,0:T(8,128)(2,1)S(1)}, bf16[448,512]{1,0:T(8,128)(2,1)S(1)}, u32[]{:S(2)}, u32[]{:S(2)}) collective-permute-start(bf16[448,512]{1,0:T(8,128)(2,1)S(1)} %collective-permute-done.13.refs_0_), channel_id=1, source_target_pairs={{0,2},{1,3},{2,0},{3,1},{4,6},{5,7},{6,4},{7,5},{8,10},{9,11},{10,... | collective-permute-start | bytes 1376264 | tf_op jit(solution)/shard_map/ppermute | solution.py:175
  (35 other events, 348.1 us)

commit v3 on v2

--- a/solution.py
+++ b/solution.py
@@ -566,7 +566,7 @@
     doc_own = lax.dynamic_slice_in_dim(docq, x * half, half, 1)
     doc_oth = lax.dynamic_slice_in_dim(docq, (1 - x) * half, half, 1)
     mine, theirs = doc_sums(
-        scal, doc_own, doc_oth, proj, proj_oth, key_basis.T, value_basis.T, owns, sends, [*stage(2, 0), *rest_got]
+        scal, doc_own, doc_oth, proj, proj_oth, key_basis.T, value_basis.T, owns, sends, rest_got
     )
     docs = (mine + send_x(theirs)).reshape(DOCS // 2, RANK, 2 * RANK)
 

time: 143 us -> 143 us (level)
  no operation moved by 1% of the time
where the time goes in v3:
time: 143 us; the launch traced here: 142 us
  Pallas kernels  85.3 us (60%)
  starting transfers between devices  27 us (19%)
  waiting for transfers between devices  21.5 us (15%)
  local copies, waits for them, and re-layouts  3.86 us (3%)
  matrix products  2.66 us (2%)
    pallas_call x4, Pallas kernels, slabs(): pl.pallas_call(functools.partial(slabs_kernel, widths, places, counts, le...  37.2 us
    pallas_call x4, Pallas kernels, attention(): pl.pallas_call(attention_kernel, out_shape=(out, out), grid_spec=pltpu.Pr...  34.2 us
    ppermute x14, waiting for transfers between devices, send_ring(): return lax.ppermute(a, ('dp', 'tensor'), pairs(move))  15.1 us
    ppermute x14, starting transfers between devices, send_ring(): return lax.ppermute(a, ('dp', 'tensor'), pairs(move))  14.3 us
    ppermute x7, starting transfers between devices, send_x(): lax.ppermute(a, ('dp', 'tensor'), pairs(lambda z, y, c, x: (z, y, c, 1 -...  9.59 us
    ppermute x7, waiting for transfers between devices, send_x(): lax.ppermute(a, ('dp', 'tensor'), pairs(lambda z, y, c, x: (z, y, c, 1 -...  6.39 us
    pallas_call x3, Pallas kernels, pick(): pl.pallas_call(functools.partial(pick_kernel, at), out_shape=jax.ShapeDty...  5.21 us
    pallas_call x2, Pallas kernels, join(): pl.pallas_call(functools.partial(join_kernel, swap), out_shape=out, grid_...  4.87 us
  transfers between devices with their start and end apart: 38, of which 6 were waited for; matrix products, arithmetic and copies ran while one was open for 3% of the time, Pallas kernels for 54%

profile of v3, /device:TPU:0, one launch (start us, length us, event | category | flops | bytes accessed | tf_op | source)
XLA Modules:
  0.0 142.3 jit_solution(13024150629036376295)
XLA Ops:
  0.9 1.9 %pick.3.refs_0_ = bf16[448,512]{1,0:T(8,128)(2,1)S(1)} custom-call(s32[14]{0:T(128)S(1)} %stack.51.scal, bf16[8192,512]{1,0:T(8,128)(2,1)} %wk.13, bf16[8192,512]{1,0:T(8,128)(2,1)} %wv.13), custom_call_target="tpu_custom_call" | custom-call | flops 5000000000 | bytes 100000 | tf_op jit(solution)/shard_map/pick/pallas_call | solution.py:482
  2.8 3.0 %collective-permute-start = (bf16[448,512]{1,0:T(8,128)(2,1)S(1)}, bf16[448,512]{1,0:T(8,128)(2,1)S(1)}, u32[]{:S(2)}, u32[]{:S(2)}) collective-permute-start(bf16[448,512]{1,0:T(8,128)(2,1)S(1)} %pick.3.refs_0_), channel_id=1, source_target_pairs={{0,1},{1,0},{2,3},{3,2},{4,5},{5,4},{6,7},{7,6},{8,9},{9,8},{10,11... | collective-permute-start | bytes 1376264 | tf_op jit(solution)/shard_map/ppermute | solution.py:171
  5.8 1.6 %pick.4.refs_1_ = bf16[448,512]{1,0:T(8,128)(2,1)S(1)} custom-call(s32[14]{0:T(128)S(1)} %stack.51.scal, bf16[8192,512]{1,0:T(8,128)(2,1)} %wk.13, bf16[8192,512]{1,0:T(8,128)(2,1)} %wv.13), custom_call_target="tpu_custom_call" | custom-call | flops 5000000000 | bytes 100000 | tf_op jit(solution)/shard_map/pick/pallas_call | solution.py:482
  7.8 2.7 %convolution_convert_fusion.proj_own = bf16[64,512]{1,0:T(8,128)(2,1)S(1)} fusion(bf16[8192,64]{0,1:T(8,128)(2,1)S(1)} %copy-done, bf16[512,8192]{1,0:T(8,128)(2,1)S(1)} %bitcast.29), kind=kOutput, calls=%fused_computation.1 | convolution fusion | flops 536903680 | bytes 9502720 | tf_op jit(solution)/shard_map/dot_general | solution.py:545
  10.4 1.8 %collective-permute-start.36 = (bf16[64,512]{1,0:T(8,128)(2,1)S(1)}, bf16[64,512]{1,0:T(8,128)(2,1)S(1)}, u32[]{:S(2)}, u32[]{:S(2)}) collective-permute-start(bf16[64,512]{1,0:T(8,128)(2,1)S(1)} %convolution_convert_fusion.proj_own), channel_id=1, source_target_pairs={{0,1},{1,0},{2,3},{3,2},{4,5},{5,4},{6,7},{7,6},{8,9},{9,8},{10,11... | collective-permute-start | bytes 196616 | tf_op jit(solution)/shard_map/ppermute | solution.py:171
  12.9 8.5 %attention_back.4 = (bf16[512,512]{1,0:T(8,128)(2,1)S(1)}, bf16[512,512]{1,0:T(8,128)(2,1)S(1)}) custom-call(s32[14]{0:T(128)S(1)} %stack.51.scal, s32[1,1024]{1,0:T(1,128)S(1)} %bitcast.20, bf16[1024,2048]{1,0:T(8,128)(2,1)} %q_ref.7, bf16[1024,2048]{1,0:T(8,128)(2,1)} %do_ref.7, bf16[1024,512]{1,0:T(8,128)(2,1)} %k_ref.7, bf16[1024,512]{1,0:T(8,128)(2,1)} %v_ref.7, ...), custom_call_target="tpu_custom_call" | custom-call | flops 5000000000 | bytes 100000 | tf_op jit(solution)/shard_map/attention_back/pallas_call | solution.py:243
  21.4 5.4 %collective-permute-done.1.refs_1_ = bf16[448,512]{1,0:T(8,128)(2,1)S(1)} collective-permute-done((bf16[448,512]{1,0:T(8,128)(2,1)S(1)}, bf16[448,512]{1,0:T(8,128)(2,1)S(1)}, u32[]{:S(2)}, u32[]{:S(2)}) %collective-permute-start.1) | collective-permute-done | bytes 458784 | tf_op jit(solution)/shard_map/ppermute | solution.py:171
  26.9 1.8 %pick.5 = bf16[1024,512]{1,0:T(8,128)(2,1)S(1)} custom-call(s32[14]{0:T(128)S(1)} %stack.51.scal, bf16[8192,512]{1,0:T(8,128)(2,1)} %wk.13, bf16[8192,512]{1,0:T(8,128)(2,1)} %wv.13, bf16[448,512]{1,0:T(8,128)(2,1)S(1)} %collective-permute-done.refs_0_, bf16[448,512]{1,0:T(8,128)(2,1)S(1)} %collective-permute-done.1.refs_1_), custom_call_target="tpu_custom_call" | custom-call | flops 5000000000 | bytes 100000 | tf_op jit(solution)/shard_map/pick/pallas_call | solution.py:482
  28.7 1.8 %collective-permute-start.28 = (bf16[1024,512]{1,0:T(8,128)(2,1)S(1)}, bf16[1024,512]{1,0:T(8,128)(2,1)}, u32[]{:S(2)}, u32[]{:S(2)}) collective-permute-start(bf16[1024,512]{1,0:T(8,128)(2,1)S(1)} %pick.5), channel_id=1, source_target_pairs={{0,1},{1,0},{2,3},{3,2},{4,5},{5,4},{6,7},{7,6},{8,9},{9,8},{10,11... | collective-permute-start | bytes 3145736 | tf_op jit(solution)/shard_map/ppermute | solution.py:171
  30.5 1.6 %collective-permute-start.4 = (bf16[448,512]{1,0:T(8,128)(2,1)S(1)}, bf16[448,512]{1,0:T(8,128)(2,1)S(1)}, u32[]{:S(2)}, u32[]{:S(2)}) collective-permute-start(bf16[448,512]{1,0:T(8,128)(2,1)S(1)} %collective-permute-done.refs_0_), channel_id=1, source_target_pairs={{0,8},{1,9},{2,10},{3,11},{4,0},{5,1},{6,2},{7,3},{8,16},{9,17},{1... | collective-permute-start | bytes 1376264 | tf_op jit(solution)/shard_map/ppermute | solution.py:183
  32.5 8.5 %attention_back.5 = (bf16[512,512]{1,0:T(8,128)(2,1)S(1)}, bf16[512,512]{1,0:T(8,128)(2,1)S(1)}) custom-call(s32[14]{0:T(128)S(1)} %stack.51.scal, s32[1,1024]{1,0:T(1,128)S(1)} %bitcast.21, bf16[1024,2048]{1,0:T(8,128)(2,1)} %q_ref.7, bf16[1024,2048]{1,0:T(8,128)(2,1)} %do_ref.7, ...), custom_call_target="tpu_custom_call", output_to_operand_aliasing={{0}: (8, {}), {1}: (9, {})} | custom-call | flops 5000000000 | bytes 100000 | tf_op jit(solution)/shard_map/attention_back/pallas_call | solution.py:243
  42.1 1.8 %collective-permute-start.2 = (bf16[448,512]{1,0:T(8,128)(2,1)S(1)}, bf16[448,512]{1,0:T(8,128)(2,1)S(1)}, u32[]{:S(2)}, u32[]{:S(2)}) collective-permute-start(bf16[448,512]{1,0:T(8,128)(2,1)S(1)} %collective-permute-done.1.refs_1_), channel_id=1, source_target_pairs={{0,8},{1,9},{2,10},{3,11},{4,0},{5,1},{6,2},{7,3},{8,16},{9,17},{1... | collective-permute-start | bytes 1376264 | tf_op jit(solution)/shard_map/ppermute | solution.py:183
  44.2 8.6 %attention_back.6 = (bf16[512,512]{1,0:T(8,128)(2,1)S(1)}, bf16[512,512]{1,0:T(8,128)(2,1)S(1)}) custom-call(s32[14]{0:T(128)S(1)} %stack.51.scal, s32[1,1024]{1,0:T(1,128)S(1)} %bitcast.22, bf16[1024,2048]{1,0:T(8,128)(2,1)} %q_ref.7, bf16[1024,2048]{1,0:T(8,128)(2,1)} %do_ref.7, bf16[1024,512]{1,0:T(8,128)(2,1)} %k_ref.7, bf16[1024,512]{1,0:T(8,128)(2,1)} %v_ref.7, ...), custom_call_target="tpu_custom_call" | custom-call | flops 5000000000 | bytes 100000 | tf_op jit(solution)/shard_map/attention_back/pallas_call | solution.py:243
  53.4 1.8 %collective-permute-start.6 = (bf16[448,512]{1,0:T(8,128)(2,1)S(1)}, bf16[448,512]{1,0:T(8,128)(2,1)S(1)}, u32[]{:S(2)}, u32[]{:S(2)}) collective-permute-start(bf16[448,512]{1,0:T(8,128)(2,1)S(1)} %collective-permute-done.4.refs_0_.refs_4_), channel_id=1, source_target_pairs={{0,8},{1,9},{2,10},{3,11},{4,0},{5,1},{6,2},{7,3},{8,16},{9,17},{1... | collective-permute-start | bytes 1376264 | tf_op jit(solution)/shard_map/ppermute | solution.py:183
  55.4 8.5 %attention_back.7 = (bf16[512,512]{1,0:T(8,128)(2,1)S(1)}, bf16[512,512]{1,0:T(8,128)(2,1)S(1)}) custom-call(s32[14]{0:T(128)S(1)} %stack.51.scal, s32[1,1024]{1,0:T(1,128)S(1)} %bitcast.23, bf16[1024,2048]{1,0:T(8,128)(2,1)} %q_ref.7, bf16[1024,2048]{1,0:T(8,128)(2,1)} %do_ref.7, ...), custom_call_target="tpu_custom_call", output_to_operand_aliasing={{0}: (8, {}), {1}: (9, {})} | custom-call | flops 5000000000 | bytes 100000 | tf_op jit(solution)/shard_map/attention_back/pallas_call | solution.py:243
  64.0 1.8 %collective-permute-start.11 = (bf16[512,512]{1,0:T(8,128)(2,1)S(1)}, bf16[512,512]{1,0:T(8,128)(2,1)S(1)}, u32[]{:S(2)}, u32[]{:S(2)}) collective-permute-start(bf16[512,512]{1,0:T(8,128)(2,1)S(1)} %get-tuple-element.20.refs_3_), channel_id=1, source_target_pairs={{0,1},{1,0},{2,3},{3,2},{4,5},{5,4},{6,7},{7,6},{8,9},{9,8},{10,11... | collective-permute-start | bytes 1572872 | tf_op jit(solution)/shard_map/ppermute | solution.py:171
  65.8 1.6 %collective-permute-start.8 = (bf16[448,512]{1,0:T(8,128)(2,1)S(1)}, bf16[448,512]{1,0:T(8,128)(2,1)S(1)}, u32[]{:S(2)}, u32[]{:S(2)}) collective-permute-start(bf16[448,512]{1,0:T(8,128)(2,1)S(1)} %collective-permute-done.2.refs_0_.refs_5_), channel_id=1, source_target_pairs={{0,8},{1,9},{2,10},{3,11},{4,0},{5,1},{6,2},{7,3},{8,16},{9,17},{1... | collective-permute-start | bytes 1376264 | tf_op jit(solution)/shard_map/ppermute | solution.py:183
  68.4 3.8 %doc_sums.1 = (f32[256,128]{1,0:T(8,128)S(1)}, f32[256,128]{1,0:T(8,128)S(1)}) custom-call(s32[14]{0:T(128)S(1)} %stack.51.scal, s32[1,512]{1,0:T(1,128)S(1)} %bitcast.25, s32[1,512]{1,0:T(1,128)S(1)} %bitcast.24, bf16[64,512]{1,0:T(8,128)(2,1)S(1)} %convolution_convert_fusion.proj_own, bf16[64,512]{1,0:T(8,128)(2,1)S(1)} %collective-permute-done.36.proj_oth, ...), custom_call_target="tpu_custom_call" | custom-call | flops 5000000000 | bytes 100000 | tf_op jit(solution)/shard_map/doc_sums/pallas_call | solution.py:298
  72.2 5.2 %collective-permute-done.8.refs_4_.refs_1_ = bf16[448,512]{1,0:T(8,128)(2,1)S(1)} collective-permute-done((bf16[448,512]{1,0:T(8,128)(2,1)S(1)}, bf16[448,512]{1,0:T(8,128)(2,1)S(1)}, u32[]{:S(2)}, u32[]{:S(2)}) %collective-permute-start.8) | collective-permute-done | bytes 458784 | tf_op jit(solution)/shard_map/ppermute | solution.py:183
  77.5 1.3 collective-permute-done.9.refs_5_
  78.8 1.6 %collective-permute-start.12 = (bf16[448,512]{1,0:T(8,128)(2,1)S(1)}, bf16[448,512]{1,0:T(8,128)(2,1)}, u32[]{:S(2)}, u32[]{:S(2)}) collective-permute-start(bf16[448,512]{1,0:T(8,128)(2,1)S(1)} %collective-permute-done.6.refs_2_.refs_0_), channel_id=1, source_target_pairs={{0,8},{1,9},{2,10},{3,11},{4,0},{5,1},{6,2},{7,3},{8,16},{9,17},{1... | collective-permute-start | bytes 1376264 | tf_op jit(solution)/shard_map/ppermute | solution.py:183
  81.0 3.0 %join.2.g_own = bf16[512,1024]{1,0:T(8,128)(2,1)} custom-call(s32[14]{0:T(128)S(1)} %stack.51.scal, bf16[512,512]{1,0:T(8,128)(2,1)} %copy-done.13, bf16[512,512]{1,0:T(8,128)(2,1)} %copy-done.12, bf16[448,512]{1,0:T(8,128)(2,1)S(1)} %collective-permute-done.6.refs_2_.refs_0_, bf16[448,512]{1,0:T(8,128)(2,1)S(1)} %collective-permute-done.7.refs_3_.refs_4_, ...), custom_call_target="tpu_custom_call" | custom-call | flops 5000000000 | bytes 100000 | tf_op jit(solution)/shard_map/join/pallas_call | solution.py:334
  85.0 0.9 collective-permute-done.37
  86.0 5.8 %collective-permute-done.12.refs_10_.refs_0_ = bf16[448,512]{1,0:T(8,128)(2,1)} collective-permute-done((bf16[448,512]{1,0:T(8,128)(2,1)S(1)}, bf16[448,512]{1,0:T(8,128)(2,1)}, u32[]{:S(2)}, u32[]{:S(2)}) %collective-permute-start.12) | collective-permute-done | bytes 458784 | tf_op jit(solution)/shard_map/ppermute | solution.py:183
  91.8 1.8 %join.3.g_oth = bf16[512,1024]{1,0:T(8,128)(2,1)} custom-call(s32[14]{0:T(128)S(1)} %stack.51.scal, bf16[512,512]{1,0:T(8,128)(2,1)S(1)} %collective-permute-done.10.refs_0_, bf16[512,512]{1,0:T(8,128)(2,1)S(1)} %collective-permute-done.11.refs_1_), custom_call_target="tpu_custom_call" | custom-call | flops 5000000000 | bytes 100000 | tf_op jit(solution)/shard_map/join/pallas_call | solution.py:334
  93.7 2.7 %collective-permute-done.21.refs_11_.refs_4_ = bf16[448,512]{1,0:T(8,128)(2,1)S(1)} collective-permute-done((bf16[448,512]{1,0:T(8,128)(2,1)S(1)}, bf16[448,512]{1,0:T(8,128)(2,1)S(1)}, u32[]{:S(2)}, u32[]{:S(2)}) %collective-permute-start.21) | collective-permute-done | bytes 458784 | tf_op jit(solution)/shard_map/ppermute | solution.py:183
  96.4 1.6 %collective-permute-start.18 = (bf16[448,512]{1,0:T(8,128)(2,1)S(1)}, bf16[448,512]{1,0:T(8,128)(2,1)S(1)}, u32[]{:S(2)}, u32[]{:S(2)}) collective-permute-start(bf16[448,512]{1,0:T(8,128)(2,1)S(1)} %collective-permute-done.8.refs_4_.refs_1_), channel_id=1, source_target_pairs={{0,8},{1,9},{2,10},{3,11},{4,0},{5,1},{6,2},{7,3},{8,16},{9,17},{1... | collective-permute-start | bytes 1376264 | tf_op jit(solution)/shard_map/ppermute | solution.py:183
  98.5 10.9 %slabs.4.refs_12_ = bf16[512,8192]{1,0:T(8,128)(2,1)} custom-call(s32[14]{0:T(128)S(1)} %stack.51.scal, bf16[512,1024]{1,0:T(8,128)(2,1)} %join.2.g_own, bf16[512,1024]{1,0:T(8,128)(2,1)} %join.3.g_oth, bf16[8192,512]{1,0:T(8,128)(2,1)} %wk.13, bf16[8192,512]{1,0:T(8,128)(2,1)} %wv.13, bf16[448,512]{1,0:T(8,128)(2,1)S(1)} %collective-permute-done.refs_0_, ...), custom_call_target="tpu_custom_call" | custom-call | flops 5000000000 | bytes 100000 | tf_op jit(solution)/shard_map/slabs/pallas_call | solution.py:443
  110.2 1.6 %collective-permute-start.13 = (bf16[448,512]{1,0:T(8,128)(2,1)}, bf16[448,512]{1,0:T(8,128)(2,1)S(1)}, u32[]{:S(2)}, u32[]{:S(2)}) collective-permute-start(bf16[448,512]{1,0:T(8,128)(2,1)} %collective-permute-done.12.refs_10_.refs_0_), channel_id=1, source_target_pairs={{0,8},{1,9},{2,10},{3,11},{4,0},{5,1},{6,2},{7,3},{8,16},{9,17},{1... | collective-permute-start | bytes 1376264 | tf_op jit(solution)/shard_map/ppermute | solution.py:183
  113.5 11.7 %slabs.5.refs_8_ = bf16[512,8192]{1,0:T(8,128)(2,1)} custom-call(s32[14]{0:T(128)S(1)} %stack.51.scal, bf16[512,1024]{1,0:T(8,128)(2,1)} %join.2.g_own, bf16[512,1024]{1,0:T(8,128)(2,1)} %join.3.g_oth, bf16[8192,512]{1,0:T(8,128)(2,1)} %wk.13, bf16[8192,512]{1,0:T(8,128)(2,1)} %wv.13, ...), custom_call_target="tpu_custom_call", output_to_operand_aliasing={{}: (17, {})} | custom-call | flops 5000000000 | bytes 100000 | tf_op jit(solution)/shard_map/slabs/pallas_call | solution.py:443
  127.5 8.6 %slabs.6.refs_4_ = bf16[512,8192]{1,0:T(8,128)(2,1)} custom-call(s32[14]{0:T(128)S(1)} %stack.51.scal, bf16[512,1024]{1,0:T(8,128)(2,1)} %join.2.g_own, bf16[512,1024]{1,0:T(8,128)(2,1)} %join.3.g_oth, bf16[8192,512]{1,0:T(8,128)(2,1)} %wk.13, bf16[8192,512]{1,0:T(8,128)(2,1)} %wv.13, ...), custom_call_target="tpu_custom_call", output_to_operand_aliasing={{}: (13, {})} | custom-call | flops 5000000000 | bytes 100000 | tf_op jit(solution)/shard_map/slabs/pallas_call | solution.py:443
  136.1 6.0 %slabs.7 = bf16[512,8192]{1,0:T(8,128)(2,1)} custom-call(s32[14]{0:T(128)S(1)} %stack.51.scal, bf16[512,1024]{1,0:T(8,128)(2,1)} %join.2.g_own, bf16[512,1024]{1,0:T(8,128)(2,1)} %join.3.g_oth, bf16[8192,512]{1,0:T(8,128)(2,1)} %wk.13, bf16[8192,512]{1,0:T(8,128)(2,1)} %wv.13, ...), custom_call_target="tpu_custom_call", output_to_operand_aliasing={{}: (9, {})} | custom-call | flops 5000000000 | bytes 100000 | tf_op jit(solution)/shard_map/slabs/pallas_call | solution.py:443
  (123 shorter events, 11.5 us)
Async XLA Ops:
  2.8 18.6 %collective-permute-start = (bf16[448,512]{1,0:T(8,128)(2,1)S(1)}, bf16[448,512]{1,0:T(8,128)(2,1)S(1)}, u32[]{:S(2)}, u32[]{:S(2)}) collective-permute-start(bf16[448,512]{1,0:T(8,128)(2,1)S(1)} %pick.3.refs_0_), channel_id=1, source_target_pairs={{0,1},{1,0},{2,3},{3,2},{4,5},{5,4},{6,7},{7,6},{8,9},{9,8},{10,11... | collective-permute-start | bytes 1376264 | tf_op jit(solution)/shard_map/ppermute | solution.py:171
  7.4 19.5 %collective-permute-start.1 = (bf16[448,512]{1,0:T(8,128)(2,1)S(1)}, bf16[448,512]{1,0:T(8,128)(2,1)S(1)}, u32[]{:S(2)}, u32[]{:S(2)}) collective-permute-start(bf16[448,512]{1,0:T(8,128)(2,1)S(1)} %pick.4.refs_1_), channel_id=1, source_target_pairs={{0,1},{1,0},{2,3},{3,2},{4,5},{5,4},{6,7},{7,6},{8,9},{9,8},{10,11... | collective-permute-start | bytes 1376264 | tf_op jit(solution)/shard_map/ppermute | solution.py:171
  10.4 31.7 %collective-permute-start.36 = (bf16[64,512]{1,0:T(8,128)(2,1)S(1)}, bf16[64,512]{1,0:T(8,128)(2,1)S(1)}, u32[]{:S(2)}, u32[]{:S(2)}) collective-permute-start(bf16[64,512]{1,0:T(8,128)(2,1)S(1)} %convolution_convert_fusion.proj_own), channel_id=1, source_target_pairs={{0,1},{1,0},{2,3},{3,2},{4,5},{5,4},{6,7},{7,6},{8,9},{9,8},{10,11... | collective-permute-start | bytes 196616 | tf_op jit(solution)/shard_map/ppermute | solution.py:171
  28.7 39.3 %collective-permute-start.28 = (bf16[1024,512]{1,0:T(8,128)(2,1)S(1)}, bf16[1024,512]{1,0:T(8,128)(2,1)}, u32[]{:S(2)}, u32[]{:S(2)}) collective-permute-start(bf16[1024,512]{1,0:T(8,128)(2,1)S(1)} %pick.5), channel_id=1, source_target_pairs={{0,1},{1,0},{2,3},{3,2},{4,5},{5,4},{6,7},{7,6},{8,9},{9,8},{10,11... | collective-permute-start | bytes 3145736 | tf_op jit(solution)/shard_map/ppermute | solution.py:171
  30.5 13.5 %collective-permute-start.4 = (bf16[448,512]{1,0:T(8,128)(2,1)S(1)}, bf16[448,512]{1,0:T(8,128)(2,1)S(1)}, u32[]{:S(2)}, u32[]{:S(2)}) collective-permute-start(bf16[448,512]{1,0:T(8,128)(2,1)S(1)} %collective-permute-done.refs_0_), channel_id=1, source_target_pairs={{0,8},{1,9},{2,10},{3,11},{4,0},{5,1},{6,2},{7,3},{8,16},{9,17},{1... | collective-permute-start | bytes 1376264 | tf_op jit(solution)/shard_map/ppermute | solution.py:183
  32.0 12.1 %collective-permute-start.5 = (bf16[448,512]{1,0:T(8,128)(2,1)S(1)}, bf16[448,512]{1,0:T(8,128)(2,1)S(1)}, u32[]{:S(2)}, u32[]{:S(2)}) collective-permute-start(bf16[448,512]{1,0:T(8,128)(2,1)S(1)} %collective-permute-done.refs_0_), channel_id=1, source_target_pairs={{0,4},{1,5},{2,6},{3,7},{4,12},{5,13},{6,14},{7,15},{8,0},{9,1},{1... | collective-permute-start | bytes 1376264 | tf_op jit(solution)/shard_map/ppermute | solution.py:183
  41.8 24.0 %collective-permute-start.10 = (bf16[512,512]{1,0:T(8,128)(2,1)S(1)}, bf16[512,512]{1,0:T(8,128)(2,1)S(1)}, u32[]{:S(2)}, u32[]{:S(2)}) collective-permute-start(bf16[512,512]{1,0:T(8,128)(2,1)S(1)} %get-tuple-element.19.refs_2_), channel_id=1, source_target_pairs={{0,1},{1,0},{2,3},{3,2},{4,5},{5,4},{6,7},{7,6},{8,9},{9,8},{10,11... | collective-permute-start | bytes 1572872 | tf_op jit(solution)/shard_map/ppermute | solution.py:171
  44.2 11.1 %collective-permute-start.30 = (bf16[448,512]{1,0:T(8,128)(2,1)S(1)}, bf16[448,512]{1,0:T(8,128)(2,1)S(1)}, u32[]{:S(2)}, u32[]{:S(2)}) collective-permute-start(bf16[448,512]{1,0:T(8,128)(2,1)S(1)} %collective-permute-done.refs_0_), channel_id=1, source_target_pairs={{0,2},{1,3},{2,0},{3,1},{4,6},{5,7},{6,4},{7,5},{8,10},{9,11},{10,... | collective-permute-start | bytes 1376264 | tf_op jit(solution)/shard_map/ppermute | solution.py:175
  52.8 11.2 %collective-permute-start.31 = (bf16[448,512]{1,0:T(8,128)(2,1)S(1)}, bf16[448,512]{1,0:T(8,128)(2,1)S(1)}, u32[]{:S(2)}, u32[]{:S(2)}) collective-permute-start(bf16[448,512]{1,0:T(8,128)(2,1)S(1)} %collective-permute-done.1.refs_1_), channel_id=1, source_target_pairs={{0,2},{1,3},{2,0},{3,1},{4,6},{5,7},{6,4},{7,5},{8,10},{9,11},{10,... | collective-permute-start | bytes 1376264 | tf_op jit(solution)/shard_map/ppermute | solution.py:175
  53.4 14.0 %collective-permute-start.6 = (bf16[448,512]{1,0:T(8,128)(2,1)S(1)}, bf16[448,512]{1,0:T(8,128)(2,1)S(1)}, u32[]{:S(2)}, u32[]{:S(2)}) collective-permute-start(bf16[448,512]{1,0:T(8,128)(2,1)S(1)} %collective-permute-done.4.refs_0_.refs_4_), channel_id=1, source_target_pairs={{0,8},{1,9},{2,10},{3,11},{4,0},{5,1},{6,2},{7,3},{8,16},{9,17},{1... | collective-permute-start | bytes 1376264 | tf_op jit(solution)/shard_map/ppermute | solution.py:183
  55.2 12.6 %collective-permute-start.7 = (bf16[448,512]{1,0:T(8,128)(2,1)S(1)}, bf16[448,512]{1,0:T(8,128)(2,1)S(1)}, u32[]{:S(2)}, u32[]{:S(2)}) collective-permute-start(bf16[448,512]{1,0:T(8,128)(2,1)S(1)} %collective-permute-done.5.refs_1_.refs_8_), channel_id=1, source_target_pairs={{0,4},{1,5},{2,6},{3,7},{4,12},{5,13},{6,14},{7,15},{8,0},{9,1},{1... | collective-permute-start | bytes 1376264 | tf_op jit(solution)/shard_map/ppermute | solution.py:183
  64.0 20.5 %collective-permute-start.11 = (bf16[512,512]{1,0:T(8,128)(2,1)S(1)}, bf16[512,512]{1,0:T(8,128)(2,1)S(1)}, u32[]{:S(2)}, u32[]{:S(2)}) collective-permute-start(bf16[512,512]{1,0:T(8,128)(2,1)S(1)} %get-tuple-element.20.refs_3_), channel_id=1, source_target_pairs={{0,1},{1,0},{2,3},{3,2},{4,5},{5,4},{6,7},{7,6},{8,9},{9,8},{10,11... | collective-permute-start | bytes 1572872 | tf_op jit(solution)/shard_map/ppermute | solution.py:171
  65.8 11.7 %collective-permute-start.8 = (bf16[448,512]{1,0:T(8,128)(2,1)S(1)}, bf16[448,512]{1,0:T(8,128)(2,1)S(1)}, u32[]{:S(2)}, u32[]{:S(2)}) collective-permute-start(bf16[448,512]{1,0:T(8,128)(2,1)S(1)} %collective-permute-done.2.refs_0_.refs_5_), channel_id=1, source_target_pairs={{0,8},{1,9},{2,10},{3,11},{4,0},{5,1},{6,2},{7,3},{8,16},{9,17},{1... | collective-permute-start | bytes 1376264 | tf_op jit(solution)/shard_map/ppermute | solution.py:183
  67.4 11.4 %collective-permute-start.9 = (bf16[448,512]{1,0:T(8,128)(2,1)S(1)}, bf16[448,512]{1,0:T(8,128)(2,1)S(1)}, u32[]{:S(2)}, u32[]{:S(2)}) collective-permute-start(bf16[448,512]{1,0:T(8,128)(2,1)S(1)} %collective-permute-done.3.refs_1_.refs_9_), channel_id=1, source_target_pairs={{0,4},{1,5},{2,6},{3,7},{4,12},{5,13},{6,14},{7,15},{8,0},{9,1},{1... | collective-permute-start | bytes 1376264 | tf_op jit(solution)/shard_map/ppermute | solution.py:183
  67.8 10.9 %collective-permute-start.32 = (bf16[448,512]{1,0:T(8,128)(2,1)S(1)}, bf16[448,512]{1,0:T(8,128)(2,1)S(1)}, u32[]{:S(2)}, u32[]{:S(2)}) collective-permute-start(bf16[448,512]{1,0:T(8,128)(2,1)S(1)} %collective-permute-done.4.refs_0_.refs_4_), channel_id=1, source_target_pairs={{0,2},{1,3},{2,0},{3,1},{4,6},{5,7},{6,4},{7,5},{8,10},{9,11},{10,... | collective-permute-start | bytes 1376264 | tf_op jit(solution)/shard_map/ppermute | solution.py:175
  67.9 12.5 %collective-permute-start.33 = (bf16[448,512]{1,0:T(8,128)(2,1)S(1)}, bf16[448,512]{1,0:T(8,128)(2,1)S(1)}, u32[]{:S(2)}, u32[]{:S(2)}) collective-permute-start(bf16[448,512]{1,0:T(8,128)(2,1)S(1)} %collective-permute-done.2.refs_0_.refs_5_), channel_id=1, source_target_pairs={{0,2},{1,3},{2,0},{3,1},{4,6},{5,7},{6,4},{7,5},{8,10},{9,11},{10,... | collective-permute-start | bytes 1376264 | tf_op jit(solution)/shard_map/ppermute | solution.py:175
  78.8 13.0 %collective-permute-start.12 = (bf16[448,512]{1,0:T(8,128)(2,1)S(1)}, bf16[448,512]{1,0:T(8,128)(2,1)}, u32[]{:S(2)}, u32[]{:S(2)}) collective-permute-start(bf16[448,512]{1,0:T(8,128)(2,1)S(1)} %collective-permute-done.6.refs_2_.refs_0_), channel_id=1, source_target_pairs={{0,8},{1,9},{2,10},{3,11},{4,0},{5,1},{6,2},{7,3},{8,16},{9,17},{1... | collective-permute-start | bytes 1376264 | tf_op jit(solution)/shard_map/ppermute | solution.py:183
  84.0 12.4 %collective-permute-start.21 = (bf16[448,512]{1,0:T(8,128)(2,1)S(1)}, bf16[448,512]{1,0:T(8,128)(2,1)S(1)}, u32[]{:S(2)}, u32[]{:S(2)}) collective-permute-start(bf16[448,512]{1,0:T(8,128)(2,1)S(1)} %collective-permute-done.7.refs_3_.refs_4_), channel_id=1, source_target_pairs={{0,4},{1,5},{2,6},{3,7},{4,12},{5,13},{6,14},{7,15},{8,0},{9,1},{1... | collective-permute-start | bytes 1376264 | tf_op jit(solution)/shard_map/ppermute | solution.py:183
  84.5 11.9 %collective-permute-start.24 = (bf16[448,512]{1,0:T(8,128)(2,1)S(1)}, bf16[448,512]{1,0:T(8,128)(2,1)S(1)}, u32[]{:S(2)}, u32[]{:S(2)}) collective-permute-start(bf16[448,512]{1,0:T(8,128)(2,1)S(1)} %collective-permute-done.6.refs_2_.refs_0_), channel_id=1, source_target_pairs={{0,2},{1,3},{2,0},{3,1},{4,6},{5,7},{6,4},{7,5},{8,10},{9,11},{10,... | collective-permute-start | bytes 1376264 | tf_op jit(solution)/shard_map/ppermute | solution.py:175
  84.5 13.5 %collective-permute-start.25 = (bf16[448,512]{1,0:T(8,128)(2,1)S(1)}, bf16[448,512]{1,0:T(8,128)(2,1)S(1)}, u32[]{:S(2)}, u32[]{:S(2)}) collective-permute-start(bf16[448,512]{1,0:T(8,128)(2,1)S(1)} %collective-permute-done.8.refs_4_.refs_1_), channel_id=1, source_target_pairs={{0,2},{1,3},{2,0},{3,1},{4,6},{5,7},{6,4},{7,5},{8,10},{9,11},{10,... | collective-permute-start | bytes 1376264 | tf_op jit(solution)/shard_map/ppermute | solution.py:175
  86.0 12.5 %collective-permute-start.26 = (bf16[448,512]{1,0:T(8,128)(2,1)S(1)}, bf16[448,512]{1,0:T(8,128)(2,1)S(1)}, u32[]{:S(2)}, u32[]{:S(2)}) collective-permute-start(bf16[448,512]{1,0:T(8,128)(2,1)S(1)} %collective-permute-done.7.refs_3_.refs_4_), channel_id=1, source_target_pairs={{0,2},{1,3},{2,0},{3,1},{4,6},{5,7},{6,4},{7,5},{8,10},{9,11},{10,... | collective-permute-start | bytes 1376264 | tf_op jit(solution)/shard_map/ppermute | solution.py:175
  91.8 20.7 %collective-permute-start.29 = (bf16[1024,512]{1,0:T(8,128)(2,1)}, bf16[1024,512]{1,0:T(8,128)(2,1)S(1)}, u32[]{:S(2)}, u32[]{:S(2)}) collective-permute-start(bf16[1024,512]{1,0:T(8,128)(2,1)} %collective-permute-done.28.refs_8_.refs_4_), channel_id=1, source_target_pairs={{0,2},{1,3},{2,0},{3,1},{4,6},{5,7},{6,4},{7,5},{8,10},{9,11},{10,... | collective-permute-start | bytes 3145736 | tf_op jit(solution)/shard_map/ppermute | solution.py:175
  96.4 13.8 %collective-permute-start.27 = (bf16[448,512]{1,0:T(8,128)(2,1)S(1)}, bf16[448,512]{1,0:T(8,128)(2,1)S(1)}, u32[]{:S(2)}, u32[]{:S(2)}) collective-permute-start(bf16[448,512]{1,0:T(8,128)(2,1)S(1)} %collective-permute-done.9.refs_5_), channel_id=1, source_target_pairs={{0,2},{1,3},{2,0},{3,1},{4,6},{5,7},{6,4},{7,5},{8,10},{9,11},{10,... | collective-permute-start | bytes 1376264 | tf_op jit(solution)/shard_map/ppermute | solution.py:175
  96.4 15.6 %collective-permute-start.18 = (bf16[448,512]{1,0:T(8,128)(2,1)S(1)}, bf16[448,512]{1,0:T(8,128)(2,1)S(1)}, u32[]{:S(2)}, u32[]{:S(2)}) collective-permute-start(bf16[448,512]{1,0:T(8,128)(2,1)S(1)} %collective-permute-done.8.refs_4_.refs_1_), channel_id=1, source_target_pairs={{0,8},{1,9},{2,10},{3,11},{4,0},{5,1},{6,2},{7,3},{8,16},{9,17},{1... | collective-permute-start | bytes 1376264 | tf_op jit(solution)/shard_map/ppermute | solution.py:183
  98.0 13.8 %collective-permute-start.14 = (bf16[448,512]{1,0:T(8,128)(2,1)S(1)}, bf16[448,512]{1,0:T(8,128)(2,1)S(1)}, u32[]{:S(2)}, u32[]{:S(2)}) collective-permute-start(bf16[448,512]{1,0:T(8,128)(2,1)S(1)} %collective-permute-done.9.refs_5_), channel_id=1, source_target_pairs={{0,4},{1,5},{2,6},{3,7},{4,12},{5,13},{6,14},{7,15},{8,0},{9,1},{1... | collective-permute-start | bytes 1376264 | tf_op jit(solution)/shard_map/ppermute | solution.py:183
  98.5 14.0 %collective-permute-start.19 = (bf16[448,512]{1,0:T(8,128)(2,1)}, bf16[448,512]{1,0:T(8,128)(2,1)S(1)}, u32[]{:S(2)}, u32[]{:S(2)}) collective-permute-start(bf16[448,512]{1,0:T(8,128)(2,1)} %collective-permute-done.12.refs_10_.refs_0_), channel_id=1, source_target_pairs={{0,2},{1,3},{2,0},{3,1},{4,6},{5,7},{6,4},{7,5},{8,10},{9,11},{10,... | collective-permute-start | bytes 1376264 | tf_op jit(solution)/shard_map/ppermute | solution.py:175
  110.2 15.1 %collective-permute-start.13 = (bf16[448,512]{1,0:T(8,128)(2,1)}, bf16[448,512]{1,0:T(8,128)(2,1)S(1)}, u32[]{:S(2)}, u32[]{:S(2)}) collective-permute-start(bf16[448,512]{1,0:T(8,128)(2,1)} %collective-permute-done.12.refs_10_.refs_0_), channel_id=1, source_target_pairs={{0,8},{1,9},{2,10},{3,11},{4,0},{5,1},{6,2},{7,3},{8,16},{9,17},{1... | collective-permute-start | bytes 1376264 | tf_op jit(solution)/shard_map/ppermute | solution.py:183
  111.8 14.1 %collective-permute-start.23 = (bf16[448,512]{1,0:T(8,128)(2,1)S(1)}, bf16[448,512]{1,0:T(8,128)(2,1)S(1)}, u32[]{:S(2)}, u32[]{:S(2)}) collective-permute-start(bf16[448,512]{1,0:T(8,128)(2,1)S(1)} %collective-permute-done.14.refs_5_), channel_id=1, source_target_pairs={{0,2},{1,3},{2,0},{3,1},{4,6},{5,7},{6,4},{7,5},{8,10},{9,11},{10,... | collective-permute-start | bytes 1376264 | tf_op jit(solution)/shard_map/ppermute | solution.py:175
  112.0 13.8 %collective-permute-start.15 = (bf16[448,512]{1,0:T(8,128)(2,1)S(1)}, bf16[448,512]{1,0:T(8,128)(2,1)S(1)}, u32[]{:S(2)}, u32[]{:S(2)}) collective-permute-start(bf16[448,512]{1,0:T(8,128)(2,1)S(1)} %collective-permute-done.14.refs_5_), channel_id=1, source_target_pairs={{0,4},{1,5},{2,6},{3,7},{4,12},{5,13},{6,14},{7,15},{8,0},{9,1},{1... | collective-permute-start | bytes 1376264 | tf_op jit(solution)/shard_map/ppermute | solution.py:183
  112.5 13.5 %collective-permute-start.20 = (bf16[448,512]{1,0:T(8,128)(2,1)S(1)}, bf16[448,512]{1,0:T(8,128)(2,1)S(1)}, u32[]{:S(2)}, u32[]{:S(2)}) collective-permute-start(bf16[448,512]{1,0:T(8,128)(2,1)S(1)} %collective-permute-done.18.refs_1_), channel_id=1, source_target_pairs={{0,2},{1,3},{2,0},{3,1},{4,6},{5,7},{6,4},{7,5},{8,10},{9,11},{10,... | collective-permute-start | bytes 1376264 | tf_op jit(solution)/shard_map/ppermute | solution.py:175
  112.5 13.4 %collective-permute-start.22 = (bf16[448,512]{1,0:T(8,128)(2,1)S(1)}, bf16[448,512]{1,0:T(8,128)(2,1)S(1)}, u32[]{:S(2)}, u32[]{:S(2)}) collective-permute-start(bf16[448,512]{1,0:T(8,128)(2,1)S(1)} %collective-permute-done.21.refs_11_.refs_4_), channel_id=1, source_target_pairs={{0,2},{1,3},{2,0},{3,1},{4,6},{5,7},{6,4},{7,5},{8,10},{9,11},{10,... | collective-permute-start | bytes 1376264 | tf_op jit(solution)/shard_map/ppermute | solution.py:175
  125.3 10.8 %collective-permute-start.16 = (bf16[448,512]{1,0:T(8,128)(2,1)S(1)}, bf16[448,512]{1,0:T(8,128)(2,1)S(1)}, u32[]{:S(2)}, u32[]{:S(2)}) collective-permute-start(bf16[448,512]{1,0:T(8,128)(2,1)S(1)} %collective-permute-done.13.refs_0_), channel_id=1, source_target_pairs={{0,2},{1,3},{2,0},{3,1},{4,6},{5,7},{6,4},{7,5},{8,10},{9,11},{10,... | collective-permute-start | bytes 1376264 | tf_op jit(solution)/shard_map/ppermute | solution.py:175
  (35 other events, 350.7 us)
